TPU v7x, 32 devices: a whole 2x2x4 slice. The times are simulated.
32 devices in a mesh: row: 4 (over y, x), col: 8 (over z, core).
Axes of the slice: x: 2, y: 2, z: 4, core: 2. Of those that a mesh axis runs over, the one named last changes fastest.
Arguments:
- pair_state: bfloat16 [192, 192, 128], P(('row', 'col')), may hold values from -6 to 6
- single_rep: bfloat16 [16, 192, 768], P(None, ('row', 'col')), may hold values from -64 to 64
- token_mask: int32 [192], replicated, may hold values 0 or 1
- chain_ids: int32 [192], replicated, may hold values from 0 to 3, never falling along the last dimension, each value on 1 to 96 neighbouring positions
- pair_gain: float32 [128], replicated, may hold values from 0.1 to 1.9
- mix_gain: float32 [128], replicated, may hold values from 0.1 to 1.9
- left_weight: bfloat16 [128, 256], replicated, may hold values from -0.5 to 0.5
- right_weight: bfloat16 [128, 256], replicated, may hold values from -0.5 to 0.5
- gate_weight: bfloat16 [128, 128], replicated, may hold values from -0.5 to 0.5
- out_weight: bfloat16 [128, 128], replicated, may hold values from -0.5 to 0.5
- bias_weight: bfloat16 [128, 16], replicated, may hold values from -1.5 to 1.5
- token_weight: bfloat16 [768, 2304], replicated, may hold values from -0.21875 to 0.21875
- merge_weight: bfloat16 [768, 768], replicated, may hold values from -0.625 to 0.625
Outputs:
- pair_tiles: bfloat16 [192, 4, 8, 6, 128], P('row', None, 'col')
- attention_out: bfloat16 [16, 192, 768], P(None, ('row', 'col'))
Inputs may be any that keep to these rules, and one draw needn't show every extreme that they name: chain_ids never falls along the tokens; a chain holds 1 to 96 tokens.
All inputs are finite; a program needn't handle non-finite values.
Results may differ from a plain program's by a relative error of at most 0.034.
Values may be sent and summed in bfloat16 or wider, within the bound.
No kernel may reach another device: no remote copies, remote signals or barrier semaphores. Data moves between devices by JAX's collectives and lax.ppermute only.
A program may use at most 256 MiB of HBM per device.

v0:
```python
import math

import jax
import jax.numpy as jnp
from jax import lax
from jax.sharding import PartitionSpec as P

epsilon = 1e-05


def normalize(values, norm_gain):
    floats = values.astype(jnp.float32)
    centered = floats - jnp.mean(floats, axis=-1, keepdims=True)
    variance = jnp.mean(centered * centered, axis=-1, keepdims=True)
    scaled = centered * lax.rsqrt(variance + epsilon)
    if norm_gain is None:
        return scaled
    return scaled * norm_gain


def gated_branch(normed, weight, pair_mask):
    half_width = weight.shape[0]
    hidden = jnp.einsum("ikc,ce->ike", normed, weight, preferred_element_type=jnp.float32)
    return (
        jax.nn.sigmoid(hidden[..., :half_width]) * hidden[..., half_width:] * pair_mask[..., None]
    ).astype(jnp.bfloat16)


def rows_blocks(pair_rows, valid_rows, valid_all, pair_gain, left_weight, group_count, group_rows):
    token_count = pair_rows.shape[1]
    channels = pair_rows.shape[2]

    def one_group(inputs):
        pair_group, valid_group = inputs
        normed_group = normalize(pair_group, pair_gain).astype(jnp.bfloat16)
        left_group = gated_branch(
            normed_group, left_weight, valid_group[:, None] * valid_all[None, :]
        )
        return (normed_group, left_group)

    grouped = (
        pair_rows.reshape(group_count, group_rows, token_count, channels),
        valid_rows.reshape(group_count, group_rows),
    )
    normed_groups, left_groups = lax.map(one_group, grouped)
    return (
        normed_groups.reshape(group_count * group_rows, token_count, channels),
        left_groups.reshape(group_count * group_rows, token_count, channels),
    )


def shards(
    pair_state,
    single_rep,
    token_mask,
    chain_ids,
    pair_gain,
    mix_gain,
    left_weight,
    right_weight,
    gate_weight,
    out_weight,
    bias_weight,
    token_weight,
    merge_weight,
):
    row_count = lax.axis_size("row")
    col_count = lax.axis_size("col")
    row_index = lax.axis_index("row")
    col_index = lax.axis_index("col")
    flat_rows = pair_state.shape[0]
    channels = pair_state.shape[2]
    samples = single_rep.shape[0]
    model_width = single_rep.shape[2]
    head_count = bias_weight.shape[1]
    head_width = model_width // head_count
    block_rows = flat_rows * col_count
    block_cols = flat_rows * row_count
    valid_all = (token_mask == 1).astype(jnp.float32)
    own_start = (row_index * col_count + col_index) * flat_rows
    row_start = row_index * block_rows
    valid_own = lax.dynamic_slice_in_dim(valid_all, own_start, flat_rows)
    valid_rows = lax.dynamic_slice_in_dim(valid_all, row_start, block_rows)
    valid_cols = lax.dynamic_index_in_dim(
        valid_all.reshape(row_count, col_count, flat_rows), col_index, 1, False
    ).reshape(block_cols)
    chain_rows = lax.dynamic_slice_in_dim(chain_ids, row_start, block_rows)
    chain_cols = lax.dynamic_index_in_dim(
        chain_ids.reshape(row_count, col_count, flat_rows), col_index, 1, False
    ).reshape(block_cols)
    projected = jnp.einsum(
        "std,de->ste", single_rep, token_weight, preferred_element_type=jnp.float32
    ).astype(jnp.bfloat16)
    queries = projected[..., :model_width]
    keys_own = projected[..., model_width : 2 * model_width]
    values_own = projected[..., 2 * model_width :]
    normed_own = normalize(pair_state, pair_gain).astype(jnp.bfloat16)
    own_mask = valid_own[:, None] * valid_all[None, :]
    right_own = gated_branch(normed_own, right_weight, own_mask)
    right_cols, keys_cols, values_cols = (
        lax.all_gather(right_own, "row", axis=0, tiled=True),
        lax.all_gather(keys_own, "row", axis=1, tiled=True),
        lax.all_gather(values_own, "row", axis=1, tiled=True),
    )
    pair_rows, query_rows = (
        lax.all_gather(pair_state, "col", axis=0, tiled=True),
        lax.all_gather(queries, "col", axis=1, tiled=True),
    )
    normed_rows, left_rows = rows_blocks(
        pair_rows, valid_rows, valid_all, pair_gain, left_weight, col_count, flat_rows
    )
    pair_tile = lax.dynamic_index_in_dim(
        pair_rows.reshape(block_rows, row_count, col_count, flat_rows, channels),
        col_index,
        2,
        False,
    ).reshape(block_rows, block_cols, channels)
    normed_tile = lax.dynamic_index_in_dim(
        normed_rows.reshape(block_rows, row_count, col_count, flat_rows, channels),
        col_index,
        2,
        False,
    ).reshape(block_rows, block_cols, channels)
    mixed_pairs = jnp.einsum(
        "ikc,jkc->ijc", left_rows, right_cols, preferred_element_type=jnp.float32
    )
    mixed_norm = normalize(mixed_pairs, mix_gain).astype(jnp.bfloat16)
    gate_value = jax.nn.sigmoid(
        jnp.einsum("ijc,ce->ije", normed_tile, gate_weight, preferred_element_type=jnp.float32)
    )
    update = jnp.einsum("ijc,ce->ije", mixed_norm, out_weight, preferred_element_type=jnp.float32)
    pair_new = (pair_tile.astype(jnp.float32) + gate_value * update).astype(jnp.bfloat16)
    bias_input = normalize(pair_new, None).astype(jnp.bfloat16)
    pair_bias = jnp.einsum(
        "ijc,ch->hij", bias_input, bias_weight, preferred_element_type=jnp.float32
    )
    query_heads = query_rows.reshape(samples, block_rows, head_count, head_width)
    key_heads = keys_cols.reshape(samples, block_cols, head_count, head_width)
    value_heads = values_cols.reshape(samples, block_cols, head_count, head_width)
    score_scale = 1.0 / math.sqrt(head_width)
    scores = (
        jnp.einsum("sihd,sjhd->shij", query_heads, key_heads, preferred_element_type=jnp.float32)
        * score_scale
        + pair_bias[None]
    )
    row_ids = row_start + jnp.arange(block_rows, dtype=jnp.int32)
    col_ids = (
        (jnp.arange(row_count, dtype=jnp.int32)[:, None] * col_count + col_index) * flat_rows
        + jnp.arange(flat_rows, dtype=jnp.int32)[None, :]
    ).reshape(block_cols)
    allowed = (valid_cols[None, :] > 0.5) & (chain_rows[:, None] == chain_cols[None, :]) | (
        row_ids[:, None] == col_ids[None, :]
    )
    local_max = jnp.max(jnp.where(allowed[None, None], scores, -1e30), axis=-1)
    row_max = lax.pmax(local_max.astype(jnp.bfloat16), "col").astype(local_max.dtype)
    weights = jnp.where(allowed[None, None], jnp.exp(scores - row_max[..., None]), 0.0).astype(
        jnp.bfloat16
    )
    totals = jnp.sum(weights.astype(jnp.float32), axis=-1)
    summed = jnp.einsum(
        "shij,sjhd->sihd", weights, value_heads, preferred_element_type=jnp.float32
    ).reshape(samples, block_rows, model_width)
    summed_own, totals_own = (
        lax.psum_scatter(
            summed.astype(jnp.bfloat16), "col", scatter_dimension=1, tiled=True
        ).astype(jnp.float32),
        lax.psum_scatter(
            totals.astype(jnp.bfloat16), "col", scatter_dimension=2, tiled=True
        ).astype(jnp.float32),
    )
    attended = (
        summed_own.reshape(samples, flat_rows, head_count, head_width)
        / jnp.transpose(totals_own, (0, 2, 1))[..., None]
    ).astype(jnp.bfloat16)
    attended = attended.reshape(samples, flat_rows, model_width)
    attention_out = jnp.einsum(
        "std,de->ste", attended, merge_weight, preferred_element_type=jnp.float32
    ).astype(jnp.bfloat16)
    return (pair_new.reshape(block_rows, row_count, 1, flat_rows, channels), attention_out)


def solution(mesh):
    in_specs = (
        P(("row", "col"), None, None),
        P(None, ("row", "col"), None),
        P(),
        P(),
        P(),
        P(),
        P(),
        P(),
        P(),
        P(),
        P(),
        P(),
        P(),
    )
    out_specs = (P("row", None, "col", None, None), P(None, ("row", "col"), None))
    return jax.shard_map(shards, mesh=mesh, in_specs=in_specs, out_specs=out_specs, check_vma=False)
```

profile of v0, /device:TPU:0, one launch (start us, length us, event | category | flops | bytes accessed | tf_op | source)
XLA Modules:
  0.0 311.6 jit_solution(12548675535412819114)
XLA Ops:
  8.1 1.3 convert_reduce_fusion.2
  9.4 1.4 fusion.49
  11.6 1.5 fusion.57
  14.1 1.6 fusion.26
  23.0 14.0 %all_gather.19 = bf16[16,24,768]{2,0,1:T(8,128)(2,1)} all-gather(bf16[16,6,768]{2,0,1:T(8,128)(2,1)} %get-tuple-element.86), channel_id=1, replica_groups=mesh['row'=4,'col'=8] {'row'}, dimensions={1}, use_global_device_ids=true | all-gather | bytes 737280 | tf_op jit(solution)/shard_map/all_gather | solution.py:102
  37.0 3.7 %reshape.292 = bf16[16,24,16,48]{3,2,0,1:T(8,128)(2,1)} reshape(bf16[16,24,768]{2,0,1:T(8,128)(2,1)} %all_gather.19) | data formatting | bytes 1179648 | tf_op jit(solution)/shard_map/reshape | solution.py:138
  40.6 12.1 %all_gather.17 = bf16[16,24,768]{2,0,1:T(8,128)(2,1)} all-gather(bf16[16,6,768]{2,0,1:T(8,128)(2,1)} %get-tuple-element.85), channel_id=1, replica_groups=mesh['row'=4,'col'=8] {'row'}, dimensions={1}, use_global_device_ids=true | all-gather | bytes 737280 | tf_op jit(solution)/shard_map/all_gather | solution.py:103
  52.8 3.6 %reshape.290 = bf16[16,24,16,48]{3,2,0,1:T(8,128)(2,1)} reshape(bf16[16,24,768]{2,0,1:T(8,128)(2,1)} %all_gather.17) | data formatting | bytes 1179648 | tf_op jit(solution)/shard_map/reshape | solution.py:139
  57.2 2.8 copy.99
  60.1 9.1 %all-gather.8.cloned.1.call-done = bf16[16,48,768]{2,0,1:T(8,128)(2,1)} async-done(((bf16[16,6,768]{2,0,1:T(8,128)(2,1)}), bf16[16,48,768]{2,0,1:T(8,128)(2,1)}) %all-gather.8.cloned.1.call-update) | async-done | bytes 1179664 | tf_op jit(solution)/shard_map/all_gather | solution.py:107
  69.2 5.8 %reshape.291 = bf16[16,48,16,48]{3,2,0,1:T(8,128)(2,1)} reshape(bf16[16,48,768]{2,0,1:T(8,128)(2,1)} %all-gather.8.cloned.1.call-done) | data formatting | bytes 2359296 | tf_op jit(solution)/shard_map/reshape | solution.py:137
  75.0 27.3 %all-gather.4.cloned.1.call-done = bf16[48,192,128]{2,1,0:T(8,128)(2,1)} async-done(((bf16[6,192,128]{2,1,0:T(8,128)(2,1)}), bf16[48,192,128]{2,1,0:T(8,128)(2,1)}) %all-gather.4.cloned.1.call-update) | async-done | bytes 2359312 | tf_op jit(solution)/shard_map/all_gather | solution.py:106
  102.3 57.2 %while.12 = (s32[]{:T(128)}, bf16[8,6,192,128]{3,2,1,0:T(8,128)(2,1)}, bf16[8,6,192,128]{3,2,1,0:T(8,128)(2,1)}, bf16[8,6,192,128]{3,2,1,0:T(8,128)(2,1)}, f32[1...) while((s32[]{:T(128)}, ...), condition=%wide.region_3.4_spmd, body=%wide.region_0.0_spmd.sunk | while | flops 78743808 | bytes 4256193 | solution.py:45
  102.3 1.1 convert_reduce_fusion.4
  103.4 1.4 fusion.84
  105.6 1.5 fusion.86
  107.1 2.3 fusion.87
  110.6 1.4 fusion.84
  112.8 1.5 fusion.86
  114.3 2.3 fusion.87
  116.6 1.1 convert_reduce_fusion.4
  117.7 1.4 fusion.84
  120.0 1.5 fusion.86
  121.4 2.3 fusion.87
  124.9 1.4 fusion.84
  127.1 1.5 fusion.86
  128.6 2.3 fusion.87
  130.9 1.1 convert_reduce_fusion.4
  132.0 1.4 fusion.84
  134.2 1.5 fusion.86
  135.7 2.3 fusion.87
  138.0 1.1 convert_reduce_fusion.4
  139.2 1.4 fusion.84
  141.4 1.5 fusion.86
  142.8 2.3 fusion.87
  146.3 1.4 fusion.84
  148.5 1.5 fusion.86
  150.0 2.3 fusion.87
  152.3 1.1 convert_reduce_fusion.4
  153.5 1.4 fusion.84
  155.7 1.5 fusion.86
  157.1 2.4 fusion.87
  159.5 5.1 %reshape_reshape.3 = bf16[48,4,8,6,128]{4,3,2,1,0:T(8,128)(2,1)} reshape(bf16[8,6,192,128]{3,2,1,0:T(8,128)(2,1)} %get-tuple-element.45) | data formatting | bytes 4718592 | tf_op jit(solution)/shard_map/reshape;reshape | solution.py:119
  166.5 4.9 %copy.100 = bf16[48,192,128]{1,0,2:T(8,128)(2,1)} copy(bf16[48,192,128]{2,1,0:T(8,128)(2,1)} %bitcast.96) | data formatting | bytes 4718592 | tf_op jit(solution)/shard_map/reshape | solution.py:48
  171.4 3.3 %bitcast_reduce_fusion = (f32[48,24]{0,1:T(8,128)S(1)}, f32[128,24,48]{2,1,0:T(8,128)S(1)}) fusion(bf16[24,192,128]{1,0,2:T(8,128)(2,1)} %copy.99, bf16[48,192,128]{1,0,2:T(8,128)(2,1)} %copy.100), kind=kOutput, calls=%fused_computation.45 | convolution fusion | flops 56769408 | bytes 4133376 | tf_op jit(solution)/shard_map/ikc,jkc->ijc/dot_general | solution.py:124
  176.2 2.4 copy.101
  178.5 3.2 %copy.96 = bf16[48,192,128]{2,0,1:T(8,128)(2,1)S(1)} copy(bf16[48,192,128]{2,1,0:T(8,128)(2,1)} %bitcast.93) | data formatting | bytes 4718592 | tf_op jit(solution)/shard_map/all_gather | solution.py:106
  182.7 1.7 convert_reduce_fusion.1
  185.8 1.4 copy.110
  187.2 2.0 fusion.47
  190.6 1.4 copy.112
  191.9 2.4 convolution_bitcast_fusion
  194.4 1.9 copy.113
  196.2 8.7 %select_reduce_fusion = (bf16[16,16,48]{2,1,0:T(8,128)(2,1)}, f32[16,16,48,24]{2,3,1,0:T(8,128)}) fusion(f32[16,48,24]{1,2,0:T(8,128)} %copy.113, pred[48,24]{0,1:T(8,128)(4,1)S(1)} %compare_or_fusion, bf16[16,24,16,48]{3,2,0,1:T(8,128)(2,1)} %reshape.292, bf16[16,48,16,48]{3,2,0,1:T(8,128)(2,1)} %reshape.291), kind=kOutput, calls=%fused_computation.39 | convolution fusion | flops 29478912 | bytes 3048576 | tf_op jit(solution)/shard_map/sihd,sjhd->shij/dot_general | solution.py:142
  204.9 28.8 %pmax.7 = bf16[16,16,48]{2,1,0:T(8,128)(2,1)} all-reduce(bf16[16,16,48]{2,1,0:T(8,128)(2,1)} %get-tuple-element.92), channel_id=1, replica_groups=mesh['row'=4,'col'=8] {'col'}, use_global_device_ids=true, to_apply=%region_11.12 | all-reduce | flops 12288 | bytes 49152 | tf_op jit(solution)/shard_map/pmax | solution.py:155
  235.2 3.9 %fusion.70 = bf16[16,16,48]{2,1,0:T(8,128)(2,1)} fusion(f32[16,16,48]{2,1,0:T(8,128)S(1)} %convert_element_type.92, f32[16,48,24]{1,2,0:T(8,128)} %copy.113, f32[16,16,48,24]{2,3,1,0:T(8,128)} %get-tuple-element.93, pred[48,24]{0,1:T(8,128)(4,1)S(1)} %compare_or_fusion), kind=kLoop, calls=%fused_computation.109 | loop fusion | flops 1757184 | bytes 1328256 | tf_op jit(solution)/shard_map/reduce_sum | solution.py:159
  239.1 1.7 copy.116
  241.1 6.3 %convolution_convert_fusion = bf16[16,16,48,48]{3,2,1,0:T(8,128)(2,1)} fusion(bf16[16,24,16,48]{3,2,0,1:T(8,128)(2,1)} %reshape.290, f32[16,16,48,24]{2,3,1,0:T(8,128)} %get-tuple-element.93, f32[16,16,48]{2,1,0:T(8,128)} %copy-done.1, f32[16,48,24]{1,2,0:T(8,128)} %copy.113, pred[48,24]{0,1:T(8,128)(4,1)S(1)} %compare_or_fusion), kind=kOutput, calls=%fused_computation.41 | convolution fusion | flops 30375936 | bytes 3073152 | tf_op jit(solution)/shard_map/shij,sjhd->sihd/dot_general | solution.py:160
  247.4 4.5 %copy.115 = bf16[16,48,768]{2,0,1:T(8,128)(2,1)} copy(bf16[16,48,768]{1,2,0:T(8,128)(2,1)} %bitcast.94) | data formatting | bytes 2359296 | tf_op jit(solution)/shard_map/convert_element_type | solution.py:165
  253.8 15.6 %reduce-scatter.5.cloned.1.call-done = bf16[16,16,6]{1,0,2:T(8,128)(2,1)} async-done(((bf16[16,16,48]{1,0,2:T(8,128)(2,1)}), bf16[16,16,6]{1,0,2:T(8,128)(2,1)}) %reduce-scatter.5.cloned.1.call-update) | async-done | bytes 3088 | tf_op jit(solution)/shard_map/reduce_scatter | solution.py:167
  270.1 1.1 div.52
  271.2 2.1 div.53
  273.4 29.3 %reduce-scatter.3.cloned.1.call-done = bf16[16,6,768]{2,0,1:T(8,128)(2,1)} async-done(((bf16[16,48,768]{2,0,1:T(8,128)(2,1)}), bf16[16,6,768]{2,0,1:T(8,128)(2,1)}) %reduce-scatter.3.cloned.1.call-update) | async-done | bytes 147472 | tf_op jit(solution)/shard_map/reduce_scatter | solution.py:164
  302.6 2.4 fusion.40
  (106 shorter events, 31.6 us)
Async XLA Ops:
  7.2 6.9 %copy-start = (bf16[768,2304]{1,0:T(8,128)(2,1)S(1)}, bf16[768,2304]{1,0:T(8,128)(2,1)}, u32[]{:S(2)}) copy-start(bf16[768,2304]{1,0:T(8,128)(2,1)} %param.26) | copy-start | bytes 10616836
  7.2 50.0 %all-gather.6.cloned.1.call-start = ((), (), s32[]{:S(2)}) async-start(), calls=%async_computation.3 | async-start | bytes 1474560 | tf_op jit(solution)/shard_map/all_gather | solution.py:101
  14.0 3.4 %copy-start.7 = (s32[192]{0:T(256)S(1)}, s32[192]{0:T(256)}, u32[]{:S(2)}) copy-start(s32[192]{0:T(256)} %param.18) | copy-start | bytes 2308
  14.1 55.1 %all-gather.8.cloned.1.call-start = ((), (), s32[]{:S(2)}) async-start(), calls=%async_computation.4 | async-start | bytes 1327104 | tf_op jit(solution)/shard_map/all_gather | solution.py:107
  16.5 85.7 %all-gather.4.cloned.1.call-start = ((), (), s32[]{:S(2)}) async-start(), calls=%async_computation.2 | async-start | bytes 2654208 | tf_op jit(solution)/shard_map/all_gather | solution.py:106
  17.3 252.1 %reduce-scatter.5.cloned.1.call-start = ((), (), s32[]{:S(2)}) async-start(), calls=%async_computation.6 | async-start | bytes 221184 | tf_op jit(solution)/shard_map/reduce_scatter | solution.py:167
  37.0 19.5 %copy-start.6 = (s32[24]{0:T(128)S(1)}, s32[24]{0:T(128)}, u32[]{:S(2)}) copy-start(s32[24]{0:T(128)} %eq.45) | copy-start | bytes 292
  60.1 42.2 %copy-start.4 = (f32[128]{0:T(128)S(1)}, f32[128]{0:T(128)}, u32[]{:S(2)}) copy-start(f32[128]{0:T(128)} %param.19) | copy-start | bytes 1540
  171.4 3.6 %copy-start.8 = (f32[128]{0:T(128)S(1)}, f32[128]{0:T(128)}, u32[]{:S(2)}) copy-start(f32[128]{0:T(128)} %param.20) | copy-start | bytes 1540
  178.5 3.4 %copy-start.3 = (bf16[48,4,1,6,128]{4,0,3,1,2:T(8,128)(2,1)S(1)}, bf16[48,4,1,6,128]{4,0,3,1,2:T(8,128)(2,1)}, u32[]{:S(2)}) copy-start(bf16[48,4,1,6,128]{4,0,3,1,2:T(8,128)(2,1)} %copy.97) | copy-start | bytes 884740
  178.5 3.4 %copy-start.9 = (bf16[128,128]{1,0:T(8,128)(2,1)S(1)}, bf16[128,128]{1,0:T(8,128)(2,1)}, u32[]{:S(2)}) copy-start(bf16[128,128]{1,0:T(8,128)(2,1)} %param.23) | copy-start | bytes 98308
  181.7 1.0 copy-start.2
  181.8 1.0 copy-start.5
  234.6 0.7 copy-start.1
  240.8 61.8 %reduce-scatter.3.cloned.1.call-start = ((), (), s32[]{:S(2)}) async-start(), calls=%async_computation.5 | async-start | bytes 1327104 | tf_op jit(solution)/shard_map/reduce_scatter | solution.py:164
Sparse Core Ops, SparseCore 0:
  14.2 30.7 all-gather.5
  46.6 22.5 all-gather.7
  70.8 31.3 all-gather.3
  240.9 28.3 reduce-scatter.4
  271.6 31.0 reduce-scatter.2
where the time goes:
time: 315 us; the launch traced here: 312 us
  waiting for transfers between devices  82 us (26%)
  local copies, waits for them, and re-layouts  63.3 us (20%)
  other arithmetic  56.8 us (18%)
  blocking collectives  54.9 us (17%)
  matrix products  39.9 us (13%)
  between operations  14 us (4%)
    reduce_scatter x1, waiting for transfers between devices, shards(): lax.psum_scatter(summed.astype(jnp.bfloat16), 'col', scatter_dimension=1,...  29.3 us
    pmax x1, blocking collectives, shards(): lax.pmax(local_max.astype(jnp.bfloat16), 'col').astype(local_max.dtype)  28.8 us
    all_gather x1, waiting for transfers between devices, shards(): lax.all_gather(pair_state, 'col', axis=0, tiled=True)  27.3 us
    dynamic_update_slice x8, other arithmetic, rows_blocks(): normed_groups, left_groups = lax.map(one_group, grouped)  18.6 us
    reduce_scatter x1, waiting for transfers between devices, shards(): lax.psum_scatter(totals.astype(jnp.bfloat16), 'col', scatter_dimension=2,...  15.6 us
    reduce_sum x11, other arithmetic, normalize(): variance = jnp.mean(centered * centered, axis=-1, keepdims=True)  15.2 us
    all_gather x1, blocking collectives, shards(): lax.all_gather(keys_own, 'row', axis=1, tiled=True)  14 us
    dot_general x9, matrix products, gated_branch(): jnp.einsum('ikc,ce->ike', normed, weight, preferred_element_type=jnp.floa...  13.1 us
  transfers between devices with their start and end apart: 5, of which 4 were waited for; matrix products, arithmetic and copies ran while one was open for 13% of the time, Pallas kernels for 0%

commit v1 on v0

v1 whole, which is shorter than its diff:
```python
import functools
import math

import jax
import jax.numpy as jnp
from jax import lax
from jax.experimental import pallas as pl
from jax.experimental.pallas import tpu as pltpu
from jax.sharding import PartitionSpec as P

epsilon = 1e-05
AXES = ("row", "col")
SUB = 8
LANES = 128
VMEM_LIMIT = 56 * 1024 * 1024
EXCLUDED = -1e30


def layer_norm(values, gain):
    mean = jnp.mean(values, axis=-1, keepdims=True)
    centered = values - mean
    variance = jnp.mean(centered * centered, axis=-1, keepdims=True)
    scaled = centered * lax.rsqrt(variance + epsilon)
    return scaled if gain is None else scaled * gain


def sigmoid(values):
    return 0.5 * jnp.tanh(0.5 * values) + 0.5


def gated(normed, weight):
    width = weight.shape[1] // 2
    hidden = jnp.dot(normed, weight, preferred_element_type=jnp.float32)
    return sigmoid(hidden[:, :width]) * hidden[:, width:]


def right_kernel(first_ref, mask_ref, pair_ref, valid_ref, gain_ref, weight_ref, right_ref):
    rows = pair_ref.shape[0]
    gain = gain_ref[...]
    weight = weight_ref[...]
    valid = valid_ref[...]

    def row(i, carry):
        normed = layer_norm(pair_ref[i].astype(jnp.float32), gain).astype(jnp.bfloat16)
        own = (mask_ref[first_ref[0] + i] == 1).astype(jnp.float32)
        right_ref[i] = (gated(normed, weight) * (valid * own)).astype(jnp.bfloat16)
        return carry

    lax.fori_loop(0, rows, row, 0, unroll=2)


def left_kernel(
    block_count, meta_ref, mask_ref, same_ref, other_ref, gain_ref, weight_ref,
    left_ref, tile_ref, floats,
):
    rows, tokens, channels = same_ref.shape
    gain = gain_ref[...]
    weight = weight_ref[...]
    row_index, col_index, same_col = meta_ref[0], meta_ref[1], meta_ref[2]
    col_count = meta_ref[3]
    floats[:, tokens:] = jnp.zeros((rows, SUB, channels), jnp.float32)
    for chunk, pair_ref in enumerate((same_ref, other_ref)):
        chunk_col = same_col ^ chunk
        base = (chunk_col % 2) * rows
        first = (row_index * col_count + chunk_col) * rows

        def row(i, carry):
            values = pair_ref[i].astype(jnp.float32)
            floats[i, :tokens] = values
            normed = layer_norm(values, gain).astype(jnp.bfloat16)
            own = (mask_ref[first + i] == 1).astype(jnp.float32)
            left_ref[base + i] = (gated(normed, weight) * own).astype(jnp.bfloat16)
            return carry

        lax.fori_loop(0, rows, row, 0, unroll=2)
        for i in range(rows):
            for block in range(block_count):
                start = ((row_index ^ block) * col_count + col_index) * rows
                tile_ref[base + i, block] = floats[i, pl.ds(start, SUB), :]


def tile_kernel(block_count, carried, meta_ref, left_ref, *refs):
    right_refs = refs[:block_count]
    refs = refs[block_count:]
    tile_ref, gain_ref, mix_ref, gate_ref, out_ref, bias_ref = refs[:6]
    new_ref, head_ref, left_f, right_f, mixed_f = refs[6 + 2 * carried :]
    pair_rows, tokens, channels = left_ref.shape
    rows = pair_rows // 2
    row_index = meta_ref[0]
    left_f[...] = left_ref[...].astype(jnp.float32)
    for block in range(block_count):
        right_f[block * rows : (block + 1) * rows] = right_refs[block][...].astype(jnp.float32)
    mixed_f[:, :, rows:, :] = jnp.zeros((pair_rows, block_count, SUB - rows, channels), jnp.float32)

    def step(n, carry):
        block, half = n // 2, n % 2

        def slab(k, sums):
            at = pl.ds(pl.multiple_of(k * SUB, SUB), SUB)
            lefts = [left_f[half * rows + i, at, :] for i in range(rows)]
            rights = [right_f[block * rows + t, at, :] for t in range(rows)]
            return tuple(
                sums[i * rows + t] + lefts[i] * rights[t] for i in range(rows) for t in range(rows)
            )

        zero = jnp.zeros((SUB, channels), jnp.float32)
        sums = lax.fori_loop(0, tokens // SUB, slab, (zero,) * (rows * rows), unroll=4)
        for i in range(rows):
            for t in range(rows):
                mixed_f[half * rows + i, block, t : t + 1, :] = jnp.sum(
                    sums[i * rows + t], axis=0, keepdims=True
                )
        return carry

    lax.fori_loop(0, 2 * block_count, step, 0)
    flat = pair_rows * block_count * SUB
    mixed = mixed_f[...].reshape(flat, channels)
    mixed_norm = layer_norm(mixed, mix_ref[...]).astype(jnp.bfloat16)
    pair = tile_ref[...].reshape(flat, channels)
    normed = layer_norm(pair, gain_ref[...]).astype(jnp.bfloat16)
    gate = sigmoid(jnp.dot(normed, gate_ref[...], preferred_element_type=jnp.float32))
    update = jnp.dot(mixed_norm, out_ref[...], preferred_element_type=jnp.float32)
    pair_new = (pair + gate * update).astype(jnp.bfloat16).astype(jnp.float32)
    split = pair_new.reshape(pair_rows, block_count, SUB, channels)
    for block in range(block_count):
        new_ref[:, row_index ^ block, 0] = split[:, block, :rows, :].astype(jnp.bfloat16)
    bias_input = layer_norm(pair_new, None).astype(jnp.bfloat16)
    bias = lax.dot_general(
        bias_ref[...], bias_input, (((1,), (1,)), ((), ())), preferred_element_type=jnp.float32
    )
    head_ref[0] = bias.astype(jnp.bfloat16)


def project_kernel(block_count, meta_ref, *refs):
    single_refs = refs[:block_count]
    weight_ref, query_ref, key_ref, value_ref, rows_f, own_f = refs[block_count:]
    col_count, samples, rows, width = single_refs[0].shape
    rows_f[...] = jnp.zeros_like(rows_f)
    own_f[...] = jnp.zeros_like(own_f)
    for col in range(col_count):
        for block in range(block_count):
            at = col * block_count + block
            values = single_refs[block][col].astype(jnp.float32)
            for s in range(samples):
                rows_f[s, at, :rows, :] = values[s]
                if block == 0:
                    own_f[s, meta_ref[1] ^ col, :rows, :] = values[s]
    for s in range(samples):
        own = own_f[s].reshape(-1, width).astype(jnp.bfloat16)
        query_ref[s] = jnp.dot(
            own, weight_ref[:, :width], preferred_element_type=jnp.float32
        ).astype(jnp.bfloat16)
        full = rows_f[s].reshape(-1, width).astype(jnp.bfloat16)
        for target, at in ((key_ref, width), (value_ref, 2 * width)):
            product = jnp.dot(
                full, weight_ref[:, at : at + width], preferred_element_type=jnp.float32
            )
            target[s] = product.T.astype(jnp.bfloat16)


def attend_kernel(col_count, token_rows, head_count, query_ref, key_ref, value_ref, *refs):
    bias_refs = refs[:col_count]
    allowed_ref, merge_ref, result_ref, bias_f, joined = refs[col_count:]
    samples, query_rows, width = query_ref.shape
    key_count = key_ref.shape[2]
    head_width = width // head_count
    scale = 1.0 / math.sqrt(head_width)
    part = key_count // col_count
    group = LANES // part
    pairs = bias_refs[0].shape[0]
    lane_tiles = bias_refs[0].shape[2] // LANES
    lane = lax.broadcasted_iota(jnp.int32, (head_count, LANES), 1) // part
    for col in range(col_count):
        for t in range(token_rows, SUB):
            bias_f[col * SUB + t] = jnp.zeros((head_count, key_count), jnp.float32)
    for pair in range(pairs):
        for tile in range(lane_tiles):
            pieces = [
                ref[pair, :, tile * LANES : (tile + 1) * LANES].astype(jnp.float32)
                for ref in bias_refs
            ]
            for m in range(group):
                inside = tile * group + m
                col = 2 * pair + inside // token_rows
                row = col * SUB + inside % token_rows
                for target in range(col_count // group):
                    total = None
                    for u in range(group):
                        piece = pieces[target * group + u]
                        shift = ((u - m) * part) % LANES
                        if shift:
                            piece = pltpu.roll(piece, shift, 1)
                        total = piece if total is None else jnp.where(lane == u, piece, total)
                    bias_f[row, :, target * LANES : (target + 1) * LANES] = total
    allowed = allowed_ref[...]
    for h in range(head_count):
        at = slice(h * head_width, (h + 1) * head_width)
        bias = bias_f[:, h, :] + allowed
        for s in range(samples):
            scores = jnp.dot(
                query_ref[s, :, at], key_ref[s, at, :], preferred_element_type=jnp.float32
            )
            scores = scores * scale + bias
            weights = jnp.exp(scores - jnp.max(scores, axis=-1, keepdims=True))
            weights = weights.astype(jnp.bfloat16)
            total = jnp.sum(weights.astype(jnp.float32), axis=-1, keepdims=True)
            summed = lax.dot_general(
                weights, value_ref[s, at, :], (((1,), (1,)), ((), ())),
                preferred_element_type=jnp.float32,
            )
            joined[s, :, at] = summed / total
    merge = merge_ref[...]
    for s in range(samples):
        merged = jnp.dot(
            joined[s].astype(jnp.bfloat16), merge, preferred_element_type=jnp.float32
        )
        split = merged.reshape(col_count, SUB, width)
        result_ref[:, s] = split[:, :token_rows, :].astype(jnp.bfloat16)


def params():
    return pltpu.CompilerParams(vmem_limit_bytes=VMEM_LIMIT)


def cost(flops, moved):
    return pl.CostEstimate(flops=flops, bytes_accessed=moved, transcendentals=0)


def whole(shape):
    return pl.BlockSpec(shape, lambda *_: (0,) * len(shape))


def shards(
    pair_state,
    single_rep,
    token_mask,
    chain_ids,
    pair_gain,
    mix_gain,
    left_weight,
    right_weight,
    gate_weight,
    out_weight,
    bias_weight,
    token_weight,
    merge_weight,
):
    row_count = lax.axis_size("row")
    col_count = lax.axis_size("col")
    row_index = lax.axis_index("row")
    col_index = lax.axis_index("col")
    rows, tokens, channels = pair_state.shape
    samples, _, width = single_rep.shape
    heads = bias_weight.shape[1]
    chips = col_count // 2
    own_samples = samples // col_count
    keys = tokens // rows * SUB
    part = row_count * SUB
    core = col_index % 2
    chip = col_index // 2

    def send(values, by_row, by_col):
        steps = [
            (r * col_count + c, (r ^ by_row) * col_count + (c ^ by_col))
            for r in range(row_count)
            for c in range(col_count)
        ]
        return lax.ppermute(values, AXES, steps)

    gain = pair_gain.reshape(1, channels)
    mix = mix_gain.reshape(1, channels)
    valid = (token_mask == 1).astype(jnp.float32)

    first = ((row_index * col_count + col_index) * rows).astype(jnp.int32)[None]
    right_own = pl.pallas_call(
        right_kernel,
        grid_spec=pltpu.PrefetchScalarGridSpec(
            num_scalar_prefetch=2,
            grid=(1,),
            in_specs=[
                whole(pair_state.shape), whole((tokens, 1)), whole(gain.shape),
                whole(right_weight.shape),
            ],
            out_specs=whole(pair_state.shape),
        ),
        out_shape=jax.ShapeDtypeStruct(pair_state.shape, jnp.bfloat16),
        compiler_params=params(),
        name="right_rows",
    )(first, token_mask, pair_state, valid[:, None], gain, right_weight)
    rights = [right_own] + [send(right_own, k, 0) for k in range(1, row_count)]

    same = [pair_state] + [send(pair_state, 0, 2 * k) for k in range(1, chips)]
    other = [send(values, 0, 1) for values in same]

    by_chip = single_rep.reshape(chips, 2, own_samples, rows, width)
    arrived = []
    for k in range(chips):
        piece = lax.dynamic_index_in_dim(by_chip, chip ^ k, 0, False)
        arrived.append(send(piece, 0, 2 * k) if k else piece)
    arrived = jnp.stack(arrived)
    kept = lax.dynamic_index_in_dim(arrived, core, 1, False)
    crossed = send(lax.dynamic_index_in_dim(arrived, 1 - core, 1, False), 0, 1)
    block_single = jnp.stack([kept, crossed], axis=1).reshape(
        col_count, own_samples, rows, width
    )
    singles = [block_single] + [send(block_single, k, 0) for k in range(1, row_count)]

    def meta_of(k):
        return jnp.stack(
            [row_index, col_index, col_index ^ (2 * k), jnp.int32(col_count), chip ^ k]
        ).astype(jnp.int32)

    query_rows = col_count * SUB
    queries, key_cols, value_cols = pl.pallas_call(
        functools.partial(project_kernel, row_count),
        grid_spec=pltpu.PrefetchScalarGridSpec(
            num_scalar_prefetch=1,
            grid=(1,),
            in_specs=[whole(block_single.shape)] * row_count + [whole(token_weight.shape)],
            out_specs=[
                whole((own_samples, query_rows, width)),
                whole((own_samples, width, keys)),
                whole((own_samples, width, keys)),
            ],
            scratch_shapes=[
                pltpu.VMEM((own_samples, keys // SUB, SUB, width), jnp.float32),
                pltpu.VMEM((own_samples, col_count, SUB, width), jnp.float32),
            ],
        ),
        out_shape=[
            jax.ShapeDtypeStruct((own_samples, query_rows, width), jnp.bfloat16),
            jax.ShapeDtypeStruct((own_samples, width, keys), jnp.bfloat16),
            jax.ShapeDtypeStruct((own_samples, width, keys), jnp.bfloat16),
        ],
        compiler_params=params(),
        name="project_tokens",
    )(meta_of(0), *singles, token_weight)

    inner = jnp.arange(SUB, dtype=jnp.int32)
    col_order = jnp.arange(col_count, dtype=jnp.int32) ^ col_index
    row_order = jnp.arange(row_count, dtype=jnp.int32) ^ row_index
    key_ids = (
        (row_order[None, :, None] * col_count + col_order[:, None, None]) * rows + inner
    ).reshape(keys)
    key_real = jnp.broadcast_to(inner < rows, (col_count, row_count, SUB)).reshape(keys)
    query_ids = (
        (row_index * col_count + jnp.arange(col_count, dtype=jnp.int32)[:, None]) * rows + inner
    ).reshape(query_rows)
    token_ids = jnp.arange(tokens, dtype=jnp.int32)

    def pick(ids, table):
        return jnp.sum(jnp.where(ids[:, None] == token_ids[None, :], table[None, :], 0), axis=1)

    key_chain = pick(key_ids, chain_ids)
    key_valid = pick(key_ids, (token_mask == 1).astype(jnp.int32))
    query_chain = pick(query_ids, chain_ids)
    allowed = (key_valid[None, :] > 0) & (query_chain[:, None] == key_chain[None, :]) | (
        query_ids[:, None] == key_ids[None, :]
    )
    allowed = jnp.where(allowed & key_real[None, :], 0.0, EXCLUDED).astype(jnp.float32)

    bias_rows = bias_weight.T
    new_shape = (rows * col_count, row_count, 1, rows, channels)
    head_shape = (chips, heads, 2 * rows * part)
    pair_new = pair_heads = None
    for k in range(chips):
        meta = meta_of(k)
        left_rows, tile = pl.pallas_call(
            functools.partial(left_kernel, row_count),
            grid_spec=pltpu.PrefetchScalarGridSpec(
                num_scalar_prefetch=2,
                grid=(1,),
                in_specs=[
                    whole(pair_state.shape), whole(pair_state.shape), whole(gain.shape),
                    whole(left_weight.shape),
                ],
                out_specs=[
                    whole((2 * rows, tokens, channels)),
                    whole((2 * rows, row_count, SUB, channels)),
                ],
                scratch_shapes=[pltpu.VMEM((rows, tokens + SUB, channels), jnp.float32)],
            ),
            out_shape=[
                jax.ShapeDtypeStruct((2 * rows, tokens, channels), jnp.bfloat16),
                jax.ShapeDtypeStruct((2 * rows, row_count, SUB, channels), jnp.float32),
            ],
            compiler_params=params(),
            name=f"left_rows_{k}",
        )(meta, token_mask, same[k], other[k], gain, left_weight)
        carried = [] if pair_new is None else [pair_new, pair_heads]
        operands = [left_rows, *rights, tile, gain, mix, gate_weight, out_weight, bias_rows]
        place = 1 + len(operands)
        pair_new, pair_heads = pl.pallas_call(
            functools.partial(tile_kernel, row_count, len(carried) // 2),
            grid_spec=pltpu.PrefetchScalarGridSpec(
                num_scalar_prefetch=1,
                grid=(1,),
                in_specs=[whole(x.shape) for x in operands]
                + [pl.BlockSpec(memory_space=pl.ANY)] * len(carried),
                out_specs=[
                    pl.BlockSpec(
                        (2 * rows,) + new_shape[1:], lambda _, ref: (ref[4], 0, 0, 0, 0)
                    ),
                    pl.BlockSpec((1,) + head_shape[1:], lambda _, ref: (ref[4], 0, 0)),
                ],
                scratch_shapes=[
                    pltpu.VMEM((2 * rows, tokens, channels), jnp.float32),
                    pltpu.VMEM((rows * row_count, tokens, channels), jnp.float32),
                    pltpu.VMEM((2 * rows, row_count, SUB, channels), jnp.float32),
                ],
            ),
            out_shape=[
                jax.ShapeDtypeStruct(new_shape, jnp.bfloat16),
                jax.ShapeDtypeStruct(head_shape, jnp.bfloat16),
            ],
            input_output_aliases={place: 0, place + 1: 1} if carried else {},
            compiler_params=params(),
            name=f"pair_tile_{k}",
        )(meta, *operands, *carried)

    near = [pair_heads] + [send(pair_heads, 0, 2 * k) for k in range(1, chips)]
    biases = []
    for values in near:
        biases += [values, send(values, 0, 1)]

    merged = pl.pallas_call(
        functools.partial(attend_kernel, col_count, rows, heads),
        out_shape=jax.ShapeDtypeStruct((col_count, own_samples, rows, width), jnp.bfloat16),
        scratch_shapes=[
            pltpu.VMEM((query_rows, heads, keys), jnp.float32),
            pltpu.VMEM((own_samples, query_rows, width), jnp.float32),
        ],
        compiler_params=params(),
        name="attend",
    )(queries, key_cols, value_cols, *biases, allowed, merge_weight)
    attention_out = lax.all_to_all(merged, "col", 0, 0, tiled=True)
    return pair_new, attention_out.reshape(samples, rows, width)


def solution(mesh):
    in_specs = (
        P(("row", "col"), None, None),
        P(None, ("row", "col"), None),
    ) + (P(),) * 11
    out_specs = (P("row", None, "col", None, None), P(None, ("row", "col"), None))
    return jax.shard_map(shards, mesh=mesh, in_specs=in_specs, out_specs=out_specs, check_vma=False)
```

time: 315 us -> 136 us (0.43)
  Pallas kernels: 0 us -> 62.2 us
  waiting for transfers between devices: 82 us -> 24 us
  blocking collectives: 54.9 us -> 0 us
  other arithmetic: 56.8 us -> 3.41 us
  local copies, waits for them, and re-layouts: 63.3 us -> 11.6 us
  matrix products: 39.9 us -> 0 us
  starting transfers between devices: 0.42 us -> 33.5 us
  between operations: 14 us -> 0.97 us
    pallas_call x0 -> x11, Pallas kernels: none -> 62.2 us  [the longest x4 25.8 us: shards(): pl.pallas_call(functools.partial(tile_kernel, row_count, len(carried) //...]
    reduce_scatter x2 -> x0, waiting for transfers between devices: 44.8 us -> none  [the longest x1 29.3 us: shards(): lax.psum_scatter(summed.astype(jnp.bfloat16), 'col', scatter_dimension=1,...]
    dot_general x17 -> x0, matrix products: 39.9 us -> none  [the longest x9 13.1 us: gated_branch(): jnp.einsum('ikc,ce->ike', normed, weight, preferred_element_type=jnp.floa...]
    all_gather x3 -> x0, waiting for transfers between devices: 36.5 us -> none  [the longest x1 27.3 us: shards(): lax.all_gather(pair_state, 'col', axis=0, tiled=True)]
    ppermute x0 -> x24, starting transfers between devices: none -> 29.9 us  [send(): return lax.ppermute(values, AXES, steps)]
    pmax x1 -> x0, blocking collectives: 28.8 us -> none  [shards(): lax.pmax(local_max.astype(jnp.bfloat16), 'col').astype(local_max.dtype)]
    reduce_sum x21 -> x2, other arithmetic: 29.5 us -> 1.66 us  [pick(): jnp.sum(jnp.where(ids[:, None] == token_ids[None, :], table[None, :], 0),...]
    all_gather x2 -> x0, blocking collectives: 26.1 us -> none  [the longest x1 14 us: shards(): lax.all_gather(keys_own, 'row', axis=1, tiled=True)]
  transfers between devices with their start and end apart: 5 -> 25, of which waited for: 4 -> 7; matrix products, arithmetic and copies ran while one was open for 13% -> 7% of each run, Pallas kernels for 0% -> 40%
where the time goes in v1:
time: 136 us
  Pallas kernels  62.2 us (46%)
  starting transfers between devices  33.5 us (25%)
  waiting for transfers between devices  24 us (18%)
  local copies, waits for them, and re-layouts  11.6 us (9%)
  other arithmetic  3.41 us (3%)
    ppermute x24, starting transfers between devices, send(): return lax.ppermute(values, AXES, steps)  29.9 us
    pallas_call x4, Pallas kernels, shards(): pl.pallas_call(functools.partial(tile_kernel, row_count, len(carried) //...  25.8 us
    pallas_call x4, Pallas kernels, shards(): pl.pallas_call(functools.partial(left_kernel, row_count), grid_spec=pltpu...  19.4 us
    ppermute x24, waiting for transfers between devices, send(): return lax.ppermute(values, AXES, steps)  17.9 us
    pallas_call x1, Pallas kernels, shards(): pl.pallas_call(functools.partial(attend_kernel, col_count, rows, heads),...  7.25 us
    all_to_all x1, waiting for transfers between devices, shards(): attention_out = lax.all_to_all(merged, 'col', 0, 0, tiled=True)  6.17 us
    pallas_call x1, Pallas kernels, shards(): pl.pallas_call(functools.partial(project_kernel, row_count), grid_spec=pl...  6.05 us
    unnamed x44, local copies, waits for them, and re-layouts  4.29 us
  transfers between devices with their start and end apart: 25, of which 7 were waited for; matrix products, arithmetic and copies ran while one was open for 7% of the time, Pallas kernels for 40%

profile of v1, /device:TPU:0, one launch (start us, length us, event | category | flops | bytes accessed | tf_op | source)
XLA Modules:
  0.0 135.7 jit_solution(13528554293559261832)
XLA Ops:
  0.6 0.5 collective-permute-start.9
  1.1 2.7 %collective-permute-start.7 = (bf16[6,192,128]{2,1,0:T(8,128)(2,1)}, bf16[6,192,128]{2,1,0:T(8,128)(2,1)S(1)}, u32[]{:S(2)}, u32[]{:S(2)}) collective-permute-start(bf16[6,192,128]{2,1,0:T(8,128)(2,1)} %same_ref.1), channel_id=1, source_target_pairs={{0,2},{1,3},{2,0},{3,1},{4,6},{5,7},{6,4},{7,5},{8,10},{9,11},{10,... | collective-permute-start | bytes 884744 | tf_op jit(solution)/shard_map/ppermute | solution.py:268
  3.8 1.0 reshape.122
  4.8 0.1 constant_dynamic-slice_fusion.4
  4.9 0.1 collective-permute-start.10
  5.1 3.0 %collective-permute-start.11 = (bf16[2,2,6,768]{3,2,1,0:T(8,128)(2,1)S(1)}, bf16[2,2,6,768]{3,2,1,0:T(8,128)(2,1)S(1)}, u32[]{:S(2)}, u32[]{:S(2)}) collective-permute-start(bf16[2,2,6,768]{3,2,1,0:T(8,128)(2,1)S(1)} %bitcast.47), channel_id=1, source_target_pairs={{0,4},{1,5},{2,6},{3,7},{4,0},{5,1},{6,2},{7,3},{8,12},{9,13},{10,... | collective-permute-start | bytes 110600 | tf_op jit(solution)/shard_map/ppermute | solution.py:268
  8.1 1.4 %collective-permute-start.12 = (bf16[2,2,6,768]{3,2,1,0:T(8,128)(2,1)S(1)}, bf16[2,2,6,768]{3,2,1,0:T(8,128)(2,1)S(1)}, u32[]{:S(2)}, u32[]{:S(2)}) collective-permute-start(bf16[2,2,6,768]{3,2,1,0:T(8,128)(2,1)S(1)} %bitcast.46), channel_id=1, source_target_pairs={{0,6},{1,7},{2,4},{3,5},{4,2},{5,3},{6,0},{7,1},{8,14},{9,15},{10,... | collective-permute-start | bytes 110600 | tf_op jit(solution)/shard_map/ppermute | solution.py:268
  9.5 0.1 add_multiply_fusion
  9.6 0.1 iota_add_fusion
  9.7 0.7 fusion
  10.4 0.8 copy.49.valid_ref
  11.2 0.1 add.116
  11.3 3.7 %right_rows.1.refs_0_ = bf16[6,192,128]{2,1,0:T(8,128)(2,1)} custom-call(s32[1]{0:T(128)} %bitcast.5.first_ref, s32[192]{0:T(256)} %mask_ref.9, bf16[6,192,128]{2,1,0:T(8,128)(2,1)} %same_ref.1, f32[192,1]{1,0:T(8,128)} %copy.49.valid_ref, f32[1,128]{1,0:T(1,128)} %bitcast.49, bf16[128,256]{1,0:T(8,128)(2,1)} %weight_ref.6), custom_call_target="tpu_custom_call" | custom-call | tf_op jit(solution)/shard_map/right_rows/pallas_call | solution.py:275
  15.0 1.7 %collective-permute-start.5 = (bf16[6,192,128]{2,1,0:T(8,128)(2,1)}, bf16[6,192,128]{2,1,0:T(8,128)(2,1)S(1)}, u32[]{:S(2)}, u32[]{:S(2)}) collective-permute-start(bf16[6,192,128]{2,1,0:T(8,128)(2,1)} %same_ref.1), channel_id=1, source_target_pairs={{0,4},{1,5},{2,6},{3,7},{4,0},{5,1},{6,2},{7,3},{8,12},{9,13},{10,... | collective-permute-start | bytes 884744 | tf_op jit(solution)/shard_map/ppermute | solution.py:268
  16.7 1.9 %collective-permute-start = (bf16[6,192,128]{2,1,0:T(8,128)(2,1)}, bf16[6,192,128]{2,1,0:T(8,128)(2,1)S(1)}, u32[]{:S(2)}, u32[]{:S(2)}) collective-permute-start(bf16[6,192,128]{2,1,0:T(8,128)(2,1)} %same_ref.1), channel_id=1, source_target_pairs={{0,6},{1,7},{2,4},{3,5},{4,2},{5,3},{6,0},{7,1},{8,14},{9,15},{10,... | collective-permute-start | bytes 884744 | tf_op jit(solution)/shard_map/ppermute | solution.py:268
  18.7 0.1 collective-permute-start.13
  18.7 0.8 select_reduce_fusion.1
  19.5 0.5 collective-permute-done.13
  20.0 1.5 %collective-permute-start.2 = (bf16[6,192,128]{2,1,0:T(8,128)(2,1)}, bf16[6,192,128]{2,1,0:T(8,128)(2,1)S(1)}, u32[]{:S(2)}, u32[]{:S(2)}) collective-permute-start(bf16[6,192,128]{2,1,0:T(8,128)(2,1)} %right_rows.1.refs_0_), channel_id=1, source_target_pairs={{0,8},{1,9},{2,10},{3,11},{4,12},{5,13},{6,14},{7,15},{8,0},{9,1},... | collective-permute-start | bytes 884744 | tf_op jit(solution)/shard_map/ppermute | solution.py:268
  21.5 0.1 iota_add_fusion.1
  21.6 1.5 %collective-permute-start.3 = (bf16[6,192,128]{2,1,0:T(8,128)(2,1)}, bf16[6,192,128]{2,1,0:T(8,128)(2,1)S(1)}, u32[]{:S(2)}, u32[]{:S(2)}) collective-permute-start(bf16[6,192,128]{2,1,0:T(8,128)(2,1)} %right_rows.1.refs_0_), channel_id=1, source_target_pairs={{0,16},{1,17},{2,18},{3,19},{4,20},{5,21},{6,22},{7,23},{8,24},{9,... | collective-permute-start | bytes 884744 | tf_op jit(solution)/shard_map/ppermute | solution.py:268
  23.1 6.2 %collective-permute-done.2.refs_1_ = bf16[6,192,128]{2,1,0:T(8,128)(2,1)S(1)} collective-permute-done((bf16[6,192,128]{2,1,0:T(8,128)(2,1)}, bf16[6,192,128]{2,1,0:T(8,128)(2,1)S(1)}, u32[]{:S(2)}, u32[]{:S(2)}) %collective-permute-start.2) | collective-permute-done | bytes 294944 | tf_op jit(solution)/shard_map/ppermute | solution.py:268
  29.3 2.4 %collective-permute-start.4 = (bf16[6,192,128]{2,1,0:T(8,128)(2,1)}, bf16[6,192,128]{2,1,0:T(8,128)(2,1)S(1)}, u32[]{:S(2)}, u32[]{:S(2)}) collective-permute-start(bf16[6,192,128]{2,1,0:T(8,128)(2,1)} %right_rows.1.refs_0_), channel_id=1, source_target_pairs={{0,24},{1,25},{2,26},{3,27},{4,28},{5,29},{6,30},{7,31},{8,16},{9,... | collective-permute-start | bytes 884744 | tf_op jit(solution)/shard_map/ppermute | solution.py:268
  31.8 5.8 %collective-permute-done.5.same_ref = bf16[6,192,128]{2,1,0:T(8,128)(2,1)S(1)} collective-permute-done((bf16[6,192,128]{2,1,0:T(8,128)(2,1)}, bf16[6,192,128]{2,1,0:T(8,128)(2,1)S(1)}, u32[]{:S(2)}, u32[]{:S(2)}) %collective-permute-start.5) | collective-permute-done | bytes 294944 | tf_op jit(solution)/shard_map/ppermute | solution.py:268
  37.6 0.5 collective-permute-start.1
  38.1 0.1 add.122
  38.2 1.6 %collective-permute-start.14 = (bf16[8,2,6,768]{3,2,1,0:T(8,128)(2,1)S(1)}, bf16[8,2,6,768]{3,2,1,0:T(8,128)(2,1)S(1)}, u32[]{:S(2)}, u32[]{:S(2)}) collective-permute-start(bf16[8,2,6,768]{3,2,1,0:T(8,128)(2,1)S(1)} %bitcast.34), channel_id=1, source_target_pairs={{0,8},{1,9},{2,10},{3,11},{4,12},{5,13},{6,14},{7,15},{8,0},{9,1},... | collective-permute-start | bytes 442376 | tf_op jit(solution)/shard_map/ppermute | solution.py:268
  39.8 1.5 %collective-permute-start.15 = (bf16[8,2,6,768]{3,2,1,0:T(8,128)(2,1)S(1)}, bf16[8,2,6,768]{3,2,1,0:T(8,128)(2,1)}, u32[]{:S(2)}, u32[]{:S(2)}) collective-permute-start(bf16[8,2,6,768]{3,2,1,0:T(8,128)(2,1)S(1)} %bitcast.35), channel_id=1, source_target_pairs={{0,16},{1,17},{2,18},{3,19},{4,20},{5,21},{6,22},{7,23},{8,24},{9,... | collective-permute-start | bytes 442376 | tf_op jit(solution)/shard_map/ppermute | solution.py:268
  41.3 0.9 select_reduce_fusion.2
  42.2 0.7 stack.83.meta_ref
  42.9 0.7 stack.81.meta_ref
  43.5 0.7 stack.78.meta_ref
  44.2 0.6 stack.75.meta_ref
  44.8 4.8 %left_rows_0.1 = (bf16[12,192,128]{2,1,0:T(8,128)(2,1)}, f32[12,4,8,128]{3,2,1,0:T(8,128)}) custom-call(s32[5]{0:T(128)} %stack.83.meta_ref, s32[192]{0:T(256)} %mask_ref.9, bf16[6,192,128]{2,1,0:T(8,128)(2,1)} %same_ref.1, bf16[6,192,128]{2,1,0:T(8,128)(2,1)} %copy-done.6, f32[1,128]{1,0:T(1,128)} %bitcast.50, bf16[128,256]{1,0:T(8,128)(2,1)} %weight_ref.9), custom_call_target="tpu_custom_call" | custom-call | tf_op jit(solution)/shard_map/left_rows_0/pallas_call | solution.py:368
  49.7 6.4 %pair_tile_0.1 = (bf16[48,4,1,6,128]{4,3,2,1,0:T(8,128)(2,1)}, bf16[4,16,384]{2,1,0:T(8,128)(2,1)}) custom-call(s32[5]{0:T(128)} %stack.83.meta_ref, bf16[12,192,128]{2,1,0:T(8,128)(2,1)} %get-tuple-element.27.left_ref, bf16[6,192,128]{2,1,0:T(8,128)(2,1)} %right_rows.1.refs_0_, bf16[6,192,128]{2,1,0:T(8,128)(2,1)} %copy-done.1, ...), custom_call_target="tpu_custom_call" | custom-call | tf_op jit(solution)/shard_map/pair_tile_0/pallas_call | solution.py:393
  56.1 0.7 copy-done.11
  56.8 4.8 %left_rows_1.1 = (bf16[12,192,128]{2,1,0:T(8,128)(2,1)}, f32[12,4,8,128]{3,2,1,0:T(8,128)}) custom-call(s32[5]{0:T(128)} %stack.81.meta_ref, s32[192]{0:T(256)} %mask_ref.9, bf16[6,192,128]{2,1,0:T(8,128)(2,1)} %copy-done.5, bf16[6,192,128]{2,1,0:T(8,128)(2,1)} %copy-done.11, f32[1,128]{1,0:T(1,128)} %bitcast.52, bf16[128,256]{1,0:T(8,128)(2,1)} %weight_ref.9), custom_call_target="tpu_custom_call" | custom-call | tf_op jit(solution)/shard_map/left_rows_1/pallas_call | solution.py:368
  61.7 0.7 copy-done.10
  62.4 4.9 %left_rows_2.1 = (bf16[12,192,128]{2,1,0:T(8,128)(2,1)}, f32[12,4,8,128]{3,2,1,0:T(8,128)}) custom-call(s32[5]{0:T(128)} %stack.78.meta_ref, s32[192]{0:T(256)} %mask_ref.9, bf16[6,192,128]{2,1,0:T(8,128)(2,1)} %copy-done.7, bf16[6,192,128]{2,1,0:T(8,128)(2,1)} %copy-done.10, f32[1,128]{1,0:T(1,128)} %bitcast.53, bf16[128,256]{1,0:T(8,128)(2,1)} %weight_ref.9), custom_call_target="tpu_custom_call" | custom-call | tf_op jit(solution)/shard_map/left_rows_2/pallas_call | solution.py:368
  67.3 0.7 copy-done.9
  67.9 4.8 %left_rows_3.1 = (bf16[12,192,128]{2,1,0:T(8,128)(2,1)}, f32[12,4,8,128]{3,2,1,0:T(8,128)}) custom-call(s32[5]{0:T(128)} %stack.75.meta_ref, s32[192]{0:T(256)} %mask_ref.9, bf16[6,192,128]{2,1,0:T(8,128)(2,1)} %copy-done.8, bf16[6,192,128]{2,1,0:T(8,128)(2,1)} %copy-done.9, f32[1,128]{1,0:T(1,128)} %bitcast.54, bf16[128,256]{1,0:T(8,128)(2,1)} %weight_ref.9), custom_call_target="tpu_custom_call" | custom-call | tf_op jit(solution)/shard_map/left_rows_3/pallas_call | solution.py:368
  72.8 6.4 %pair_tile_1.1 = (bf16[48,4,1,6,128]{4,3,2,1,0:T(8,128)(2,1)}, bf16[4,16,384]{2,1,0:T(8,128)(2,1)}) custom-call(s32[5]{0:T(128)} %stack.81.meta_ref, bf16[12,192,128]{2,1,0:T(8,128)(2,1)} %get-tuple-element.25.left_ref, bf16[6,192,128]{2,1,0:T(8,128)(2,1)} %right_rows.1.refs_0_, ...), custom_call_target="tpu_custom_call", output_to_operand_aliasing={{0}: (12, {}), {1}: (13, {})} | custom-call | tf_op jit(solution)/shard_map/pair_tile_1/pallas_call | solution.py:393
  79.2 6.4 %pair_tile_2.1 = (bf16[48,4,1,6,128]{4,3,2,1,0:T(8,128)(2,1)}, bf16[4,16,384]{2,1,0:T(8,128)(2,1)}) custom-call(s32[5]{0:T(128)} %stack.78.meta_ref, bf16[12,192,128]{2,1,0:T(8,128)(2,1)} %get-tuple-element.23.left_ref, bf16[6,192,128]{2,1,0:T(8,128)(2,1)} %right_rows.1.refs_0_, ...), custom_call_target="tpu_custom_call", output_to_operand_aliasing={{0}: (12, {}), {1}: (13, {})} | custom-call | tf_op jit(solution)/shard_map/pair_tile_2/pallas_call | solution.py:393
  85.6 6.6 %pair_tile_3.1 = (bf16[48,4,1,6,128]{4,3,2,1,0:T(8,128)(2,1)}, bf16[4,16,384]{2,1,0:T(8,128)(2,1)}) custom-call(s32[5]{0:T(128)} %stack.75.meta_ref, bf16[12,192,128]{2,1,0:T(8,128)(2,1)} %get-tuple-element.21.left_ref, bf16[6,192,128]{2,1,0:T(8,128)(2,1)} %right_rows.1.refs_0_, ...), custom_call_target="tpu_custom_call", output_to_operand_aliasing={{0}: (12, {}), {1}: (13, {})} | custom-call | tf_op jit(solution)/shard_map/pair_tile_3/pallas_call | solution.py:393
  92.2 5.8 %collective-permute-start.18 = (bf16[4,16,384]{2,1,0:T(8,128)(2,1)}, bf16[4,16,384]{2,1,0:T(8,128)(2,1)S(1)}, u32[]{:S(2)}, u32[]{:S(2)}) collective-permute-start(bf16[4,16,384]{2,1,0:T(8,128)(2,1)} %get-tuple-element.39.refs_0_), channel_id=1, source_target_pairs={{0,2},{1,3},{2,0},{3,1},{4,6},{5,7},{6,4},{7,5},{8,10},{9,11},{10,... | collective-permute-start | bytes 147464 | tf_op jit(solution)/shard_map/ppermute | solution.py:268
  98.0 1.1 collective-permute-start.20
  99.1 1.5 %collective-permute-start.22 = (bf16[4,16,384]{2,1,0:T(8,128)(2,1)}, bf16[4,16,384]{2,1,0:T(8,128)(2,1)S(1)}, u32[]{:S(2)}, u32[]{:S(2)}) collective-permute-start(bf16[4,16,384]{2,1,0:T(8,128)(2,1)} %get-tuple-element.39.refs_0_), channel_id=1, source_target_pairs={{0,6},{1,7},{2,4},{3,5},{4,2},{5,3},{6,0},{7,1},{8,14},{9,15},{10,... | collective-permute-start | bytes 147464 | tf_op jit(solution)/shard_map/ppermute | solution.py:268
  100.6 0.1 and.34
  100.7 0.5 collective-permute-start.16
  101.3 0.5 collective-permute-start.19
  101.8 2.9 %collective-permute-done.20.refs_4_ = bf16[4,16,384]{2,1,0:T(8,128)(2,1)S(1)} collective-permute-done((bf16[4,16,384]{2,1,0:T(8,128)(2,1)}, bf16[4,16,384]{2,1,0:T(8,128)(2,1)S(1)}, u32[]{:S(2)}, u32[]{:S(2)}) %collective-permute-start.20) | collective-permute-done | bytes 49184 | tf_op jit(solution)/shard_map/ppermute | solution.py:268
  104.6 0.7 collective-permute-done.22.refs_6_
  105.3 0.7 and_select_fusion.refs_8_
  106.0 1.8 %collective-permute-done.16.refs_3_ = bf16[8,2,6,768]{3,2,1,0:T(8,128)(2,1)S(1)} collective-permute-done((bf16[8,2,6,768]{3,2,1,0:T(8,128)(2,1)S(1)}, bf16[8,2,6,768]{3,2,1,0:T(8,128)(2,1)S(1)}, u32[]{:S(2)}, u32[]{:S(2)}) %collective-permute-start.16) | collective-permute-done | bytes 147488 | tf_op jit(solution)/shard_map/ppermute | solution.py:268
  107.9 0.7 copy-done.13
  108.5 6.1 %project_tokens.1 = (bf16[2,64,768]{2,1,0:T(8,128)(2,1)}, bf16[2,768,256]{2,1,0:T(8,128)(2,1)}, bf16[2,768,256]{2,1,0:T(8,128)(2,1)}) custom-call(s32[5]{0:T(128)} %stack.83.meta_ref, bf16[8,2,6,768]{3,2,1,0:T(8,128)(2,1)} %bitcast.37, bf16[8,2,6,768]{3,2,1,0:T(8,128)(2,1)} %copy-done.12, bf16[8,2,6,768]{3,2,1,0:T(8,128)(2,1)} %collective-permute-done.15.refs_2_, ...), custom_call_target="tpu_custom_call" | custom-call | tf_op jit(solution)/shard_map/project_tokens/pallas_call | solution.py:314
  114.7 0.5 copy-done.17
  115.3 7.3 %attend.1 = bf16[8,2,6,768]{3,2,1,0:T(8,128)(2,1)} custom-call(bf16[2,64,768]{2,1,0:T(8,128)(2,1)} %get-tuple-element.36.query_ref, bf16[2,768,256]{2,1,0:T(8,128)(2,1)} %get-tuple-element.37.key_ref, bf16[2,768,256]{2,1,0:T(8,128)(2,1)} %get-tuple-element.38.value_ref, bf16[4,16,384]{2,1,0:T(8,128)(2,1)} %get-tuple-element.39.refs_0_, ...), custom_call_target="tpu_custom_call" | custom-call | tf_op jit(solution)/shard_map/attend/pallas_call | solution.py:426
  122.5 1.7 %copy.54 = bf16[8,2,6,768]{3,1,2,0:T(2,128)(2,1)} copy(bf16[8,2,6,768]{3,2,1,0:T(8,128)(2,1)} %attend.1) | data formatting | bytes 294912 | tf_op jit(solution)/shard_map/attend/pallas_call | solution.py:426
  124.2 3.7 %all-to-all-start = ((bf16[8,2,6,768]{3,1,2,0:T(2,128)(2,1)}), bf16[8,2,6,768]{3,1,2,0:T(2,128)(2,1)S(1)}, u32[]{:S(2)}, u32[]{:S(2)}) async-start(bf16[8,2,6,768]{3,1,2,0:T(2,128)(2,1)} %copy.54), calls=%async_computation | async-start | bytes 294912 | tf_op jit(solution)/shard_map/all_to_all | solution.py:436
  127.9 0.8 copy.56
  128.7 6.2 %all-to-all-done = bf16[8,2,6,768]{3,1,2,0:T(2,128)(2,1)S(1)} async-done(((bf16[8,2,6,768]{3,1,2,0:T(2,128)(2,1)}), bf16[8,2,6,768]{3,1,2,0:T(2,128)(2,1)S(1)}, u32[]{:S(2)}, u32[]{:S(2)}) %all-to-all-start) | async-done | bytes 147488 | tf_op jit(solution)/shard_map/all_to_all | solution.py:436
  134.9 0.1 copy.55
  135.0 0.7 reshape.124
  (73 shorter events, 0.4 us)
Async XLA Ops:
  0.6 21.0 %collective-permute-start.9 = (bf16[6,192,128]{2,1,0:T(8,128)(2,1)}, bf16[6,192,128]{2,1,0:T(8,128)(2,1)S(1)}, u32[]{:S(2)}, u32[]{:S(2)}) collective-permute-start(bf16[6,192,128]{2,1,0:T(8,128)(2,1)} %same_ref.1), channel_id=1, source_target_pairs={{0,1},{1,0},{2,3},{3,2},{4,5},{5,4},{6,7},{7,6},{8,9},{9,8},{10,11... | collective-permute-start | bytes 884744 | tf_op jit(solution)/shard_map/ppermute | solution.py:268
  1.1 30.6 %collective-permute-start.7 = (bf16[6,192,128]{2,1,0:T(8,128)(2,1)}, bf16[6,192,128]{2,1,0:T(8,128)(2,1)S(1)}, u32[]{:S(2)}, u32[]{:S(2)}) collective-permute-start(bf16[6,192,128]{2,1,0:T(8,128)(2,1)} %same_ref.1), channel_id=1, source_target_pairs={{0,2},{1,3},{2,0},{3,1},{4,6},{5,7},{6,4},{7,5},{8,10},{9,11},{10,... | collective-permute-start | bytes 884744 | tf_op jit(solution)/shard_map/ppermute | solution.py:268
  4.9 10.1 %collective-permute-start.10 = (bf16[2,2,6,768]{3,2,1,0:T(8,128)(2,1)S(1)}, bf16[2,2,6,768]{3,2,1,0:T(8,128)(2,1)S(1)}, u32[]{:S(2)}, u32[]{:S(2)}) collective-permute-start(bf16[2,2,6,768]{3,2,1,0:T(8,128)(2,1)S(1)} %bitcast.48), channel_id=1, source_target_pairs={{0,2},{1,3},{2,0},{3,1},{4,6},{5,7},{6,4},{7,5},{8,10},{9,11},{10,... | collective-permute-start | bytes 110600 | tf_op jit(solution)/shard_map/ppermute | solution.py:268
  5.1 11.6 %collective-permute-start.11 = (bf16[2,2,6,768]{3,2,1,0:T(8,128)(2,1)S(1)}, bf16[2,2,6,768]{3,2,1,0:T(8,128)(2,1)S(1)}, u32[]{:S(2)}, u32[]{:S(2)}) collective-permute-start(bf16[2,2,6,768]{3,2,1,0:T(8,128)(2,1)S(1)} %bitcast.47), channel_id=1, source_target_pairs={{0,4},{1,5},{2,6},{3,7},{4,0},{5,1},{6,2},{7,3},{8,12},{9,13},{10,... | collective-permute-start | bytes 110600 | tf_op jit(solution)/shard_map/ppermute | solution.py:268
  8.1 10.4 %collective-permute-start.12 = (bf16[2,2,6,768]{3,2,1,0:T(8,128)(2,1)S(1)}, bf16[2,2,6,768]{3,2,1,0:T(8,128)(2,1)S(1)}, u32[]{:S(2)}, u32[]{:S(2)}) collective-permute-start(bf16[2,2,6,768]{3,2,1,0:T(8,128)(2,1)S(1)} %bitcast.46), channel_id=1, source_target_pairs={{0,6},{1,7},{2,4},{3,5},{4,2},{5,3},{6,0},{7,1},{8,14},{9,15},{10,... | collective-permute-start | bytes 110600 | tf_op jit(solution)/shard_map/ppermute | solution.py:268
  15.0 22.6 %collective-permute-start.5 = (bf16[6,192,128]{2,1,0:T(8,128)(2,1)}, bf16[6,192,128]{2,1,0:T(8,128)(2,1)S(1)}, u32[]{:S(2)}, u32[]{:S(2)}) collective-permute-start(bf16[6,192,128]{2,1,0:T(8,128)(2,1)} %same_ref.1), channel_id=1, source_target_pairs={{0,4},{1,5},{2,6},{3,7},{4,0},{5,1},{6,2},{7,3},{8,12},{9,13},{10,... | collective-permute-start | bytes 884744 | tf_op jit(solution)/shard_map/ppermute | solution.py:268
  16.7 20.9 %collective-permute-start = (bf16[6,192,128]{2,1,0:T(8,128)(2,1)}, bf16[6,192,128]{2,1,0:T(8,128)(2,1)S(1)}, u32[]{:S(2)}, u32[]{:S(2)}) collective-permute-start(bf16[6,192,128]{2,1,0:T(8,128)(2,1)} %same_ref.1), channel_id=1, source_target_pairs={{0,6},{1,7},{2,4},{3,5},{4,2},{5,3},{6,0},{7,1},{8,14},{9,15},{10,... | collective-permute-start | bytes 884744 | tf_op jit(solution)/shard_map/ppermute | solution.py:268
  18.7 1.4 %collective-permute-start.13 = (bf16[4,2,6,768]{3,2,1,0:T(8,128)(2,1)S(1)}, bf16[4,2,6,768]{3,2,1,0:T(8,128)(2,1)S(1)}, u32[]{:S(2)}, u32[]{:S(2)}) collective-permute-start(bf16[4,2,6,768]{3,2,1,0:T(8,128)(2,1)S(1)} %get-tuple-element.53), channel_id=1, source_target_pairs={{0,1},{1,0},{2,3},{3,2},{4,5},{5,4},{6,7},{7,6},{8,9},{9,8},{10,11... | collective-permute-start | bytes 221192 | tf_op jit(solution)/shard_map/ppermute | solution.py:268
  20.0 9.3 %collective-permute-start.2 = (bf16[6,192,128]{2,1,0:T(8,128)(2,1)}, bf16[6,192,128]{2,1,0:T(8,128)(2,1)S(1)}, u32[]{:S(2)}, u32[]{:S(2)}) collective-permute-start(bf16[6,192,128]{2,1,0:T(8,128)(2,1)} %right_rows.1.refs_0_), channel_id=1, source_target_pairs={{0,8},{1,9},{2,10},{3,11},{4,12},{5,13},{6,14},{7,15},{8,0},{9,1},... | collective-permute-start | bytes 884744 | tf_op jit(solution)/shard_map/ppermute | solution.py:268
  21.6 23.2 %copy-start.6 = (bf16[6,192,128]{2,1,0:T(8,128)(2,1)}, bf16[6,192,128]{2,1,0:T(8,128)(2,1)S(1)}, u32[]{:S(2)}) copy-start(bf16[6,192,128]{2,1,0:T(8,128)(2,1)S(1)} %collective-permute-done.9.other_ref) | copy-start | bytes 884740
  21.6 16.6 %collective-permute-start.3 = (bf16[6,192,128]{2,1,0:T(8,128)(2,1)}, bf16[6,192,128]{2,1,0:T(8,128)(2,1)S(1)}, u32[]{:S(2)}, u32[]{:S(2)}) collective-permute-start(bf16[6,192,128]{2,1,0:T(8,128)(2,1)} %right_rows.1.refs_0_), channel_id=1, source_target_pairs={{0,16},{1,17},{2,18},{3,19},{4,20},{5,21},{6,22},{7,23},{8,24},{9,... | collective-permute-start | bytes 884744 | tf_op jit(solution)/shard_map/ppermute | solution.py:268
  29.3 20.4 %copy-start.1 = (bf16[6,192,128]{2,1,0:T(8,128)(2,1)}, bf16[6,192,128]{2,1,0:T(8,128)(2,1)S(1)}, u32[]{:S(2)}) copy-start(bf16[6,192,128]{2,1,0:T(8,128)(2,1)S(1)} %collective-permute-done.2.refs_1_) | copy-start | bytes 884740
  29.3 10.5 %collective-permute-start.4 = (bf16[6,192,128]{2,1,0:T(8,128)(2,1)}, bf16[6,192,128]{2,1,0:T(8,128)(2,1)S(1)}, u32[]{:S(2)}, u32[]{:S(2)}) collective-permute-start(bf16[6,192,128]{2,1,0:T(8,128)(2,1)} %right_rows.1.refs_0_), channel_id=1, source_target_pairs={{0,24},{1,25},{2,26},{3,27},{4,28},{5,29},{6,30},{7,31},{8,16},{9,... | collective-permute-start | bytes 884744 | tf_op jit(solution)/shard_map/ppermute | solution.py:268
  31.7 24.3 %copy-start.5 = (bf16[6,192,128]{2,1,0:T(8,128)(2,1)}, bf16[6,192,128]{2,1,0:T(8,128)(2,1)S(1)}, u32[]{:S(2)}) copy-start(bf16[6,192,128]{2,1,0:T(8,128)(2,1)S(1)} %collective-permute-done.7.same_ref) | copy-start | bytes 884740
  31.8 24.3 %collective-permute-start.8 = (bf16[6,192,128]{2,1,0:T(8,128)(2,1)S(1)}, bf16[6,192,128]{2,1,0:T(8,128)(2,1)S(1)}, u32[]{:S(2)}, u32[]{:S(2)}) collective-permute-start(bf16[6,192,128]{2,1,0:T(8,128)(2,1)S(1)} %collective-permute-done.7.same_ref), channel_id=1, source_target_pairs={{0,1},{1,0},{2,3},{3,2},{4,5},{5,4},{6,7},{7,6},{8,9},{9,8},{10,11... | collective-permute-start | bytes 884744 | tf_op jit(solution)/shard_map/ppermute | solution.py:268
  37.6 24.1 %copy-start.7 = (bf16[6,192,128]{2,1,0:T(8,128)(2,1)}, bf16[6,192,128]{2,1,0:T(8,128)(2,1)S(1)}, u32[]{:S(2)}) copy-start(bf16[6,192,128]{2,1,0:T(8,128)(2,1)S(1)} %collective-permute-done.5.same_ref) | copy-start | bytes 884740
  37.6 24.1 %collective-permute-start.6 = (bf16[6,192,128]{2,1,0:T(8,128)(2,1)S(1)}, bf16[6,192,128]{2,1,0:T(8,128)(2,1)S(1)}, u32[]{:S(2)}, u32[]{:S(2)}) collective-permute-start(bf16[6,192,128]{2,1,0:T(8,128)(2,1)S(1)} %collective-permute-done.5.same_ref), channel_id=1, source_target_pairs={{0,1},{1,0},{2,3},{3,2},{4,5},{5,4},{6,7},{7,6},{8,9},{9,8},{10,11... | collective-permute-start | bytes 884744 | tf_op jit(solution)/shard_map/ppermute | solution.py:268
  37.6 29.7 %copy-start.8 = (bf16[6,192,128]{2,1,0:T(8,128)(2,1)}, bf16[6,192,128]{2,1,0:T(8,128)(2,1)S(1)}, u32[]{:S(2)}) copy-start(bf16[6,192,128]{2,1,0:T(8,128)(2,1)S(1)} %collective-permute-done.same_ref) | copy-start | bytes 884740
  37.6 29.6 %collective-permute-start.1 = (bf16[6,192,128]{2,1,0:T(8,128)(2,1)S(1)}, bf16[6,192,128]{2,1,0:T(8,128)(2,1)S(1)}, u32[]{:S(2)}, u32[]{:S(2)}) collective-permute-start(bf16[6,192,128]{2,1,0:T(8,128)(2,1)S(1)} %collective-permute-done.same_ref), channel_id=1, source_target_pairs={{0,1},{1,0},{2,3},{3,2},{4,5},{5,4},{6,7},{7,6},{8,9},{9,8},{10,11... | collective-permute-start | bytes 884744 | tf_op jit(solution)/shard_map/ppermute | solution.py:268
  38.2 69.6 %copy-start.4 = (bf16[4,2,2,6,768]{4,3,2,1,0:T(8,128)(2,1)}, bf16[4,2,2,6,768]{4,3,2,1,0:T(8,128)(2,1)S(1)}, u32[]{:S(2)}) copy-start(bf16[4,2,2,6,768]{4,3,2,1,0:T(8,128)(2,1)S(1)} %pad_maximum_fusion.1) | copy-start | bytes 442372
  38.2 11.4 %copy-start.2 = (bf16[6,192,128]{2,1,0:T(8,128)(2,1)}, bf16[6,192,128]{2,1,0:T(8,128)(2,1)S(1)}, u32[]{:S(2)}) copy-start(bf16[6,192,128]{2,1,0:T(8,128)(2,1)S(1)} %collective-permute-done.3.refs_2_) | copy-start | bytes 884740
  38.2 62.4 %collective-permute-start.14 = (bf16[8,2,6,768]{3,2,1,0:T(8,128)(2,1)S(1)}, bf16[8,2,6,768]{3,2,1,0:T(8,128)(2,1)S(1)}, u32[]{:S(2)}, u32[]{:S(2)}) collective-permute-start(bf16[8,2,6,768]{3,2,1,0:T(8,128)(2,1)S(1)} %bitcast.34), channel_id=1, source_target_pairs={{0,8},{1,9},{2,10},{3,11},{4,12},{5,13},{6,14},{7,15},{8,0},{9,1},... | collective-permute-start | bytes 442376 | tf_op jit(solution)/shard_map/ppermute | solution.py:268
  39.8 9.9 %copy-start.3 = (bf16[6,192,128]{2,1,0:T(8,128)(2,1)}, bf16[6,192,128]{2,1,0:T(8,128)(2,1)S(1)}, u32[]{:S(2)}) copy-start(bf16[6,192,128]{2,1,0:T(8,128)(2,1)S(1)} %collective-permute-done.4.refs_3_) | copy-start | bytes 884740
  39.8 61.4 %collective-permute-start.15 = (bf16[8,2,6,768]{3,2,1,0:T(8,128)(2,1)S(1)}, bf16[8,2,6,768]{3,2,1,0:T(8,128)(2,1)}, u32[]{:S(2)}, u32[]{:S(2)}) collective-permute-start(bf16[8,2,6,768]{3,2,1,0:T(8,128)(2,1)S(1)} %bitcast.35), channel_id=1, source_target_pairs={{0,16},{1,17},{2,18},{3,19},{4,20},{5,21},{6,22},{7,23},{8,24},{9,... | collective-permute-start | bytes 442376 | tf_op jit(solution)/shard_map/ppermute | solution.py:268
  56.1 0.7 copy-start.11
  61.7 0.7 copy-start.10
  67.2 0.7 copy-start.9
  92.2 9.1 %collective-permute-start.18 = (bf16[4,16,384]{2,1,0:T(8,128)(2,1)}, bf16[4,16,384]{2,1,0:T(8,128)(2,1)S(1)}, u32[]{:S(2)}, u32[]{:S(2)}) collective-permute-start(bf16[4,16,384]{2,1,0:T(8,128)(2,1)} %get-tuple-element.39.refs_0_), channel_id=1, source_target_pairs={{0,2},{1,3},{2,0},{3,1},{4,6},{5,7},{6,4},{7,5},{8,10},{9,11},{10,... | collective-permute-start | bytes 147464 | tf_op jit(solution)/shard_map/ppermute | solution.py:268
  98.0 6.7 %collective-permute-start.20 = (bf16[4,16,384]{2,1,0:T(8,128)(2,1)}, bf16[4,16,384]{2,1,0:T(8,128)(2,1)S(1)}, u32[]{:S(2)}, u32[]{:S(2)}) collective-permute-start(bf16[4,16,384]{2,1,0:T(8,128)(2,1)} %get-tuple-element.39.refs_0_), channel_id=1, source_target_pairs={{0,4},{1,5},{2,6},{3,7},{4,0},{5,1},{6,2},{7,3},{8,12},{9,13},{10,... | collective-permute-start | bytes 147464 | tf_op jit(solution)/shard_map/ppermute | solution.py:268
  99.1 6.2 %collective-permute-start.22 = (bf16[4,16,384]{2,1,0:T(8,128)(2,1)}, bf16[4,16,384]{2,1,0:T(8,128)(2,1)S(1)}, u32[]{:S(2)}, u32[]{:S(2)}) collective-permute-start(bf16[4,16,384]{2,1,0:T(8,128)(2,1)} %get-tuple-element.39.refs_0_), channel_id=1, source_target_pairs={{0,6},{1,7},{2,4},{3,5},{4,2},{5,3},{6,0},{7,1},{8,14},{9,15},{10,... | collective-permute-start | bytes 147464 | tf_op jit(solution)/shard_map/ppermute | solution.py:268
  100.7 7.2 %copy-start.12 = (bf16[8,2,6,768]{3,2,1,0:T(8,128)(2,1)}, bf16[8,2,6,768]{3,2,1,0:T(8,128)(2,1)S(1)}, u32[]{:S(2)}) copy-start(bf16[8,2,6,768]{3,2,1,0:T(8,128)(2,1)S(1)} %collective-permute-done.14.refs_1_) | copy-start | bytes 442372
  100.7 7.1 %collective-permute-start.16 = (bf16[8,2,6,768]{3,2,1,0:T(8,128)(2,1)S(1)}, bf16[8,2,6,768]{3,2,1,0:T(8,128)(2,1)S(1)}, u32[]{:S(2)}, u32[]{:S(2)}) collective-permute-start(bf16[8,2,6,768]{3,2,1,0:T(8,128)(2,1)S(1)} %bitcast.36), channel_id=1, source_target_pairs={{0,24},{1,25},{2,26},{3,27},{4,28},{5,29},{6,30},{7,31},{8,16},{9,... | collective-permute-start | bytes 442376 | tf_op jit(solution)/shard_map/ppermute | solution.py:268
  101.3 13.3 %collective-permute-start.17 = (bf16[4,16,384]{2,1,0:T(8,128)(2,1)}, bf16[4,16,384]{2,1,0:T(8,128)(2,1)S(1)}, u32[]{:S(2)}, u32[]{:S(2)}) collective-permute-start(bf16[4,16,384]{2,1,0:T(8,128)(2,1)} %get-tuple-element.39.refs_0_), channel_id=1, source_target_pairs={{0,1},{1,0},{2,3},{3,2},{4,5},{5,4},{6,7},{7,6},{8,9},{9,8},{10,11... | collective-permute-start | bytes 147464 | tf_op jit(solution)/shard_map/ppermute | solution.py:268
  101.3 13.4 %copy-start.14 = (bf16[4,16,384]{2,1,0:T(8,128)(2,1)}, bf16[4,16,384]{2,1,0:T(8,128)(2,1)S(1)}, u32[]{:S(2)}) copy-start(bf16[4,16,384]{2,1,0:T(8,128)(2,1)S(1)} %collective-permute-done.18.refs_2_) | copy-start | bytes 147460
  101.3 13.3 %collective-permute-start.19 = (bf16[4,16,384]{2,1,0:T(8,128)(2,1)S(1)}, bf16[4,16,384]{2,1,0:T(8,128)(2,1)S(1)}, u32[]{:S(2)}, u32[]{:S(2)}) collective-permute-start(bf16[4,16,384]{2,1,0:T(8,128)(2,1)S(1)} %collective-permute-done.18.refs_2_), channel_id=1, source_target_pairs={{0,1},{1,0},{2,3},{3,2},{4,5},{5,4},{6,7},{7,6},{8,9},{9,8},{10,11... | collective-permute-start | bytes 147464 | tf_op jit(solution)/shard_map/ppermute | solution.py:268
  104.6 10.0 %copy-start.15 = (bf16[4,16,384]{2,1,0:T(8,128)(2,1)}, bf16[4,16,384]{2,1,0:T(8,128)(2,1)S(1)}, u32[]{:S(2)}) copy-start(bf16[4,16,384]{2,1,0:T(8,128)(2,1)S(1)} %collective-permute-done.20.refs_4_) | copy-start | bytes 147460
  104.6 10.0 %collective-permute-start.21 = (bf16[4,16,384]{2,1,0:T(8,128)(2,1)S(1)}, bf16[4,16,384]{2,1,0:T(8,128)(2,1)S(1)}, u32[]{:S(2)}, u32[]{:S(2)}) collective-permute-start(bf16[4,16,384]{2,1,0:T(8,128)(2,1)S(1)} %collective-permute-done.20.refs_4_), channel_id=1, source_target_pairs={{0,1},{1,0},{2,3},{3,2},{4,5},{5,4},{6,7},{7,6},{8,9},{9,8},{10,11... | collective-permute-start | bytes 147464 | tf_op jit(solution)/shard_map/ppermute | solution.py:268
  105.3 9.4 %copy-start.16 = (bf16[4,16,384]{2,1,0:T(8,128)(2,1)}, bf16[4,16,384]{2,1,0:T(8,128)(2,1)S(1)}, u32[]{:S(2)}) copy-start(bf16[4,16,384]{2,1,0:T(8,128)(2,1)S(1)} %collective-permute-done.22.refs_6_) | copy-start | bytes 147460
  105.3 9.3 %collective-permute-start.23 = (bf16[4,16,384]{2,1,0:T(8,128)(2,1)S(1)}, bf16[4,16,384]{2,1,0:T(8,128)(2,1)S(1)}, u32[]{:S(2)}, u32[]{:S(2)}) collective-permute-start(bf16[4,16,384]{2,1,0:T(8,128)(2,1)S(1)} %collective-permute-done.22.refs_6_), channel_id=1, source_target_pairs={{0,1},{1,0},{2,3},{3,2},{4,5},{5,4},{6,7},{7,6},{8,9},{9,8},{10,11... | collective-permute-start | bytes 147464 | tf_op jit(solution)/shard_map/ppermute | solution.py:268
  106.0 21.9 %copy-start = (bf16[48,4,1,6,128]{4,3,2,1,0:T(8,128)(2,1)S(1)}, bf16[48,4,1,6,128]{4,3,2,1,0:T(8,128)(2,1)}, u32[]{:S(2)}) copy-start(bf16[48,4,1,6,128]{4,3,2,1,0:T(8,128)(2,1)} %get-tuple-element.48) | copy-start | bytes 884740
  107.9 0.7 copy-start.13
  114.6 0.6 copy-start.17
  114.6 0.6 copy-start.18
  114.6 0.6 copy-start.19
  114.6 0.6 copy-start.20
  124.2 10.7 %all-to-all-start = ((bf16[8,2,6,768]{3,1,2,0:T(2,128)(2,1)}), bf16[8,2,6,768]{3,1,2,0:T(2,128)(2,1)S(1)}, u32[]{:S(2)}, u32[]{:S(2)}) async-start(bf16[8,2,6,768]{3,1,2,0:T(2,128)(2,1)} %copy.54), calls=%async_computation | async-start | bytes 294912 | tf_op jit(solution)/shard_map/all_to_all | solution.py:436

commit v2 on v1

v2 whole, which is shorter than its diff:
```python
import functools
import math

import jax
import jax.numpy as jnp
from jax import lax
from jax.experimental import pallas as pl
from jax.experimental.pallas import tpu as pltpu
from jax.sharding import PartitionSpec as P

epsilon = 1e-05
AXES = ("row", "col")
SUB = 8
LANES = 128
FLAT_ROWS = 1152
EXCLUDED = -1e30
SCALARS = pl.BlockSpec(memory_space=pltpu.SMEM)
BLOCK = pl.BlockSpec(memory_space=pltpu.VMEM)


def layer_norm(values, gain):
    mean = jnp.mean(values, axis=-1, keepdims=True)
    centered = values - mean
    variance = jnp.mean(centered * centered, axis=-1, keepdims=True)
    scaled = centered * lax.rsqrt(variance + epsilon)
    return scaled if gain is None else scaled * gain


def sigmoid(values):
    return 0.5 * jnp.tanh(0.5 * values) + 0.5


def gated(normed, weight):
    width = weight.shape[1] // 2
    hidden = jnp.dot(normed, weight, preferred_element_type=jnp.float32)
    return sigmoid(hidden[:, :width]) * hidden[:, width:]


def edge_rows(values, gain, weight):
    count, tokens, channels = values.shape
    flat = layer_norm(values.reshape(count * tokens, channels), gain).astype(jnp.bfloat16)
    return gated(flat, weight).reshape(count, tokens, channels)


def in_groups(rows, tokens, step):
    group = max(1, min(rows, FLAT_ROWS // tokens))
    while rows % group:
        group -= 1
    if group == rows:
        step(0, rows)
    else:
        lax.fori_loop(0, rows // group, lambda g, carry: (step(g * group, group), carry)[1], 0)


def right_kernel(place_ref, mask_ref, valid_ref, gain_ref, weight_ref, *refs):
    pair_refs, right_ref = refs[:-1], refs[-1]
    rows, tokens, channels = pair_refs[0].shape
    gain = gain_ref[...]
    weight = weight_ref[...]
    row_index, col_index, col_count = place_ref[0], place_ref[1], place_ref[2]
    valid = jnp.broadcast_to((valid_ref[...] == 1).astype(jnp.float32), (channels, tokens)).T
    for block, pair_ref in enumerate(pair_refs):
        first = ((row_index ^ block) * col_count + col_index) * rows

        def step(start, count):
            edges = edge_rows(pair_ref[pl.ds(start, count)].astype(jnp.float32), gain, weight)
            for i in range(count):
                own = (mask_ref[first + start + i] == 1).astype(jnp.float32)
                right_ref[block * rows + start + i] = (
                    (edges[i] * (valid * own)).astype(jnp.bfloat16).astype(jnp.float32)
                )

        in_groups(rows, tokens, step)


def pair_kernel(block_count, step_at, earlier, place_ref, mask_ref, *refs):
    same_ref, other_ref, right_ref = refs[:3]
    gain_ref, mix_ref, left_ref, gate_ref, out_ref, bias_ref = refs[3:9]
    given = refs[9 : 9 + 2 * len(earlier)]
    new_ref, head_ref, left_f, floats, tile_f, mixed_f = refs[9 + 2 * len(earlier) :]
    rows, tokens, channels = same_ref.shape
    pair_rows = 2 * rows
    gain = gain_ref[...]
    weight = left_ref[...]
    row_index, col_index, col_count = place_ref[0], place_ref[1], place_ref[2]
    floats[:, tokens:] = jnp.zeros((rows, SUB, channels), jnp.float32)
    for chunk, pair_ref in enumerate((same_ref, other_ref)):
        chunk_col = col_index ^ (2 * step_at + chunk)
        base = (chunk_col % 2) * rows
        first = (row_index * col_count + chunk_col) * rows

        def step(start, count):
            values = pair_ref[pl.ds(start, count)].astype(jnp.float32)
            floats[pl.ds(start, count), :tokens] = values
            edges = edge_rows(values, gain, weight)
            for i in range(count):
                own = (mask_ref[first + start + i] == 1).astype(jnp.float32)
                left_f[base + start + i] = (
                    (edges[i] * own).astype(jnp.bfloat16).astype(jnp.float32)
                )

        in_groups(rows, tokens, step)
        for i in range(rows):
            for block in range(block_count):
                start = ((row_index ^ block) * col_count + col_index) * rows
                tile_f[base + i, block] = floats[i, pl.ds(start, SUB), :]
    mixed_f[:, :, rows:, :] = jnp.zeros((pair_rows, block_count, SUB - rows, channels), jnp.float32)

    def product(n, carry):
        block, half = n // 2, n % 2

        def slab(k, sums):
            at = pl.ds(pl.multiple_of(k * SUB, SUB), SUB)
            lefts = [left_f[half * rows + i, at, :] for i in range(rows)]
            rights = [right_ref[block * rows + t, at, :] for t in range(rows)]
            return tuple(
                sums[i * rows + t] + lefts[i] * rights[t] for i in range(rows) for t in range(rows)
            )

        zero = jnp.zeros((SUB, channels), jnp.float32)
        sums = lax.fori_loop(0, tokens // SUB, slab, (zero,) * (rows * rows), unroll=24)
        for i in range(rows):
            for t in range(rows):
                mixed_f[half * rows + i, block, t : t + 1, :] = jnp.sum(
                    sums[i * rows + t], axis=0, keepdims=True
                )
        return carry

    lax.fori_loop(0, 2 * block_count, product, 0)
    flat = pair_rows * block_count * SUB
    mixed_norm = layer_norm(mixed_f[...].reshape(flat, channels), mix_ref[...]).astype(jnp.bfloat16)
    pair = tile_f[...].reshape(flat, channels)
    normed = layer_norm(pair, gain).astype(jnp.bfloat16)
    gate = sigmoid(jnp.dot(normed, gate_ref[...], preferred_element_type=jnp.float32))
    update = jnp.dot(mixed_norm, out_ref[...], preferred_element_type=jnp.float32)
    pair_new = (pair + gate * update).astype(jnp.bfloat16).astype(jnp.float32)
    split = pair_new.reshape(pair_rows, block_count, SUB, channels)
    bias_input = layer_norm(pair_new, None).astype(jnp.bfloat16)
    bias = lax.dot_general(
        bias_ref[...], bias_input, (((0,), (1,)), ((), ())), preferred_element_type=jnp.float32
    )
    joins = new_ref.shape[0] > pair_rows
    chip = col_index // 2
    place = chip ^ step_at if joins else 0
    for block in range(block_count):
        new_ref[pl.ds(place * pair_rows, pair_rows), row_index ^ block, 0] = split[
            :, block, :rows, :
        ].astype(jnp.bfloat16)
    head_ref[place] = bias.astype(jnp.bfloat16)
    for n, k in enumerate(earlier):
        new_ref[pl.ds((chip ^ k) * pair_rows, pair_rows)] = given[2 * n][...]
        head_ref[chip ^ k] = given[2 * n + 1][0]


def project_kernel(block_count, place_ref, chain_ref, valid_ref, weight_ref, *refs):
    single_refs = refs[:block_count]
    query_ref, key_ref, value_ref, allowed_ref, rows_f, own_f = refs[block_count:]
    col_count, rows, samples, width = single_refs[0].shape
    query_rows, key_count = allowed_ref.shape
    tokens = chain_ref.shape[1]
    row_index, col_index = place_ref[0], place_ref[1]
    rows_f[...] = jnp.zeros_like(rows_f)
    own_f[...] = jnp.zeros_like(own_f)
    for col in range(col_count):
        for block in range(block_count):
            at = col * block_count + block
            for t in range(rows):
                values = single_refs[block][col_index ^ col, t].astype(jnp.float32)
                for s in range(samples):
                    rows_f[s, at, t : t + 1, :] = values[s : s + 1]
        for t in range(rows):
            values = single_refs[0][col, t].astype(jnp.float32)
            for s in range(samples):
                own_f[s, col, t : t + 1, :] = values[s : s + 1]
    for s in range(samples):
        own = own_f[s].reshape(-1, width).astype(jnp.bfloat16)
        query_ref[s] = jnp.dot(
            own, weight_ref[:, :width], preferred_element_type=jnp.float32
        ).astype(jnp.bfloat16)
        full = rows_f[s].reshape(-1, width).astype(jnp.bfloat16)
        for target, at in ((key_ref, width), (value_ref, 2 * width)):
            product = jnp.dot(
                full, weight_ref[:, at : at + width], preferred_element_type=jnp.float32
            )
            target[s] = product.T.astype(jnp.bfloat16)

    def key_tokens(shape, axis):
        place = lax.broadcasted_iota(jnp.int32, shape, axis)
        t = place % SUB
        block = (place // SUB) % block_count
        col = place // (SUB * block_count)
        token = ((row_index ^ block) * col_count + (col_index ^ col)) * rows + t
        return jnp.where(t < rows, token, -1)

    def query_tokens(shape):
        place = lax.broadcasted_iota(jnp.int32, shape, 0)
        t = place % SUB
        token = (row_index * col_count + place // SUB) * rows + t
        return jnp.where(t < rows, token, -2)

    chains = chain_ref[...].astype(jnp.float32)
    valid = (valid_ref[...] == 1).astype(jnp.float32)
    token = lax.broadcasted_iota(jnp.int32, (query_rows, tokens), 1)
    hit = query_tokens((query_rows, tokens)) == token
    query_chain = jnp.sum(jnp.where(hit, chains, 0.0), axis=1, keepdims=True)
    token = lax.broadcasted_iota(jnp.int32, (key_count, tokens), 1)
    hit = jnp.where(key_tokens((key_count, tokens), 0) == token, 1.0, 0.0).astype(jnp.bfloat16)

    def of_keys(table):
        table = jnp.broadcast_to(table, (SUB, tokens)).astype(jnp.bfloat16)
        return lax.dot_general(
            table, hit, (((1,), (1,)), ((), ())), preferred_element_type=jnp.float32
        )[:1]

    keys = key_tokens((query_rows, key_count), 1)
    near = (of_keys(valid) > 0.5) & (of_keys(chains) == query_chain) & (keys >= 0)
    allowed = near | (keys == query_tokens((query_rows, key_count)))
    allowed_ref[...] = jnp.where(allowed, 0.0, EXCLUDED)


def attend_kernel(col_count, token_rows, head_count, query_ref, key_ref, value_ref, *refs):
    bias_refs = refs[:col_count]
    allowed_ref, merge_ref, result_ref, bias_f, joined = refs[col_count:]
    samples, query_rows, width = query_ref.shape
    key_count = key_ref.shape[2]
    head_width = width // head_count
    scale = 1.0 / math.sqrt(head_width)
    part = key_count // col_count
    group = LANES // part
    pairs = bias_refs[0].shape[0]
    lane_tiles = bias_refs[0].shape[2] // LANES
    lane = lax.broadcasted_iota(jnp.int32, (head_count, LANES), 1) // part
    for col in range(col_count):
        for t in range(token_rows, SUB):
            bias_f[col * SUB + t] = jnp.zeros((head_count, key_count), jnp.float32)
    for pair in range(pairs):
        for tile in range(lane_tiles):
            pieces = [
                ref[pair, :, tile * LANES : (tile + 1) * LANES].astype(jnp.float32)
                for ref in bias_refs
            ]
            for m in range(group):
                inside = tile * group + m
                col = 2 * pair + inside // token_rows
                row = col * SUB + inside % token_rows
                for target in range(col_count // group):
                    total = None
                    for u in range(group):
                        piece = pieces[target * group + u]
                        shift = ((u - m) * part) % LANES
                        if shift:
                            piece = pltpu.roll(piece, shift, 1)
                        total = piece if total is None else jnp.where(lane == u, piece, total)
                    bias_f[row, :, target * LANES : (target + 1) * LANES] = total
    allowed = allowed_ref[...]
    parts = [[] for _ in range(samples)]
    for h in range(head_count):
        at = slice(h * head_width, (h + 1) * head_width)
        bias = bias_f[:, h, :] + allowed
        for s in range(samples):
            scores = jnp.dot(
                query_ref[s, :, at], key_ref[s, at, :], preferred_element_type=jnp.float32
            )
            scores = scores * scale + bias
            weights = jnp.exp(scores - jnp.max(scores, axis=-1, keepdims=True))
            weights = weights.astype(jnp.bfloat16)
            total = jnp.sum(weights.astype(jnp.float32), axis=-1, keepdims=True)
            summed = lax.dot_general(
                weights, value_ref[s, at, :], (((1,), (1,)), ((), ())),
                preferred_element_type=jnp.float32,
            )
            parts[s].append(summed / total)
    lane_parts = range(width // LANES)
    for s in range(samples):
        attended = jnp.concatenate(parts[s], axis=1)
        for n in lane_parts:
            joined[n, pl.ds(s, query_rows, stride=samples), :] = attended[
                :, n * LANES : (n + 1) * LANES
            ]
    attended = jnp.concatenate([joined[n] for n in lane_parts], axis=1).astype(jnp.bfloat16)
    merged = jnp.dot(attended, merge_ref[...], preferred_element_type=jnp.float32)
    split = merged.reshape(col_count, SUB * samples, width)
    result_ref[...] = split[:, : token_rows * samples, :].astype(jnp.bfloat16)


def call(kernel, name, operands, scalars, outs, scratch, time_us):
    def size(shape, kind):
        return math.prod(shape) * jnp.dtype(kind).itemsize

    held = sum(size(x.shape, x.dtype) for x in operands) + sum(size(*x) for x in outs)
    work = sum(size(*x) for x in scratch)
    limit = min(60 << 20, int(1.25 * (held + work)) + (6 << 20))
    return pl.pallas_call(
        kernel,
        in_specs=[SCALARS] * scalars + [BLOCK] * (len(operands) - scalars),
        out_specs=[BLOCK] * len(outs),
        out_shape=[jax.ShapeDtypeStruct(*x) for x in outs],
        scratch_shapes=[pltpu.VMEM(*x) for x in scratch],
        cost_estimate=pl.CostEstimate(
            flops=0, bytes_accessed=int(time_us * 3.6e6), transcendentals=0
        ),
        compiler_params=pltpu.CompilerParams(vmem_limit_bytes=limit),
        name=name,
    )(*operands)


def shards(
    pair_state,
    single_rep,
    token_mask,
    chain_ids,
    pair_gain,
    mix_gain,
    left_weight,
    right_weight,
    gate_weight,
    out_weight,
    bias_weight,
    token_weight,
    merge_weight,
):
    row_count = lax.axis_size("row")
    col_count = lax.axis_size("col")
    row_index = lax.axis_index("row")
    col_index = lax.axis_index("col")
    rows, tokens, channels = pair_state.shape
    samples, _, width = single_rep.shape
    heads = bias_weight.shape[1]
    chips = col_count // 2
    own_samples = samples // col_count
    keys = tokens // rows * SUB
    query_rows = col_count * SUB
    part = row_count * SUB
    bf16, f32 = jnp.bfloat16, jnp.float32

    def send(values, by_row, by_col):
        steps = [
            (r * col_count + c, (r ^ by_row) * col_count + (c ^ by_col))
            for r in range(row_count)
            for c in range(col_count)
        ]
        return lax.ppermute(values, AXES, steps)

    place = jnp.stack([row_index, col_index, jnp.int32(col_count)]).astype(jnp.int32)
    gain = pair_gain.reshape(1, channels)
    mix = mix_gain.reshape(1, channels)
    valid_row = token_mask.reshape(1, tokens)
    chain_row = chain_ids.reshape(1, tokens)

    same = [pair_state] + [send(pair_state, 0, 2 * k) for k in range(1, chips)]
    other = [send(values, 0, 1) for values in same]
    columns = [pair_state] + [send(pair_state, k, 0) for k in range(1, row_count)]

    by_token = jnp.transpose(single_rep, (1, 0, 2)).reshape(rows, col_count, own_samples, width)
    own_single = lax.all_to_all(jnp.transpose(by_token, (1, 0, 2, 3)), "col", 0, 0, tiled=True)
    singles = [own_single] + [send(own_single, k, 0) for k in range(1, row_count)]

    (rights,) = call(
        right_kernel, "right_rows",
        [place, token_mask, valid_row, gain, right_weight, *columns], 2,
        [((row_count * rows, tokens, channels), f32)], [], 3.0,
    )
    done = []
    for k in range(chips):
        last = k == chips - 1
        count = chips if last else 1
        earlier = tuple(range(k)) if last else ()
        pair_new, pair_heads = call(
            functools.partial(pair_kernel, row_count, k, earlier), f"pair_rows_{k}",
            [
                place, token_mask, same[k], other[k], rights, gain, mix, left_weight,
                gate_weight, out_weight, bias_weight, *(x for n in earlier for x in done[n]),
            ], 2,
            [
                ((count * 2 * rows, row_count, 1, rows, channels), bf16),
                ((count, heads, 2 * rows * part), bf16),
            ],
            [
                ((2 * rows, tokens, channels), f32),
                ((rows, tokens + SUB, channels), f32),
                ((2 * rows, row_count, SUB, channels), f32),
                ((2 * rows, row_count, SUB, channels), f32),
            ], 4.0,
        )
        done.append((pair_new, pair_heads))

    queries, key_cols, value_cols, allowed = call(
        functools.partial(project_kernel, row_count), "project_tokens",
        [place, chain_row, valid_row, token_weight, *singles], 1,
        [
            ((own_samples, query_rows, width), bf16),
            ((own_samples, width, keys), bf16),
            ((own_samples, width, keys), bf16),
            ((query_rows, keys), f32),
        ],
        [
            ((own_samples, keys // SUB, SUB, width), f32),
            ((own_samples, col_count, SUB, width), f32),
        ], 5.0,
    )

    near = [pair_heads] + [send(pair_heads, 0, 2 * k) for k in range(1, chips)]
    biases = []
    for values in near:
        biases += [values, send(values, 0, 1)]

    (merged,) = call(
        functools.partial(attend_kernel, col_count, rows, heads), "attend",
        [queries, key_cols, value_cols, *biases, allowed, merge_weight], 0,
        [((col_count, rows * own_samples, width), bf16)],
        [((query_rows, heads, keys), f32), ((width // LANES, own_samples * query_rows, LANES), f32)], 6.0,
    )
    arrived = lax.all_to_all(merged, "col", 0, 0, tiled=True)
    arrived = arrived.reshape(col_count, rows, own_samples, width)
    attention_out = jnp.transpose(arrived, (0, 2, 1, 3)).reshape(samples, rows, width)
    return pair_new, attention_out


def solution(mesh):
    in_specs = (
        P(("row", "col"), None, None),
        P(None, ("row", "col"), None),
    ) + (P(),) * 11
    out_specs = (P("row", None, "col", None, None), P(None, ("row", "col"), None))
    return jax.shard_map(shards, mesh=mesh, in_specs=in_specs, out_specs=out_specs, check_vma=False)
```

time: 136 us -> 99.3 us (0.73)
  Pallas kernels: 62.2 us -> 31.5 us
  waiting for transfers between devices: 24 us -> 30.2 us
  starting transfers between devices: 33.5 us -> 28.7 us
  local copies, waits for them, and re-layouts: 11.6 us -> 7.43 us
  other arithmetic: 3.41 us -> 0.08 us
    pallas_call x11 -> x7, Pallas kernels: 62.2 us -> 31.5 us  [call(): pl.pallas_call(kernel, in_specs=[SCALARS] * scalars + [BLOCK] * (len(oper...]
    ppermute x24 -> x20, starting transfers between devices: 29.9 us -> 20.6 us  [send(): return lax.ppermute(values, AXES, steps)]
    all_to_all x1 -> x2, waiting for transfers between devices: 6.17 us -> 14.2 us  [the longest x1 7.43 us: shards(): arrived = lax.all_to_all(merged, 'col', 0, 0, tiled=True)]
    all_to_all x1 -> x2, starting transfers between devices: 3.65 us -> 8.08 us  [the longest x1 4.69 us: shards(): lax.all_to_all(jnp.transpose(by_token, (1, 0, 2, 3)), 'col', 0, 0, tiled=...]
    another operation x4 -> x0, local copies, waits for them, and re-layouts: 2.61 us -> none  [meta_of(): jnp.stack([row_index, col_index, col_index ^ 2 * k, jnp.int32(col_count),...]
    ppermute x24 -> x20, waiting for transfers between devices: 17.9 us -> 16 us  [send(): return lax.ppermute(values, AXES, steps)]
    pallas_call x1 -> x0, local copies, waits for them, and re-layouts: 1.7 us -> none  [shards(): pl.pallas_call(functools.partial(attend_kernel, col_count, rows, heads),...]
    reduce_sum x2 -> x0, other arithmetic: 1.66 us -> none  [pick(): jnp.sum(jnp.where(ids[:, None] == token_ids[None, :], table[None, :], 0),...]
  transfers between devices with their start and end apart: 25 -> 22, of which waited for: 7 -> 7; matrix products, arithmetic and copies ran while one was open for 7% -> 3% of each run, Pallas kernels for 40% -> 26%
where the time goes in v2:
time: 99.3 us; the launch traced here: 98.7 us
  Pallas kernels  31.5 us (32%)
  waiting for transfers between devices  30.2 us (30%)
  starting transfers between devices  28.7 us (29%)
  local copies, waits for them, and re-layouts  7.43 us (7%)
    pallas_call x7, Pallas kernels, call(): pl.pallas_call(kernel, in_specs=[SCALARS] * scalars + [BLOCK] * (len(oper...  31.5 us
    ppermute x20, starting transfers between devices, send(): return lax.ppermute(values, AXES, steps)  20.6 us
    ppermute x20, waiting for transfers between devices, send(): return lax.ppermute(values, AXES, steps)  16 us
    all_to_all x1, waiting for transfers between devices, shards(): arrived = lax.all_to_all(merged, 'col', 0, 0, tiled=True)  7.43 us
    all_to_all x1, waiting for transfers between devices, shards(): lax.all_to_all(jnp.transpose(by_token, (1, 0, 2, 3)), 'col', 0, 0, tiled=...  6.79 us
    unnamed x30, local copies, waits for them, and re-layouts  4.82 us
    all_to_all x1, starting transfers between devices, shards(): lax.all_to_all(jnp.transpose(by_token, (1, 0, 2, 3)), 'col', 0, 0, tiled=...  4.69 us
    all_to_all x1, starting transfers between devices, shards(): arrived = lax.all_to_all(merged, 'col', 0, 0, tiled=True)  3.39 us
  transfers between devices with their start and end apart: 22, of which 7 were waited for; matrix products, arithmetic and copies ran while one was open for 3% of the time, Pallas kernels for 26%

profile of v2, /device:TPU:0, one launch (start us, length us, event | category | flops | bytes accessed | tf_op | source)
XLA Modules:
  0.0 98.7 jit_solution(15694239994044239349)
XLA Ops:
  0.6 0.0 copy-start.3
  0.6 0.0 copy-start.11
  0.7 0.0 copy-start.9
  0.7 3.0 %collective-permute-start.2 = (bf16[6,192,128]{2,1,0:T(8,128)(2,1)}, bf16[6,192,128]{2,1,0:T(8,128)(2,1)S(1)}, u32[]{:S(2)}, u32[]{:S(2)}) collective-permute-start(bf16[6,192,128]{2,1,0:T(8,128)(2,1)} %refs_0_.3), channel_id=1, source_target_pairs={{0,8},{1,9},{2,10},{3,11},{4,12},{5,13},{6,14},{7,15},{8,0},{9,1},... | collective-permute-start | bytes 884744 | tf_op jit(solution)/shard_map/ppermute | solution.py:342
  3.7 1.5 %collective-permute-start.3 = (bf16[6,192,128]{2,1,0:T(8,128)(2,1)}, bf16[6,192,128]{2,1,0:T(8,128)(2,1)S(1)}, u32[]{:S(2)}, u32[]{:S(2)}) collective-permute-start(bf16[6,192,128]{2,1,0:T(8,128)(2,1)} %refs_0_.3), channel_id=1, source_target_pairs={{0,16},{1,17},{2,18},{3,19},{4,20},{5,21},{6,22},{7,23},{8,24},{9,... | collective-permute-start | bytes 884744 | tf_op jit(solution)/shard_map/ppermute | solution.py:342
  5.2 1.6 %collective-permute-start.6 = (bf16[6,192,128]{2,1,0:T(8,128)(2,1)}, bf16[6,192,128]{2,1,0:T(8,128)(2,1)S(1)}, u32[]{:S(2)}, u32[]{:S(2)}) collective-permute-start(bf16[6,192,128]{2,1,0:T(8,128)(2,1)} %refs_0_.3), channel_id=1, source_target_pairs={{0,2},{1,3},{2,0},{3,1},{4,6},{5,7},{6,4},{7,5},{8,10},{9,11},{10,... | collective-permute-start | bytes 884744 | tf_op jit(solution)/shard_map/ppermute | solution.py:342
  6.8 2.6 %collective-permute-start.8 = (bf16[6,192,128]{2,1,0:T(8,128)(2,1)}, bf16[6,192,128]{2,1,0:T(8,128)(2,1)S(1)}, u32[]{:S(2)}, u32[]{:S(2)}) collective-permute-start(bf16[6,192,128]{2,1,0:T(8,128)(2,1)} %refs_0_.3), channel_id=1, source_target_pairs={{0,4},{1,5},{2,6},{3,7},{4,0},{5,1},{6,2},{7,3},{8,12},{9,13},{10,... | collective-permute-start | bytes 884744 | tf_op jit(solution)/shard_map/ppermute | solution.py:342
  9.4 0.2 collective-permute-start
  9.6 1.3 %collective-permute-done.2.refs_1_ = bf16[6,192,128]{2,1,0:T(8,128)(2,1)S(1)} collective-permute-done((bf16[6,192,128]{2,1,0:T(8,128)(2,1)}, bf16[6,192,128]{2,1,0:T(8,128)(2,1)S(1)}, u32[]{:S(2)}, u32[]{:S(2)}) %collective-permute-start.2) | collective-permute-done | bytes 294944 | tf_op jit(solution)/shard_map/ppermute | solution.py:342
  10.9 2.7 %collective-permute-start.4 = (bf16[6,192,128]{2,1,0:T(8,128)(2,1)}, bf16[6,192,128]{2,1,0:T(8,128)(2,1)}, u32[]{:S(2)}, u32[]{:S(2)}) collective-permute-start(bf16[6,192,128]{2,1,0:T(8,128)(2,1)} %refs_0_.3), channel_id=1, source_target_pairs={{0,24},{1,25},{2,26},{3,27},{4,28},{5,29},{6,30},{7,31},{8,16},{9,... | collective-permute-start | bytes 884744 | tf_op jit(solution)/shard_map/ppermute | solution.py:342
  13.6 0.0 collective-permute-done.3.refs_2_
  13.6 0.0 collective-permute-start.5
  13.6 5.3 %collective-permute-done.6.refs_0_ = bf16[6,192,128]{2,1,0:T(8,128)(2,1)S(1)} collective-permute-done((bf16[6,192,128]{2,1,0:T(8,128)(2,1)}, bf16[6,192,128]{2,1,0:T(8,128)(2,1)S(1)}, u32[]{:S(2)}, u32[]{:S(2)}) %collective-permute-start.6) | collective-permute-done | bytes 294944 | tf_op jit(solution)/shard_map/ppermute | solution.py:342
  18.9 0.0 collective-permute-start.7
  18.9 1.0 reshape.29
  19.9 0.8 copy.37
  20.6 4.7 %all-to-all-start = ((bf16[8,6,2,768]{3,2,1,0:T(2,128)(2,1)}), bf16[8,6,2,768]{3,2,1,0:T(2,128)(2,1)S(1)}, u32[]{:S(2)}, u32[]{:S(2)}) async-start(bf16[8,6,2,768]{3,2,1,0:T(2,128)(2,1)} %bitcast.14), calls=%async_computation | async-start | bytes 294912 | tf_op jit(solution)/shard_map/all_to_all | solution.py:355
  25.3 5.4 %collective-permute-done.8.refs_0_ = bf16[6,192,128]{2,1,0:T(8,128)(2,1)S(1)} collective-permute-done((bf16[6,192,128]{2,1,0:T(8,128)(2,1)}, bf16[6,192,128]{2,1,0:T(8,128)(2,1)S(1)}, u32[]{:S(2)}, u32[]{:S(2)}) %collective-permute-start.8) | collective-permute-done | bytes 294944 | tf_op jit(solution)/shard_map/ppermute | solution.py:342
  30.7 0.0 collective-permute-start.9
  30.7 0.0 collective-permute-done.refs_0_
  30.7 0.5 collective-permute-start.1
  31.2 6.8 %all-to-all-done.refs_0_ = bf16[8,6,2,768]{3,2,1,0:T(2,128)(2,1)S(1)} async-done(((bf16[8,6,2,768]{3,2,1,0:T(2,128)(2,1)}), bf16[8,6,2,768]{3,2,1,0:T(2,128)(2,1)S(1)}, u32[]{:S(2)}, u32[]{:S(2)}) %all-to-all-start) | async-done | bytes 147488 | tf_op jit(solution)/shard_map/all_to_all | solution.py:355
  38.0 0.0 collective-permute-done.4.refs_3_
  38.0 0.5 collective-permute-start.10
  38.5 0.0 collective-permute-done.5.refs_1_
  38.6 0.5 collective-permute-start.11
  39.1 0.0 collective-permute-done.7.refs_1_
  39.1 2.5 %collective-permute-start.12 = (bf16[8,6,2,768]{3,2,1,0:T(2,128)(2,1)S(1)}, bf16[8,6,2,768]{3,2,1,0:T(2,128)(2,1)}, u32[]{:S(2)}, u32[]{:S(2)}) collective-permute-start(bf16[8,6,2,768]{3,2,1,0:T(2,128)(2,1)S(1)} %all-to-all-done.refs_0_), channel_id=1, source_target_pairs={{0,24},{1,25},{2,26},{3,27},{4,28},{5,29},{6,30},{7,31},{8,16},{9,... | collective-permute-start | bytes 442376 | tf_op jit(solution)/shard_map/ppermute | solution.py:342
  41.5 0.1 pad_add_fusion.place_ref
  41.6 0.8 copy.31.refs_8_
  42.4 1.0 copy-done.2
  43.4 0.8 copy-done.7
  44.2 0.7 copy-done.8
  44.9 0.7 copy-done.10
  45.5 2.7 %right_rows.1.refs_2_ = f32[24,192,128]{2,1,0:T(8,128)S(1)} custom-call(s32[3]{0:T(128)S(1)} %pad_add_fusion.place_ref, s32[192]{0:T(256)S(1)} %copy-done.8, s32[1,192]{1,0:T(1,128)S(1)} %bitcast.15, f32[1,128]{1,0:T(1,128)S(1)} %bitcast.17, bf16[128,256]{1,0:T(8,128)(2,1)S(1)} %copy-done.7, bf16[6,192,128]{2,1,0:T(8,128)(2,1)S(1)} %copy-done.2, ...), custom_call_target="tpu_custom_call" | custom-call | bytes 10800000 | tf_op jit(solution)/shard_map/right_rows/pallas_call | solution.py:293
  48.4 4.8 %pair_rows_0.1 = (bf16[12,4,1,6,128]{4,3,2,1,0:T(8,128)(2,1)S(1)}, bf16[1,16,384]{2,1,0:T(8,128)(2,1)S(1)}) custom-call(s32[3]{0:T(128)S(1)} %pad_add_fusion.place_ref, s32[192]{0:T(256)S(1)} %copy-done.9, bf16[6,192,128]{2,1,0:T(8,128)(2,1)S(1)} %copy-done.3, bf16[6,192,128]{2,1,0:T(8,128)(2,1)S(1)} %collective-permute-done.5.refs_1_, ...), custom_call_target="tpu_custom_call" | custom-call | bytes 14400000 | tf_op jit(solution)/shard_map/pair_rows_0/pallas_call | solution.py:293
  53.1 4.8 %pair_rows_1.1 = (bf16[12,4,1,6,128]{4,3,2,1,0:T(8,128)(2,1)S(1)}, bf16[1,16,384]{2,1,0:T(8,128)(2,1)S(1)}) custom-call(s32[3]{0:T(128)S(1)} %pad_add_fusion.place_ref, s32[192]{0:T(256)S(1)} %copy-done.9, bf16[6,192,128]{2,1,0:T(8,128)(2,1)S(1)} %collective-permute-done.6.refs_0_, bf16[6,192,128]{2,1,0:T(8,128)(2,1)S(1)} %collective-permute-done.7.refs_1_, ...), custom_call_target="tpu_custom_call" | custom-call | bytes 14400000 | tf_op jit(solution)/shard_map/pair_rows_1/pallas_call | solution.py:293
  57.9 0.0 collective-permute-done.9.refs_1_
  57.9 0.0 copy-start
  57.9 4.8 %pair_rows_2.1 = (bf16[12,4,1,6,128]{4,3,2,1,0:T(8,128)(2,1)S(1)}, bf16[1,16,384]{2,1,0:T(8,128)(2,1)S(1)}) custom-call(s32[3]{0:T(128)S(1)} %pad_add_fusion.place_ref, s32[192]{0:T(256)S(1)} %copy-done.9, bf16[6,192,128]{2,1,0:T(8,128)(2,1)S(1)} %collective-permute-done.8.refs_0_, bf16[6,192,128]{2,1,0:T(8,128)(2,1)S(1)} %collective-permute-done.9.refs_1_, ...), custom_call_target="tpu_custom_call" | custom-call | bytes 14400000 | tf_op jit(solution)/shard_map/pair_rows_2/pallas_call | solution.py:293
  62.7 0.0 collective-permute-done.1.refs_1_
  62.7 5.0 %pair_rows_3.1 = (bf16[48,4,1,6,128]{4,3,2,1,0:T(8,128)(2,1)S(1)}, bf16[4,16,384]{2,1,0:T(8,128)(2,1)S(1)}) custom-call(s32[3]{0:T(128)S(1)} %pad_add_fusion.place_ref, s32[192]{0:T(256)S(1)} %copy-done.9, bf16[6,192,128]{2,1,0:T(8,128)(2,1)S(1)} %collective-permute-done.refs_0_, bf16[6,192,128]{2,1,0:T(8,128)(2,1)S(1)} %collective-permute-done.1.refs_1_, ...), custom_call_target="tpu_custom_call" | custom-call | bytes 14400000 | tf_op jit(solution)/shard_map/pair_rows_3/pallas_call | solution.py:293
  67.7 0.0 copy-start.1
  67.7 0.2 collective-permute-start.14
  67.9 2.9 %collective-permute-start.16 = (bf16[4,16,384]{2,1,0:T(8,128)(2,1)S(1)}, bf16[4,16,384]{2,1,0:T(8,128)(2,1)S(1)}, u32[]{:S(2)}, u32[]{:S(2)}) collective-permute-start(bf16[4,16,384]{2,1,0:T(8,128)(2,1)S(1)} %get-tuple-element.24.refs_0_), channel_id=1, source_target_pairs={{0,4},{1,5},{2,6},{3,7},{4,0},{5,1},{6,2},{7,3},{8,12},{9,13},{10,... | collective-permute-start | bytes 147464 | tf_op jit(solution)/shard_map/ppermute | solution.py:342
  70.8 0.0 collective-permute-done.10.refs_1_
  70.8 1.4 %collective-permute-start.18 = (bf16[4,16,384]{2,1,0:T(8,128)(2,1)S(1)}, bf16[4,16,384]{2,1,0:T(8,128)(2,1)S(1)}, u32[]{:S(2)}, u32[]{:S(2)}) collective-permute-start(bf16[4,16,384]{2,1,0:T(8,128)(2,1)S(1)} %get-tuple-element.24.refs_0_), channel_id=1, source_target_pairs={{0,6},{1,7},{2,4},{3,5},{4,2},{5,3},{6,0},{7,1},{8,14},{9,15},{10,... | collective-permute-start | bytes 147464 | tf_op jit(solution)/shard_map/ppermute | solution.py:342
  72.2 0.0 collective-permute-done.11.refs_2_
  72.2 0.0 collective-permute-start.13
  72.2 0.0 collective-permute-done.14.refs_2_
  72.2 0.5 collective-permute-start.15
  72.7 0.2 collective-permute-done.16.refs_4_
  72.9 0.0 collective-permute-start.17
  72.9 3.8 %collective-permute-done.18.refs_6_ = bf16[4,16,384]{2,1,0:T(8,128)(2,1)S(1)} collective-permute-done((bf16[4,16,384]{2,1,0:T(8,128)(2,1)S(1)}, bf16[4,16,384]{2,1,0:T(8,128)(2,1)S(1)}, u32[]{:S(2)}, u32[]{:S(2)}) %collective-permute-start.18) | collective-permute-done | bytes 49184 | tf_op jit(solution)/shard_map/ppermute | solution.py:342
  76.7 0.0 collective-permute-start.19
  76.7 3.3 %project_tokens.1 = (bf16[2,64,768]{2,1,0:T(8,128)(2,1)S(1)}, bf16[2,768,256]{2,1,0:T(8,128)(2,1)S(1)}, bf16[2,768,256]{2,1,0:T(8,128)(2,1)S(1)}, f32[64,256]{1,0:T(8,128)S(1)}) custom-call(s32[3]{0:T(128)S(1)} %pad_add_fusion.place_ref, s32[1,192]{1,0:T(1,128)S(1)} %bitcast.26, s32[1,192]{1,0:T(1,128)S(1)} %bitcast.16, bf16[768,2304]{1,0:T(8,128)(2,1)S(1)} %copy-done, ...), custom_call_target="tpu_custom_call" | custom-call | bytes 18000000 | tf_op jit(solution)/shard_map/project_tokens/pallas_call | solution.py:293
  80.0 0.0 collective-permute-done.15.refs_3_
  80.0 0.0 collective-permute-done.17.refs_5_
  80.0 6.2 %attend.1 = bf16[8,12,768]{2,1,0:T(8,128)(2,1)} custom-call(bf16[2,64,768]{2,1,0:T(8,128)(2,1)S(1)} %get-tuple-element.21.query_ref, bf16[2,768,256]{2,1,0:T(8,128)(2,1)S(1)} %get-tuple-element.22.key_ref, bf16[2,768,256]{2,1,0:T(8,128)(2,1)S(1)} %get-tuple-element.23.value_ref, bf16[4,16,384]{2,1,0:T(8,128)(2,1)S(1)} %get-tuple-element.24.refs_0_, ...), custom_call_target="tpu_custom_call" | custom-call | bytes 21600000 | tf_op jit(solution)/shard_map/attend/pallas_call | solution.py:293
  86.2 3.4 %all-to-all-start.1 = ((bf16[8,12,768]{2,1,0:T(8,128)(2,1)}), bf16[8,12,768]{2,1,0:T(8,128)(2,1)S(1)}, u32[]{:S(2)}, u32[]{:S(2)}) async-start(bf16[8,12,768]{2,1,0:T(8,128)(2,1)} %attend.1), calls=%async_computation.1 | async-start | bytes 393216 | tf_op jit(solution)/shard_map/all_to_all | solution.py:413
  89.6 0.8 copy.35
  90.4 7.4 %all-to-all-done.1 = bf16[8,12,768]{2,1,0:T(8,128)(2,1)S(1)} async-done(((bf16[8,12,768]{2,1,0:T(8,128)(2,1)}), bf16[8,12,768]{2,1,0:T(8,128)(2,1)S(1)}, u32[]{:S(2)}, u32[]{:S(2)}) %all-to-all-start.1) | async-done | bytes 147488 | tf_op jit(solution)/shard_map/all_to_all | solution.py:413
  97.9 0.1 copy.34
  98.0 0.7 reshape.31
  (23 shorter events, 0.1 us)
Async XLA Ops:
  0.6 47.7 %copy-start.3 = (bf16[6,192,128]{2,1,0:T(8,128)(2,1)S(1)}, bf16[6,192,128]{2,1,0:T(8,128)(2,1)}, u32[]{:S(2)}) copy-start(bf16[6,192,128]{2,1,0:T(8,128)(2,1)} %refs_0_.3) | copy-start | bytes 884740
  0.6 47.7 %copy-start.11 = (f32[128]{0:T(128)S(1)}, f32[128]{0:T(128)}, u32[]{:S(2)}) copy-start(f32[128]{0:T(128)} %param.17) | copy-start | bytes 1540
  0.7 47.7 %copy-start.9 = (s32[192]{0:T(256)S(1)}, s32[192]{0:T(256)}, u32[]{:S(2)}) copy-start(s32[192]{0:T(256)} %mask_ref.9) | copy-start | bytes 2308
  0.7 47.7 %copy-start.12 = (f32[128]{0:T(128)S(1)}, f32[128]{0:T(128)}, u32[]{:S(2)}) copy-start(f32[128]{0:T(128)} %param.18) | copy-start | bytes 1540
  0.7 47.7 %copy-start.4 = (bf16[128,256]{1,0:T(8,128)(2,1)S(1)}, bf16[128,256]{1,0:T(8,128)(2,1)}, u32[]{:S(2)}) copy-start(bf16[128,256]{1,0:T(8,128)(2,1)} %refs_5_.7) | copy-start | bytes 196612
  0.7 47.7 %copy-start.5 = (bf16[128,128]{1,0:T(8,128)(2,1)S(1)}, bf16[128,128]{1,0:T(8,128)(2,1)}, u32[]{:S(2)}) copy-start(bf16[128,128]{1,0:T(8,128)(2,1)} %refs_6_.7) | copy-start | bytes 98308
  0.7 47.7 %copy-start.6 = (bf16[128,128]{1,0:T(8,128)(2,1)S(1)}, bf16[128,128]{1,0:T(8,128)(2,1)}, u32[]{:S(2)}) copy-start(bf16[128,128]{1,0:T(8,128)(2,1)} %refs_7_.7) | copy-start | bytes 98308
  0.7 10.2 %collective-permute-start.2 = (bf16[6,192,128]{2,1,0:T(8,128)(2,1)}, bf16[6,192,128]{2,1,0:T(8,128)(2,1)S(1)}, u32[]{:S(2)}, u32[]{:S(2)}) collective-permute-start(bf16[6,192,128]{2,1,0:T(8,128)(2,1)} %refs_0_.3), channel_id=1, source_target_pairs={{0,8},{1,9},{2,10},{3,11},{4,12},{5,13},{6,14},{7,15},{8,0},{9,1},... | collective-permute-start | bytes 884744 | tf_op jit(solution)/shard_map/ppermute | solution.py:342
  3.7 9.9 %collective-permute-start.3 = (bf16[6,192,128]{2,1,0:T(8,128)(2,1)}, bf16[6,192,128]{2,1,0:T(8,128)(2,1)S(1)}, u32[]{:S(2)}, u32[]{:S(2)}) collective-permute-start(bf16[6,192,128]{2,1,0:T(8,128)(2,1)} %refs_0_.3), channel_id=1, source_target_pairs={{0,16},{1,17},{2,18},{3,19},{4,20},{5,21},{6,22},{7,23},{8,24},{9,... | collective-permute-start | bytes 884744 | tf_op jit(solution)/shard_map/ppermute | solution.py:342
  5.2 13.7 %collective-permute-start.6 = (bf16[6,192,128]{2,1,0:T(8,128)(2,1)}, bf16[6,192,128]{2,1,0:T(8,128)(2,1)S(1)}, u32[]{:S(2)}, u32[]{:S(2)}) collective-permute-start(bf16[6,192,128]{2,1,0:T(8,128)(2,1)} %refs_0_.3), channel_id=1, source_target_pairs={{0,2},{1,3},{2,0},{3,1},{4,6},{5,7},{6,4},{7,5},{8,10},{9,11},{10,... | collective-permute-start | bytes 884744 | tf_op jit(solution)/shard_map/ppermute | solution.py:342
  6.8 23.9 %collective-permute-start.8 = (bf16[6,192,128]{2,1,0:T(8,128)(2,1)}, bf16[6,192,128]{2,1,0:T(8,128)(2,1)S(1)}, u32[]{:S(2)}, u32[]{:S(2)}) collective-permute-start(bf16[6,192,128]{2,1,0:T(8,128)(2,1)} %refs_0_.3), channel_id=1, source_target_pairs={{0,4},{1,5},{2,6},{3,7},{4,0},{5,1},{6,2},{7,3},{8,12},{9,13},{10,... | collective-permute-start | bytes 884744 | tf_op jit(solution)/shard_map/ppermute | solution.py:342
  9.4 21.3 %collective-permute-start = (bf16[6,192,128]{2,1,0:T(8,128)(2,1)}, bf16[6,192,128]{2,1,0:T(8,128)(2,1)S(1)}, u32[]{:S(2)}, u32[]{:S(2)}) collective-permute-start(bf16[6,192,128]{2,1,0:T(8,128)(2,1)} %refs_0_.3), channel_id=1, source_target_pairs={{0,6},{1,7},{2,4},{3,5},{4,2},{5,3},{6,0},{7,1},{8,14},{9,15},{10,... | collective-permute-start | bytes 884744 | tf_op jit(solution)/shard_map/ppermute | solution.py:342
  10.9 27.1 %collective-permute-start.4 = (bf16[6,192,128]{2,1,0:T(8,128)(2,1)}, bf16[6,192,128]{2,1,0:T(8,128)(2,1)}, u32[]{:S(2)}, u32[]{:S(2)}) collective-permute-start(bf16[6,192,128]{2,1,0:T(8,128)(2,1)} %refs_0_.3), channel_id=1, source_target_pairs={{0,24},{1,25},{2,26},{3,27},{4,28},{5,29},{6,30},{7,31},{8,16},{9,... | collective-permute-start | bytes 884744 | tf_op jit(solution)/shard_map/ppermute | solution.py:342
  13.6 24.9 %collective-permute-start.5 = (bf16[6,192,128]{2,1,0:T(8,128)(2,1)}, bf16[6,192,128]{2,1,0:T(8,128)(2,1)S(1)}, u32[]{:S(2)}, u32[]{:S(2)}) collective-permute-start(bf16[6,192,128]{2,1,0:T(8,128)(2,1)} %refs_0_.3), channel_id=1, source_target_pairs={{0,1},{1,0},{2,3},{3,2},{4,5},{5,4},{6,7},{7,6},{8,9},{9,8},{10,11... | collective-permute-start | bytes 884744 | tf_op jit(solution)/shard_map/ppermute | solution.py:342
  18.9 20.2 %collective-permute-start.7 = (bf16[6,192,128]{2,1,0:T(8,128)(2,1)S(1)}, bf16[6,192,128]{2,1,0:T(8,128)(2,1)S(1)}, u32[]{:S(2)}, u32[]{:S(2)}) collective-permute-start(bf16[6,192,128]{2,1,0:T(8,128)(2,1)S(1)} %collective-permute-done.6.refs_0_), channel_id=1, source_target_pairs={{0,1},{1,0},{2,3},{3,2},{4,5},{5,4},{6,7},{7,6},{8,9},{9,8},{10,11... | collective-permute-start | bytes 884744 | tf_op jit(solution)/shard_map/ppermute | solution.py:342
  20.6 17.4 %all-to-all-start = ((bf16[8,6,2,768]{3,2,1,0:T(2,128)(2,1)}), bf16[8,6,2,768]{3,2,1,0:T(2,128)(2,1)S(1)}, u32[]{:S(2)}, u32[]{:S(2)}) async-start(bf16[8,6,2,768]{3,2,1,0:T(2,128)(2,1)} %bitcast.14), calls=%async_computation | async-start | bytes 294912 | tf_op jit(solution)/shard_map/all_to_all | solution.py:355
  30.7 27.2 %collective-permute-start.9 = (bf16[6,192,128]{2,1,0:T(8,128)(2,1)S(1)}, bf16[6,192,128]{2,1,0:T(8,128)(2,1)S(1)}, u32[]{:S(2)}, u32[]{:S(2)}) collective-permute-start(bf16[6,192,128]{2,1,0:T(8,128)(2,1)S(1)} %collective-permute-done.8.refs_0_), channel_id=1, source_target_pairs={{0,1},{1,0},{2,3},{3,2},{4,5},{5,4},{6,7},{7,6},{8,9},{9,8},{10,11... | collective-permute-start | bytes 884744 | tf_op jit(solution)/shard_map/ppermute | solution.py:342
  30.7 32.0 %collective-permute-start.1 = (bf16[6,192,128]{2,1,0:T(8,128)(2,1)S(1)}, bf16[6,192,128]{2,1,0:T(8,128)(2,1)S(1)}, u32[]{:S(2)}, u32[]{:S(2)}) collective-permute-start(bf16[6,192,128]{2,1,0:T(8,128)(2,1)S(1)} %collective-permute-done.refs_0_), channel_id=1, source_target_pairs={{0,1},{1,0},{2,3},{3,2},{4,5},{5,4},{6,7},{7,6},{8,9},{9,8},{10,11... | collective-permute-start | bytes 884744 | tf_op jit(solution)/shard_map/ppermute | solution.py:342
  38.0 32.8 %collective-permute-start.10 = (bf16[8,6,2,768]{3,2,1,0:T(2,128)(2,1)S(1)}, bf16[8,6,2,768]{3,2,1,0:T(2,128)(2,1)S(1)}, u32[]{:S(2)}, u32[]{:S(2)}) collective-permute-start(bf16[8,6,2,768]{3,2,1,0:T(2,128)(2,1)S(1)} %all-to-all-done.refs_0_), channel_id=1, source_target_pairs={{0,8},{1,9},{2,10},{3,11},{4,12},{5,13},{6,14},{7,15},{8,0},{9,1},... | collective-permute-start | bytes 442376 | tf_op jit(solution)/shard_map/ppermute | solution.py:342
  38.6 33.6 %collective-permute-start.11 = (bf16[8,6,2,768]{3,2,1,0:T(2,128)(2,1)S(1)}, bf16[8,6,2,768]{3,2,1,0:T(2,128)(2,1)}, u32[]{:S(2)}, u32[]{:S(2)}) collective-permute-start(bf16[8,6,2,768]{3,2,1,0:T(2,128)(2,1)S(1)} %all-to-all-done.refs_0_), channel_id=1, source_target_pairs={{0,16},{1,17},{2,18},{3,19},{4,20},{5,21},{6,22},{7,23},{8,24},{9,... | collective-permute-start | bytes 442376 | tf_op jit(solution)/shard_map/ppermute | solution.py:342
  39.1 37.6 %collective-permute-start.12 = (bf16[8,6,2,768]{3,2,1,0:T(2,128)(2,1)S(1)}, bf16[8,6,2,768]{3,2,1,0:T(2,128)(2,1)}, u32[]{:S(2)}, u32[]{:S(2)}) collective-permute-start(bf16[8,6,2,768]{3,2,1,0:T(2,128)(2,1)S(1)} %all-to-all-done.refs_0_), channel_id=1, source_target_pairs={{0,24},{1,25},{2,26},{3,27},{4,28},{5,29},{6,30},{7,31},{8,16},{9,... | collective-permute-start | bytes 442376 | tf_op jit(solution)/shard_map/ppermute | solution.py:342
  42.4 1.0 copy-start.2
  43.4 0.8 copy-start.7
  44.2 0.7 copy-start.8
  44.9 0.7 copy-start.10
  57.9 18.8 %copy-start = (bf16[768,2304]{1,0:T(8,128)(2,1)S(1)}, bf16[768,2304]{1,0:T(8,128)(2,1)}, u32[]{:S(2)}) copy-start(bf16[768,2304]{1,0:T(8,128)(2,1)} %weight_ref.3) | copy-start | bytes 10616836
  62.7 14.0 %copy-start.13 = (s32[192]{0:T(256)S(1)}, s32[192]{0:T(256)}, u32[]{:S(2)}) copy-start(s32[192]{0:T(256)} %param.16) | copy-start | bytes 2308
  67.7 12.3 %copy-start.1 = (bf16[768,768]{1,0:T(8,128)(2,1)S(1)}, bf16[768,768]{1,0:T(8,128)(2,1)}, u32[]{:S(2)}) copy-start(bf16[768,768]{1,0:T(8,128)(2,1)} %refs_9_.1) | copy-start | bytes 3538948
  67.7 4.5 %collective-permute-start.14 = (bf16[4,16,384]{2,1,0:T(8,128)(2,1)S(1)}, bf16[4,16,384]{2,1,0:T(8,128)(2,1)S(1)}, u32[]{:S(2)}, u32[]{:S(2)}) collective-permute-start(bf16[4,16,384]{2,1,0:T(8,128)(2,1)S(1)} %get-tuple-element.24.refs_0_), channel_id=1, source_target_pairs={{0,2},{1,3},{2,0},{3,1},{4,6},{5,7},{6,4},{7,5},{8,10},{9,11},{10,... | collective-permute-start | bytes 147464 | tf_op jit(solution)/shard_map/ppermute | solution.py:342
  67.9 5.0 %collective-permute-start.16 = (bf16[4,16,384]{2,1,0:T(8,128)(2,1)S(1)}, bf16[4,16,384]{2,1,0:T(8,128)(2,1)S(1)}, u32[]{:S(2)}, u32[]{:S(2)}) collective-permute-start(bf16[4,16,384]{2,1,0:T(8,128)(2,1)S(1)} %get-tuple-element.24.refs_0_), channel_id=1, source_target_pairs={{0,4},{1,5},{2,6},{3,7},{4,0},{5,1},{6,2},{7,3},{8,12},{9,13},{10,... | collective-permute-start | bytes 147464 | tf_op jit(solution)/shard_map/ppermute | solution.py:342
  70.8 5.9 %collective-permute-start.18 = (bf16[4,16,384]{2,1,0:T(8,128)(2,1)S(1)}, bf16[4,16,384]{2,1,0:T(8,128)(2,1)S(1)}, u32[]{:S(2)}, u32[]{:S(2)}) collective-permute-start(bf16[4,16,384]{2,1,0:T(8,128)(2,1)S(1)} %get-tuple-element.24.refs_0_), channel_id=1, source_target_pairs={{0,6},{1,7},{2,4},{3,5},{4,2},{5,3},{6,0},{7,1},{8,14},{9,15},{10,... | collective-permute-start | bytes 147464 | tf_op jit(solution)/shard_map/ppermute | solution.py:342
  72.2 7.8 %collective-permute-start.13 = (bf16[4,16,384]{2,1,0:T(8,128)(2,1)S(1)}, bf16[4,16,384]{2,1,0:T(8,128)(2,1)S(1)}, u32[]{:S(2)}, u32[]{:S(2)}) collective-permute-start(bf16[4,16,384]{2,1,0:T(8,128)(2,1)S(1)} %get-tuple-element.24.refs_0_), channel_id=1, source_target_pairs={{0,1},{1,0},{2,3},{3,2},{4,5},{5,4},{6,7},{7,6},{8,9},{9,8},{10,11... | collective-permute-start | bytes 147464 | tf_op jit(solution)/shard_map/ppermute | solution.py:342
  72.2 7.8 %collective-permute-start.15 = (bf16[4,16,384]{2,1,0:T(8,128)(2,1)S(1)}, bf16[4,16,384]{2,1,0:T(8,128)(2,1)S(1)}, u32[]{:S(2)}, u32[]{:S(2)}) collective-permute-start(bf16[4,16,384]{2,1,0:T(8,128)(2,1)S(1)} %collective-permute-done.14.refs_2_), channel_id=1, source_target_pairs={{0,1},{1,0},{2,3},{3,2},{4,5},{5,4},{6,7},{7,6},{8,9},{9,8},{10,11... | collective-permute-start | bytes 147464 | tf_op jit(solution)/shard_map/ppermute | solution.py:342
  72.9 7.1 %collective-permute-start.17 = (bf16[4,16,384]{2,1,0:T(8,128)(2,1)S(1)}, bf16[4,16,384]{2,1,0:T(8,128)(2,1)S(1)}, u32[]{:S(2)}, u32[]{:S(2)}) collective-permute-start(bf16[4,16,384]{2,1,0:T(8,128)(2,1)S(1)} %collective-permute-done.16.refs_4_), channel_id=1, source_target_pairs={{0,1},{1,0},{2,3},{3,2},{4,5},{5,4},{6,7},{7,6},{8,9},{9,8},{10,11... | collective-permute-start | bytes 147464 | tf_op jit(solution)/shard_map/ppermute | solution.py:342
  76.7 3.3 %collective-permute-start.19 = (bf16[4,16,384]{2,1,0:T(8,128)(2,1)S(1)}, bf16[4,16,384]{2,1,0:T(8,128)(2,1)S(1)}, u32[]{:S(2)}, u32[]{:S(2)}) collective-permute-start(bf16[4,16,384]{2,1,0:T(8,128)(2,1)S(1)} %collective-permute-done.18.refs_6_), channel_id=1, source_target_pairs={{0,1},{1,0},{2,3},{3,2},{4,5},{5,4},{6,7},{7,6},{8,9},{9,8},{10,11... | collective-permute-start | bytes 147464 | tf_op jit(solution)/shard_map/ppermute | solution.py:342
  86.2 11.7 %all-to-all-start.1 = ((bf16[8,12,768]{2,1,0:T(8,128)(2,1)}), bf16[8,12,768]{2,1,0:T(8,128)(2,1)S(1)}, u32[]{:S(2)}, u32[]{:S(2)}) async-start(bf16[8,12,768]{2,1,0:T(8,128)(2,1)} %attend.1), calls=%async_computation.1 | async-start | bytes 393216 | tf_op jit(solution)/shard_map/all_to_all | solution.py:413

commit v3 on v2

--- a/solution.py
+++ b/solution.py
@@ -52,13 +52,13 @@
         lax.fori_loop(0, rows // group, lambda g, carry: (step(g * group, group), carry)[1], 0)
 
 
-def right_kernel(place_ref, mask_ref, valid_ref, gain_ref, weight_ref, *refs):
+def right_kernel(place_ref, mask_ref, table_ref, gains_ref, weight_ref, *refs):
     pair_refs, right_ref = refs[:-1], refs[-1]
     rows, tokens, channels = pair_refs[0].shape
-    gain = gain_ref[...]
-    weight = weight_ref[...]
+    gain = gains_ref[0:1]
+    weight = weight_ref[:, 2 * channels : 4 * channels]
     row_index, col_index, col_count = place_ref[0], place_ref[1], place_ref[2]
-    valid = jnp.broadcast_to((valid_ref[...] == 1).astype(jnp.float32), (channels, tokens)).T
+    valid = jnp.broadcast_to((table_ref[0:1] == 1).astype(jnp.float32), (channels, tokens)).T
     for block, pair_ref in enumerate(pair_refs):
         first = ((row_index ^ block) * col_count + col_index) * rows
 
@@ -73,91 +73,91 @@
         in_groups(rows, tokens, step)
 
 
-def pair_kernel(block_count, step_at, earlier, place_ref, mask_ref, *refs):
-    same_ref, other_ref, right_ref = refs[:3]
-    gain_ref, mix_ref, left_ref, gate_ref, out_ref, bias_ref = refs[3:9]
-    given = refs[9 : 9 + 2 * len(earlier)]
-    new_ref, head_ref, left_f, floats, tile_f, mixed_f = refs[9 + 2 * len(earlier) :]
-    rows, tokens, channels = same_ref.shape
+def pair_kernel(block_count, steps, head_count, place_ref, mask_ref, *refs):
+    pair_refs = refs[: 2 * steps]
+    right_ref, gains_ref, weight_ref, new_ref, head_ref, left_f, floats, tile_f, mixed_f = refs[
+        2 * steps :
+    ]
+    rows, tokens, channels = pair_refs[0].shape
     pair_rows = 2 * rows
-    gain = gain_ref[...]
-    weight = left_ref[...]
+    gain, mix = gains_ref[0:1], gains_ref[1:2]
+    weight = weight_ref[:, : 2 * channels]
+    gate_weight = weight_ref[:, 4 * channels : 5 * channels]
+    out_weight = weight_ref[:, 5 * channels : 6 * channels]
+    bias_weight = weight_ref[:, 6 * channels : 6 * channels + head_count]
     row_index, col_index, col_count = place_ref[0], place_ref[1], place_ref[2]
     floats[:, tokens:] = jnp.zeros((rows, SUB, channels), jnp.float32)
-    for chunk, pair_ref in enumerate((same_ref, other_ref)):
-        chunk_col = col_index ^ (2 * step_at + chunk)
-        base = (chunk_col % 2) * rows
-        first = (row_index * col_count + chunk_col) * rows
-
-        def step(start, count):
-            values = pair_ref[pl.ds(start, count)].astype(jnp.float32)
-            floats[pl.ds(start, count), :tokens] = values
-            edges = edge_rows(values, gain, weight)
-            for i in range(count):
-                own = (mask_ref[first + start + i] == 1).astype(jnp.float32)
-                left_f[base + start + i] = (
-                    (edges[i] * own).astype(jnp.bfloat16).astype(jnp.float32)
+    mixed_f[:, :, rows:, :] = jnp.zeros((pair_rows, block_count, SUB - rows, channels), jnp.float32)
+    chip = col_index // 2
+    for step_at in range(steps):
+        for chunk, pair_ref in enumerate(pair_refs[2 * step_at : 2 * step_at + 2]):
+            chunk_col = col_index ^ (2 * step_at + chunk)
+            base = (chunk_col % 2) * rows
+            first = (row_index * col_count + chunk_col) * rows
+
+            def step(start, count):
+                values = pair_ref[pl.ds(start, count)].astype(jnp.float32)
+                floats[pl.ds(start, count), :tokens] = values
+                edges = edge_rows(values, gain, weight)
+                for i in range(count):
+                    own = (mask_ref[first + start + i] == 1).astype(jnp.float32)
+                    left_f[base + start + i] = (
+                        (edges[i] * own).astype(jnp.bfloat16).astype(jnp.float32)
+                    )
+
+            in_groups(rows, tokens, step)
+            for i in range(rows):
+                for block in range(block_count):
+                    start = ((row_index ^ block) * col_count + col_index) * rows
+                    tile_f[base + i, block] = floats[i, pl.ds(start, SUB), :]
+
+        def product(n, carry):
+            block, half = n // 2, n % 2
+
+            def slab(k, sums):
+                at = pl.ds(pl.multiple_of(k * SUB, SUB), SUB)
+                lefts = [left_f[half * rows + i, at, :] for i in range(rows)]
+                rights = [right_ref[block * rows + t, at, :] for t in range(rows)]
+                return tuple(
+                    sums[i * rows + t] + lefts[i] * rights[t] for i in range(rows) for t in range(rows)
                 )
 
-        in_groups(rows, tokens, step)
-        for i in range(rows):
-            for block in range(block_count):
-                start = ((row_index ^ block) * col_count + col_index) * rows
-                tile_f[base + i, block] = floats[i, pl.ds(start, SUB), :]
-    mixed_f[:, :, rows:, :] = jnp.zeros((pair_rows, block_count, SUB - rows, channels), jnp.float32)
-
-    def product(n, carry):
-        block, half = n // 2, n % 2
-
-        def slab(k, sums):
-            at = pl.ds(pl.multiple_of(k * SUB, SUB), SUB)
-            lefts = [left_f[half * rows + i, at, :] for i in range(rows)]
-            rights = [right_ref[block * rows + t, at, :] for t in range(rows)]
-            return tuple(
-                sums[i * rows + t] + lefts[i] * rights[t] for i in range(rows) for t in range(rows)
-            )
-
-        zero = jnp.zeros((SUB, channels), jnp.float32)
-        sums = lax.fori_loop(0, tokens // SUB, slab, (zero,) * (rows * rows), unroll=24)
-        for i in range(rows):
-            for t in range(rows):
-                mixed_f[half * rows + i, block, t : t + 1, :] = jnp.sum(
-                    sums[i * rows + t], axis=0, keepdims=True
-                )
-        return carry
-
-    lax.fori_loop(0, 2 * block_count, product, 0)
-    flat = pair_rows * block_count * SUB
-    mixed_norm = layer_norm(mixed_f[...].reshape(flat, channels), mix_ref[...]).astype(jnp.bfloat16)
-    pair = tile_f[...].reshape(flat, channels)
-    normed = layer_norm(pair, gain).astype(jnp.bfloat16)
-    gate = sigmoid(jnp.dot(normed, gate_ref[...], preferred_element_type=jnp.float32))
-    update = jnp.dot(mixed_norm, out_ref[...], preferred_element_type=jnp.float32)
-    pair_new = (pair + gate * update).astype(jnp.bfloat16).astype(jnp.float32)
-    split = pair_new.reshape(pair_rows, block_count, SUB, channels)
-    bias_input = layer_norm(pair_new, None).astype(jnp.bfloat16)
-    bias = lax.dot_general(
-        bias_ref[...], bias_input, (((0,), (1,)), ((), ())), preferred_element_type=jnp.float32
-    )
-    joins = new_ref.shape[0] > pair_rows
-    chip = col_index // 2
-    place = chip ^ step_at if joins else 0
-    for block in range(block_count):
-        new_ref[pl.ds(place * pair_rows, pair_rows), row_index ^ block, 0] = split[
-            :, block, :rows, :
-        ].astype(jnp.bfloat16)
-    head_ref[place] = bias.astype(jnp.bfloat16)
-    for n, k in enumerate(earlier):
-        new_ref[pl.ds((chip ^ k) * pair_rows, pair_rows)] = given[2 * n][...]
-        head_ref[chip ^ k] = given[2 * n + 1][0]
-
-
-def project_kernel(block_count, place_ref, chain_ref, valid_ref, weight_ref, *refs):
+            zero = jnp.zeros((SUB, channels), jnp.float32)
+            sums = lax.fori_loop(0, tokens // SUB, slab, (zero,) * (rows * rows), unroll=24)
+            for i in range(rows):
+                for t in range(rows):
+                    mixed_f[half * rows + i, block, t : t + 1, :] = jnp.sum(
+                        sums[i * rows + t], axis=0, keepdims=True
+                    )
+            return carry
+
+        lax.fori_loop(0, 2 * block_count, product, 0)
+        flat = pair_rows * block_count * SUB
+        mixed_norm = layer_norm(mixed_f[...].reshape(flat, channels), mix).astype(jnp.bfloat16)
+        pair = tile_f[...].reshape(flat, channels)
+        normed = layer_norm(pair, gain).astype(jnp.bfloat16)
+        gate = sigmoid(jnp.dot(normed, gate_weight, preferred_element_type=jnp.float32))
+        update = jnp.dot(mixed_norm, out_weight, preferred_element_type=jnp.float32)
+        pair_new = (pair + gate * update).astype(jnp.bfloat16).astype(jnp.float32)
+        split = pair_new.reshape(pair_rows, block_count, SUB, channels)
+        bias_input = layer_norm(pair_new, None).astype(jnp.bfloat16)
+        bias = lax.dot_general(
+            bias_weight, bias_input, (((0,), (1,)), ((), ())), preferred_element_type=jnp.float32
+        )
+        place = chip ^ step_at
+        for block in range(block_count):
+            new_ref[pl.ds(place * pair_rows, pair_rows), row_index ^ block, 0] = split[
+                :, block, :rows, :
+            ].astype(jnp.bfloat16)
+        head_ref[place] = bias.astype(jnp.bfloat16)
+
+
+def project_kernel(block_count, place_ref, table_ref, weight_ref, *refs):
     single_refs = refs[:block_count]
     query_ref, key_ref, value_ref, allowed_ref, rows_f, own_f = refs[block_count:]
     col_count, rows, samples, width = single_refs[0].shape
     query_rows, key_count = allowed_ref.shape
-    tokens = chain_ref.shape[1]
+    tokens = table_ref.shape[1]
     row_index, col_index = place_ref[0], place_ref[1]
     rows_f[...] = jnp.zeros_like(rows_f)
     own_f[...] = jnp.zeros_like(own_f)
@@ -198,8 +198,8 @@
         token = (row_index * col_count + place // SUB) * rows + t
         return jnp.where(t < rows, token, -2)
 
-    chains = chain_ref[...].astype(jnp.float32)
-    valid = (valid_ref[...] == 1).astype(jnp.float32)
+    chains = table_ref[1:2].astype(jnp.float32)
+    valid = (table_ref[0:1] == 1).astype(jnp.float32)
     token = lax.broadcasted_iota(jnp.int32, (query_rows, tokens), 1)
     hit = query_tokens((query_rows, tokens)) == token
     query_chain = jnp.sum(jnp.where(hit, chains, 0.0), axis=1, keepdims=True)
@@ -342,10 +342,12 @@
         return lax.ppermute(values, AXES, steps)
 
     place = jnp.stack([row_index, col_index, jnp.int32(col_count)]).astype(jnp.int32)
-    gain = pair_gain.reshape(1, channels)
-    mix = mix_gain.reshape(1, channels)
-    valid_row = token_mask.reshape(1, tokens)
-    chain_row = chain_ids.reshape(1, tokens)
+    gains = jnp.stack([pair_gain, mix_gain])
+    table = jnp.stack([token_mask, chain_ids])
+    bias_columns = jnp.pad(bias_weight, ((0, 0), (0, LANES - heads)))
+    weights = jnp.concatenate(
+        [left_weight, right_weight, gate_weight, out_weight, bias_columns], axis=1
+    )
 
     same = [pair_state] + [send(pair_state, 0, 2 * k) for k in range(1, chips)]
     other = [send(values, 0, 1) for values in same]
@@ -357,36 +359,30 @@
 
     (rights,) = call(
         right_kernel, "right_rows",
-        [place, token_mask, valid_row, gain, right_weight, *columns], 2,
+        [place, token_mask, table, gains, weights, *columns], 2,
         [((row_count * rows, tokens, channels), f32)], [], 3.0,
     )
-    done = []
-    for k in range(chips):
-        last = k == chips - 1
-        count = chips if last else 1
-        earlier = tuple(range(k)) if last else ()
-        pair_new, pair_heads = call(
-            functools.partial(pair_kernel, row_count, k, earlier), f"pair_rows_{k}",
-            [
-                place, token_mask, same[k], other[k], rights, gain, mix, left_weight,
-                gate_weight, out_weight, bias_weight, *(x for n in earlier for x in done[n]),
-            ], 2,
-            [
-                ((count * 2 * rows, row_count, 1, rows, channels), bf16),
-                ((count, heads, 2 * rows * part), bf16),
-            ],
-            [
-                ((2 * rows, tokens, channels), f32),
-                ((rows, tokens + SUB, channels), f32),
-                ((2 * rows, row_count, SUB, channels), f32),
-                ((2 * rows, row_count, SUB, channels), f32),
-            ], 4.0,
-        )
-        done.append((pair_new, pair_heads))
+    pair_new, pair_heads = call(
+        functools.partial(pair_kernel, row_count, chips, heads), "pair_rows",
+        [
+            place, token_mask, *(x for k in range(chips) for x in (same[k], other[k])), rights,
+            gains, weights,
+        ], 2,
+        [
+            ((rows * col_count, row_count, 1, rows, channels), bf16),
+            ((chips, heads, 2 * rows * part), bf16),
+        ],
+        [
+            ((2 * rows, tokens, channels), f32),
+            ((rows, tokens + SUB, channels), f32),
+            ((2 * rows, row_count, SUB, channels), f32),
+            ((2 * rows, row_count, SUB, channels), f32),
+        ], 4.0,
+    )
 
     queries, key_cols, value_cols, allowed = call(
         functools.partial(project_kernel, row_count), "project_tokens",
-        [place, chain_row, valid_row, token_weight, *singles], 1,
+        [place, table, token_weight, *singles], 1,
         [
             ((own_samples, query_rows, width), bf16),
             ((own_samples, width, keys), bf16),

time: 99.3 us -> 95.5 us (0.962)
  waiting for transfers between devices: 30.2 us -> 26.7 us
  Pallas kernels: 31.5 us -> 29.3 us
  local copies, waits for them, and re-layouts: 7.43 us -> 9.14 us
  other arithmetic: 0.08 us -> 1.46 us
  starting transfers between devices: 28.7 us -> 27.4 us
    pallas_call x7 -> x4, Pallas kernels: 31.5 us -> 29.3 us  [call(): pl.pallas_call(kernel, in_specs=[SCALARS] * scalars + [BLOCK] * (len(oper...]
    all_to_all x1, waiting for transfers between devices: 6.79 us -> 4.71 us  [shards(): lax.all_to_all(jnp.transpose(by_token, (1, 0, 2, 3)), 'col', 0, 0, tiled=...]
    unnamed x30 -> x18, local copies, waits for them, and re-layouts: 4.82 us -> 6.51 us
    ppermute x20, starting transfers between devices: 20.6 us -> 19 us  [send(): return lax.ppermute(values, AXES, steps)]
    ppermute x20, waiting for transfers between devices: 16 us -> 14.6 us  [send(): return lax.ppermute(values, AXES, steps)]
    another operation x0 -> x2, other arithmetic: none -> 1.38 us  [the longest x1 0.7 us: shards(): table = jnp.stack([token_mask, chain_ids])]
  transfers between devices with their start and end apart: 22 -> 22, of which waited for: 7 -> 5; matrix products, arithmetic and copies ran while one was open for 3% -> 8% of each run, Pallas kernels for 26% -> 24%
where the time goes in v3:
time: 95.5 us; the launch traced here: 94.9 us
  Pallas kernels  29.3 us (31%)
  starting transfers between devices  27.4 us (29%)
  waiting for transfers between devices  26.7 us (28%)
  local copies, waits for them, and re-layouts  9.14 us (10%)
  other arithmetic  1.46 us (2%)
    pallas_call x4, Pallas kernels, call(): pl.pallas_call(kernel, in_specs=[SCALARS] * scalars + [BLOCK] * (len(oper...  29.3 us
    ppermute x20, starting transfers between devices, send(): return lax.ppermute(values, AXES, steps)  19 us
    ppermute x20, waiting for transfers between devices, send(): return lax.ppermute(values, AXES, steps)  14.6 us
    all_to_all x1, waiting for transfers between devices, shards(): arrived = lax.all_to_all(merged, 'col', 0, 0, tiled=True)  7.43 us
    unnamed x18, local copies, waits for them, and re-layouts  6.51 us
    all_to_all x1, starting transfers between devices, shards(): lax.all_to_all(jnp.transpose(by_token, (1, 0, 2, 3)), 'col', 0, 0, tiled=...  5.01 us
    all_to_all x1, waiting for transfers between devices, shards(): lax.all_to_all(jnp.transpose(by_token, (1, 0, 2, 3)), 'col', 0, 0, tiled=...  4.71 us
    all_to_all x1, starting transfers between devices, shards(): arrived = lax.all_to_all(merged, 'col', 0, 0, tiled=True)  3.39 us
  transfers between devices with their start and end apart: 22, of which 5 were waited for; matrix products, arithmetic and copies ran while one was open for 8% of the time, Pallas kernels for 24%

profile of v3, /device:TPU:0, one launch (start us, length us, event | category | flops | bytes accessed | tf_op | source)
XLA Modules:
  0.0 94.9 jit_solution(16690984604696815315)
XLA Ops:
  0.6 3.0 %collective-permute-start.7 = (bf16[6,192,128]{2,1,0:T(8,128)(2,1)}, bf16[6,192,128]{2,1,0:T(8,128)(2,1)S(1)}, u32[]{:S(2)}, u32[]{:S(2)}) collective-permute-start(bf16[6,192,128]{2,1,0:T(8,128)(2,1)} %refs_0_.3), channel_id=1, source_target_pairs={{0,8},{1,9},{2,10},{3,11},{4,12},{5,13},{6,14},{7,15},{8,0},{9,1},... | collective-permute-start | bytes 884744 | tf_op jit(solution)/shard_map/ppermute | solution.py:342
  3.6 1.5 %collective-permute-start.8 = (bf16[6,192,128]{2,1,0:T(8,128)(2,1)}, bf16[6,192,128]{2,1,0:T(8,128)(2,1)S(1)}, u32[]{:S(2)}, u32[]{:S(2)}) collective-permute-start(bf16[6,192,128]{2,1,0:T(8,128)(2,1)} %refs_0_.3), channel_id=1, source_target_pairs={{0,16},{1,17},{2,18},{3,19},{4,20},{5,21},{6,22},{7,23},{8,24},{9,... | collective-permute-start | bytes 884744 | tf_op jit(solution)/shard_map/ppermute | solution.py:342
  5.2 1.6 %collective-permute-start.1 = (bf16[6,192,128]{2,1,0:T(8,128)(2,1)}, bf16[6,192,128]{2,1,0:T(8,128)(2,1)S(1)}, u32[]{:S(2)}, u32[]{:S(2)}) collective-permute-start(bf16[6,192,128]{2,1,0:T(8,128)(2,1)} %refs_0_.3), channel_id=1, source_target_pairs={{0,2},{1,3},{2,0},{3,1},{4,6},{5,7},{6,4},{7,5},{8,10},{9,11},{10,... | collective-permute-start | bytes 884744 | tf_op jit(solution)/shard_map/ppermute | solution.py:342
  6.7 2.6 %collective-permute-start.3 = (bf16[6,192,128]{2,1,0:T(8,128)(2,1)}, bf16[6,192,128]{2,1,0:T(8,128)(2,1)S(1)}, u32[]{:S(2)}, u32[]{:S(2)}) collective-permute-start(bf16[6,192,128]{2,1,0:T(8,128)(2,1)} %refs_0_.3), channel_id=1, source_target_pairs={{0,4},{1,5},{2,6},{3,7},{4,0},{5,1},{6,2},{7,3},{8,12},{9,13},{10,... | collective-permute-start | bytes 884744 | tf_op jit(solution)/shard_map/ppermute | solution.py:342
  9.3 0.2 collective-permute-start.5
  9.5 1.0 %reshape.13 = bf16[6,8,2,768]{3,2,1,0:T(2,128)(2,1)S(1)} reshape(bf16[6,16,768]{2,1,0:T(8,128)(2,1)} %bitcast.17) | data formatting | bytes 294912 | tf_op jit(solution)/shard_map/reshape | solution.py:356
  10.5 0.8 copy.28
  11.3 5.0 %all-to-all-start = ((bf16[8,6,2,768]{3,2,1,0:T(2,128)(2,1)}), bf16[8,6,2,768]{3,2,1,0:T(2,128)(2,1)S(1)}, u32[]{:S(2)}, u32[]{:S(2)}) async-start(bf16[8,6,2,768]{3,2,1,0:T(2,128)(2,1)} %bitcast.14), calls=%async_computation | async-start | bytes 294912 | tf_op jit(solution)/shard_map/all_to_all | solution.py:357
  16.3 0.8 constant_dynamic-update-slice_fusion.3
  17.1 0.8 constant_dynamic-update-slice_fusion.2
  18.0 0.8 constant_dynamic-update-slice_fusion.1
  18.7 0.0 collective-permute-done.7.refs_1_
  18.8 0.5 collective-permute-start.9
  19.3 0.8 constant_dynamic-update-slice_fusion
  20.1 0.8 copy.22
  20.9 0.0 collective-permute-done.8.refs_2_
  20.9 0.3 collective-permute-start
  21.2 0.0 collective-permute-done.1.refs_2_
  21.2 0.3 collective-permute-start.2
  21.5 10.5 %collective-permute-done.3.refs_4_ = bf16[6,192,128]{2,1,0:T(8,128)(2,1)S(1)} collective-permute-done((bf16[6,192,128]{2,1,0:T(8,128)(2,1)}, bf16[6,192,128]{2,1,0:T(8,128)(2,1)S(1)}, u32[]{:S(2)}, u32[]{:S(2)}) %collective-permute-start.3) | collective-permute-done | bytes 294944 | tf_op jit(solution)/shard_map/ppermute | solution.py:342
  32.0 0.0 collective-permute-start.4
  32.0 0.0 collective-permute-done.5.refs_6_
  32.0 0.5 collective-permute-start.6
  32.5 0.7 pad_add_fusion.table_ref
  33.2 4.7 %all-to-all-done.refs_0_ = bf16[8,6,2,768]{3,2,1,0:T(2,128)(2,1)S(1)} async-done(((bf16[8,6,2,768]{3,2,1,0:T(2,128)(2,1)}), bf16[8,6,2,768]{3,2,1,0:T(2,128)(2,1)S(1)}, u32[]{:S(2)}, u32[]{:S(2)}) %all-to-all-start) | async-done | bytes 147488 | tf_op jit(solution)/shard_map/all_to_all | solution.py:357
  37.9 0.0 collective-permute-done.9.refs_3_
  37.9 0.5 collective-permute-start.10
  38.5 0.7 pad_maximum_fusion.gains_ref.refs_9_
  39.2 0.0 collective-permute-done.refs_1_
  39.2 0.6 collective-permute-start.11
  39.7 0.0 collective-permute-done.2.refs_3_
  39.7 2.5 %collective-permute-start.12 = (bf16[8,6,2,768]{3,2,1,0:T(2,128)(2,1)S(1)}, bf16[8,6,2,768]{3,2,1,0:T(2,128)(2,1)S(1)}, u32[]{:S(2)}, u32[]{:S(2)}) collective-permute-start(bf16[8,6,2,768]{3,2,1,0:T(2,128)(2,1)S(1)} %all-to-all-done.refs_0_), channel_id=1, source_target_pairs={{0,24},{1,25},{2,26},{3,27},{4,28},{5,29},{6,30},{7,31},{8,16},{9,... | collective-permute-start | bytes 442376 | tf_op jit(solution)/shard_map/ppermute | solution.py:342
  42.2 0.1 pad_add_fusion.1.place_ref
  42.3 1.0 %copy-done.1 = bf16[6,192,128]{2,1,0:T(8,128)(2,1)S(1)} copy-done((bf16[6,192,128]{2,1,0:T(8,128)(2,1)S(1)}, bf16[6,192,128]{2,1,0:T(8,128)(2,1)}, u32[]{:S(2)}) %copy-start.1) | copy-done | bytes 294936
  43.2 0.7 copy-done.4
  43.9 2.3 %right_rows.1.refs_8_ = f32[24,192,128]{2,1,0:T(8,128)S(1)} custom-call(s32[3]{0:T(128)S(1)} %pad_add_fusion.1.place_ref, s32[192]{0:T(256)S(1)} %copy-done.4, s32[2,192]{1,0:T(2,128)S(1)} %pad_add_fusion.table_ref, f32[2,128]{1,0:T(2,128)S(1)} %pad_maximum_fusion.gains_ref.refs_9_, bf16[128,896]{1,0:T(8,128)(2,1)S(1)} %pad_dynamic-update-slice_fusion.weight_ref.refs_10_, ...), custom_call_target="tpu_custom_call" | custom-call | bytes 10800000 | tf_op jit(solution)/shard_map/right_rows/pallas_call | solution.py:293
  46.2 0.0 copy-start
  46.2 0.0 collective-permute-done.4.refs_5_
  46.3 0.0 collective-permute-done.6.refs_7_
  46.3 17.6 %pair_rows.1 = (bf16[48,4,1,6,128]{4,3,2,1,0:T(8,128)(2,1)S(1)}, bf16[4,16,384]{2,1,0:T(8,128)(2,1)S(1)}) custom-call(s32[3]{0:T(128)S(1)} %pad_add_fusion.1.place_ref, s32[192]{0:T(256)S(1)} %copy-done.5, bf16[6,192,128]{2,1,0:T(8,128)(2,1)S(1)} %copy-done.2, bf16[6,192,128]{2,1,0:T(8,128)(2,1)S(1)} %collective-permute-done.refs_1_, ...), custom_call_target="tpu_custom_call" | custom-call | bytes 14400000 | tf_op jit(solution)/shard_map/pair_rows/pallas_call | solution.py:293
  63.9 0.6 collective-permute-start.14
  64.4 2.5 %collective-permute-start.16 = (bf16[4,16,384]{2,1,0:T(8,128)(2,1)S(1)}, bf16[4,16,384]{2,1,0:T(8,128)(2,1)S(1)}, u32[]{:S(2)}, u32[]{:S(2)}) collective-permute-start(bf16[4,16,384]{2,1,0:T(8,128)(2,1)S(1)} %get-tuple-element.12.refs_0_), channel_id=1, source_target_pairs={{0,4},{1,5},{2,6},{3,7},{4,0},{5,1},{6,2},{7,3},{8,12},{9,13},{10,... | collective-permute-start | bytes 147464 | tf_op jit(solution)/shard_map/ppermute | solution.py:342
  66.9 0.0 collective-permute-done.10.refs_1_
  66.9 1.4 %collective-permute-start.18 = (bf16[4,16,384]{2,1,0:T(8,128)(2,1)S(1)}, bf16[4,16,384]{2,1,0:T(8,128)(2,1)S(1)}, u32[]{:S(2)}, u32[]{:S(2)}) collective-permute-start(bf16[4,16,384]{2,1,0:T(8,128)(2,1)S(1)} %get-tuple-element.12.refs_0_), channel_id=1, source_target_pairs={{0,6},{1,7},{2,4},{3,5},{4,2},{5,3},{6,0},{7,1},{8,14},{9,15},{10,... | collective-permute-start | bytes 147464 | tf_op jit(solution)/shard_map/ppermute | solution.py:342
  68.3 0.0 collective-permute-done.11.refs_2_
  68.3 0.0 collective-permute-start.13
  68.3 0.0 collective-permute-done.14.refs_2_
  68.3 0.5 collective-permute-start.15
  68.8 1.9 %collective-permute-done.16.refs_4_ = bf16[4,16,384]{2,1,0:T(8,128)(2,1)S(1)} collective-permute-done((bf16[4,16,384]{2,1,0:T(8,128)(2,1)S(1)}, bf16[4,16,384]{2,1,0:T(8,128)(2,1)S(1)}, u32[]{:S(2)}, u32[]{:S(2)}) %collective-permute-start.16) | collective-permute-done | bytes 49184 | tf_op jit(solution)/shard_map/ppermute | solution.py:342
  70.7 0.0 collective-permute-start.17
  70.7 2.1 %collective-permute-done.18.refs_6_ = bf16[4,16,384]{2,1,0:T(8,128)(2,1)S(1)} collective-permute-done((bf16[4,16,384]{2,1,0:T(8,128)(2,1)S(1)}, bf16[4,16,384]{2,1,0:T(8,128)(2,1)S(1)}, u32[]{:S(2)}, u32[]{:S(2)}) %collective-permute-start.18) | collective-permute-done | bytes 49184 | tf_op jit(solution)/shard_map/ppermute | solution.py:342
  72.8 0.0 collective-permute-start.19
  72.8 0.0 collective-permute-done.12.refs_3_
  72.8 3.2 %project_tokens.1 = (bf16[2,64,768]{2,1,0:T(8,128)(2,1)S(1)}, bf16[2,768,256]{2,1,0:T(8,128)(2,1)S(1)}, bf16[2,768,256]{2,1,0:T(8,128)(2,1)S(1)}, f32[64,256]{1,0:T(8,128)S(1)}) custom-call(s32[3]{0:T(128)S(1)} %pad_add_fusion.1.place_ref, s32[2,192]{1,0:T(2,128)S(1)} %pad_add_fusion.table_ref, bf16[768,2304]{1,0:T(8,128)(2,1)S(1)} %copy-done, ...), custom_call_target="tpu_custom_call" | custom-call | bytes 18000000 | tf_op jit(solution)/shard_map/project_tokens/pallas_call | solution.py:293
  76.1 0.0 collective-permute-done.13.refs_1_
  76.1 0.0 collective-permute-done.15.refs_3_
  76.1 0.0 collective-permute-done.17.refs_5_
  76.1 0.0 collective-permute-done.19.refs_7_
  76.1 6.2 %attend.1 = bf16[8,12,768]{2,1,0:T(8,128)(2,1)} custom-call(bf16[2,64,768]{2,1,0:T(8,128)(2,1)S(1)} %get-tuple-element.9.query_ref, bf16[2,768,256]{2,1,0:T(8,128)(2,1)S(1)} %get-tuple-element.10.key_ref, bf16[2,768,256]{2,1,0:T(8,128)(2,1)S(1)} %get-tuple-element.11.value_ref, bf16[4,16,384]{2,1,0:T(8,128)(2,1)S(1)} %get-tuple-element.12.refs_0_, ...), custom_call_target="tpu_custom_call" | custom-call | bytes 21600000 | tf_op jit(solution)/shard_map/attend/pallas_call | solution.py:293
  82.3 3.4 %all-to-all-start.1 = ((bf16[8,12,768]{2,1,0:T(8,128)(2,1)}), bf16[8,12,768]{2,1,0:T(8,128)(2,1)S(1)}, u32[]{:S(2)}, u32[]{:S(2)}) async-start(bf16[8,12,768]{2,1,0:T(8,128)(2,1)} %attend.1), calls=%async_computation.1 | async-start | bytes 393216 | tf_op jit(solution)/shard_map/all_to_all | solution.py:409
  85.7 0.8 copy.26
  86.5 7.4 %all-to-all-done.1 = bf16[8,12,768]{2,1,0:T(8,128)(2,1)S(1)} async-done(((bf16[8,12,768]{2,1,0:T(8,128)(2,1)}), bf16[8,12,768]{2,1,0:T(8,128)(2,1)S(1)}, u32[]{:S(2)}, u32[]{:S(2)}) %all-to-all-start.1) | async-done | bytes 147488 | tf_op jit(solution)/shard_map/all_to_all | solution.py:409
  94.0 0.1 copy.25
  94.1 0.7 reshape.15
  (11 shorter events, 0.1 us)
Async XLA Ops:
  0.6 18.1 %collective-permute-start.7 = (bf16[6,192,128]{2,1,0:T(8,128)(2,1)}, bf16[6,192,128]{2,1,0:T(8,128)(2,1)S(1)}, u32[]{:S(2)}, u32[]{:S(2)}) collective-permute-start(bf16[6,192,128]{2,1,0:T(8,128)(2,1)} %refs_0_.3), channel_id=1, source_target_pairs={{0,8},{1,9},{2,10},{3,11},{4,12},{5,13},{6,14},{7,15},{8,0},{9,1},... | collective-permute-start | bytes 884744 | tf_op jit(solution)/shard_map/ppermute | solution.py:342
  3.6 17.2 %collective-permute-start.8 = (bf16[6,192,128]{2,1,0:T(8,128)(2,1)}, bf16[6,192,128]{2,1,0:T(8,128)(2,1)S(1)}, u32[]{:S(2)}, u32[]{:S(2)}) collective-permute-start(bf16[6,192,128]{2,1,0:T(8,128)(2,1)} %refs_0_.3), channel_id=1, source_target_pairs={{0,16},{1,17},{2,18},{3,19},{4,20},{5,21},{6,22},{7,23},{8,24},{9,... | collective-permute-start | bytes 884744 | tf_op jit(solution)/shard_map/ppermute | solution.py:342
  5.2 16.0 %collective-permute-start.1 = (bf16[6,192,128]{2,1,0:T(8,128)(2,1)}, bf16[6,192,128]{2,1,0:T(8,128)(2,1)S(1)}, u32[]{:S(2)}, u32[]{:S(2)}) collective-permute-start(bf16[6,192,128]{2,1,0:T(8,128)(2,1)} %refs_0_.3), channel_id=1, source_target_pairs={{0,2},{1,3},{2,0},{3,1},{4,6},{5,7},{6,4},{7,5},{8,10},{9,11},{10,... | collective-permute-start | bytes 884744 | tf_op jit(solution)/shard_map/ppermute | solution.py:342
  6.7 25.3 %collective-permute-start.3 = (bf16[6,192,128]{2,1,0:T(8,128)(2,1)}, bf16[6,192,128]{2,1,0:T(8,128)(2,1)S(1)}, u32[]{:S(2)}, u32[]{:S(2)}) collective-permute-start(bf16[6,192,128]{2,1,0:T(8,128)(2,1)} %refs_0_.3), channel_id=1, source_target_pairs={{0,4},{1,5},{2,6},{3,7},{4,0},{5,1},{6,2},{7,3},{8,12},{9,13},{10,... | collective-permute-start | bytes 884744 | tf_op jit(solution)/shard_map/ppermute | solution.py:342
  9.3 22.7 %collective-permute-start.5 = (bf16[6,192,128]{2,1,0:T(8,128)(2,1)}, bf16[6,192,128]{2,1,0:T(8,128)(2,1)S(1)}, u32[]{:S(2)}, u32[]{:S(2)}) collective-permute-start(bf16[6,192,128]{2,1,0:T(8,128)(2,1)} %refs_0_.3), channel_id=1, source_target_pairs={{0,6},{1,7},{2,4},{3,5},{4,2},{5,3},{6,0},{7,1},{8,14},{9,15},{10,... | collective-permute-start | bytes 884744 | tf_op jit(solution)/shard_map/ppermute | solution.py:342
  11.3 35.0 %copy-start.2 = (bf16[6,192,128]{2,1,0:T(8,128)(2,1)S(1)}, bf16[6,192,128]{2,1,0:T(8,128)(2,1)}, u32[]{:S(2)}) copy-start(bf16[6,192,128]{2,1,0:T(8,128)(2,1)} %refs_0_.3) | copy-start | bytes 884740
  11.3 35.0 %copy-start.5 = (s32[192]{0:T(256)S(1)}, s32[192]{0:T(256)}, u32[]{:S(2)}) copy-start(s32[192]{0:T(256)} %mask_ref.3) | copy-start | bytes 2308
  11.3 26.7 %all-to-all-start = ((bf16[8,6,2,768]{3,2,1,0:T(2,128)(2,1)}), bf16[8,6,2,768]{3,2,1,0:T(2,128)(2,1)S(1)}, u32[]{:S(2)}, u32[]{:S(2)}) async-start(bf16[8,6,2,768]{3,2,1,0:T(2,128)(2,1)} %bitcast.14), calls=%async_computation | async-start | bytes 294912 | tf_op jit(solution)/shard_map/all_to_all | solution.py:357
  18.8 19.2 %collective-permute-start.9 = (bf16[6,192,128]{2,1,0:T(8,128)(2,1)}, bf16[6,192,128]{2,1,0:T(8,128)(2,1)S(1)}, u32[]{:S(2)}, u32[]{:S(2)}) collective-permute-start(bf16[6,192,128]{2,1,0:T(8,128)(2,1)} %refs_0_.3), channel_id=1, source_target_pairs={{0,24},{1,25},{2,26},{3,27},{4,28},{5,29},{6,30},{7,31},{8,16},{9,... | collective-permute-start | bytes 884744 | tf_op jit(solution)/shard_map/ppermute | solution.py:342
  20.9 18.3 %collective-permute-start = (bf16[6,192,128]{2,1,0:T(8,128)(2,1)}, bf16[6,192,128]{2,1,0:T(8,128)(2,1)S(1)}, u32[]{:S(2)}, u32[]{:S(2)}) collective-permute-start(bf16[6,192,128]{2,1,0:T(8,128)(2,1)} %refs_0_.3), channel_id=1, source_target_pairs={{0,1},{1,0},{2,3},{3,2},{4,5},{5,4},{6,7},{7,6},{8,9},{9,8},{10,11... | collective-permute-start | bytes 884744 | tf_op jit(solution)/shard_map/ppermute | solution.py:342
  21.2 18.6 %collective-permute-start.2 = (bf16[6,192,128]{2,1,0:T(8,128)(2,1)S(1)}, bf16[6,192,128]{2,1,0:T(8,128)(2,1)S(1)}, u32[]{:S(2)}, u32[]{:S(2)}) collective-permute-start(bf16[6,192,128]{2,1,0:T(8,128)(2,1)S(1)} %collective-permute-done.1.refs_2_), channel_id=1, source_target_pairs={{0,1},{1,0},{2,3},{3,2},{4,5},{5,4},{6,7},{7,6},{8,9},{9,8},{10,11... | collective-permute-start | bytes 884744 | tf_op jit(solution)/shard_map/ppermute | solution.py:342
  32.0 14.2 %collective-permute-start.4 = (bf16[6,192,128]{2,1,0:T(8,128)(2,1)S(1)}, bf16[6,192,128]{2,1,0:T(8,128)(2,1)S(1)}, u32[]{:S(2)}, u32[]{:S(2)}) collective-permute-start(bf16[6,192,128]{2,1,0:T(8,128)(2,1)S(1)} %collective-permute-done.3.refs_4_), channel_id=1, source_target_pairs={{0,1},{1,0},{2,3},{3,2},{4,5},{5,4},{6,7},{7,6},{8,9},{9,8},{10,11... | collective-permute-start | bytes 884744 | tf_op jit(solution)/shard_map/ppermute | solution.py:342
  32.0 14.2 %collective-permute-start.6 = (bf16[6,192,128]{2,1,0:T(8,128)(2,1)S(1)}, bf16[6,192,128]{2,1,0:T(8,128)(2,1)}, u32[]{:S(2)}, u32[]{:S(2)}) collective-permute-start(bf16[6,192,128]{2,1,0:T(8,128)(2,1)S(1)} %collective-permute-done.5.refs_6_), channel_id=1, source_target_pairs={{0,1},{1,0},{2,3},{3,2},{4,5},{5,4},{6,7},{7,6},{8,9},{9,8},{10,11... | collective-permute-start | bytes 884744 | tf_op jit(solution)/shard_map/ppermute | solution.py:342
  37.9 29.0 %collective-permute-start.10 = (bf16[8,6,2,768]{3,2,1,0:T(2,128)(2,1)S(1)}, bf16[8,6,2,768]{3,2,1,0:T(2,128)(2,1)}, u32[]{:S(2)}, u32[]{:S(2)}) collective-permute-start(bf16[8,6,2,768]{3,2,1,0:T(2,128)(2,1)S(1)} %all-to-all-done.refs_0_), channel_id=1, source_target_pairs={{0,8},{1,9},{2,10},{3,11},{4,12},{5,13},{6,14},{7,15},{8,0},{9,1},... | collective-permute-start | bytes 442376 | tf_op jit(solution)/shard_map/ppermute | solution.py:342
  39.2 29.1 %collective-permute-start.11 = (bf16[8,6,2,768]{3,2,1,0:T(2,128)(2,1)S(1)}, bf16[8,6,2,768]{3,2,1,0:T(2,128)(2,1)S(1)}, u32[]{:S(2)}, u32[]{:S(2)}) collective-permute-start(bf16[8,6,2,768]{3,2,1,0:T(2,128)(2,1)S(1)} %all-to-all-done.refs_0_), channel_id=1, source_target_pairs={{0,16},{1,17},{2,18},{3,19},{4,20},{5,21},{6,22},{7,23},{8,24},{9,... | collective-permute-start | bytes 442376 | tf_op jit(solution)/shard_map/ppermute | solution.py:342
  39.7 33.1 %collective-permute-start.12 = (bf16[8,6,2,768]{3,2,1,0:T(2,128)(2,1)S(1)}, bf16[8,6,2,768]{3,2,1,0:T(2,128)(2,1)S(1)}, u32[]{:S(2)}, u32[]{:S(2)}) collective-permute-start(bf16[8,6,2,768]{3,2,1,0:T(2,128)(2,1)S(1)} %all-to-all-done.refs_0_), channel_id=1, source_target_pairs={{0,24},{1,25},{2,26},{3,27},{4,28},{5,29},{6,30},{7,31},{8,16},{9,... | collective-permute-start | bytes 442376 | tf_op jit(solution)/shard_map/ppermute | solution.py:342
  42.3 1.0 %copy-start.1 = (bf16[6,192,128]{2,1,0:T(8,128)(2,1)S(1)}, bf16[6,192,128]{2,1,0:T(8,128)(2,1)}, u32[]{:S(2)}) copy-start(bf16[6,192,128]{2,1,0:T(8,128)(2,1)} %refs_0_.3) | copy-start | bytes 884740
  43.2 0.7 copy-start.4
  46.2 26.6 %copy-start = (bf16[768,2304]{1,0:T(8,128)(2,1)S(1)}, bf16[768,2304]{1,0:T(8,128)(2,1)}, u32[]{:S(2)}) copy-start(bf16[768,2304]{1,0:T(8,128)(2,1)} %weight_ref.1) | copy-start | bytes 10616836
  63.9 12.2 %copy-start.3 = (bf16[768,768]{1,0:T(8,128)(2,1)S(1)}, bf16[768,768]{1,0:T(8,128)(2,1)}, u32[]{:S(2)}) copy-start(bf16[768,768]{1,0:T(8,128)(2,1)} %refs_9_.1) | copy-start | bytes 3538948
  63.9 4.4 %collective-permute-start.14 = (bf16[4,16,384]{2,1,0:T(8,128)(2,1)S(1)}, bf16[4,16,384]{2,1,0:T(8,128)(2,1)S(1)}, u32[]{:S(2)}, u32[]{:S(2)}) collective-permute-start(bf16[4,16,384]{2,1,0:T(8,128)(2,1)S(1)} %get-tuple-element.12.refs_0_), channel_id=1, source_target_pairs={{0,2},{1,3},{2,0},{3,1},{4,6},{5,7},{6,4},{7,5},{8,10},{9,11},{10,... | collective-permute-start | bytes 147464 | tf_op jit(solution)/shard_map/ppermute | solution.py:342
  64.4 6.3 %collective-permute-start.16 = (bf16[4,16,384]{2,1,0:T(8,128)(2,1)S(1)}, bf16[4,16,384]{2,1,0:T(8,128)(2,1)S(1)}, u32[]{:S(2)}, u32[]{:S(2)}) collective-permute-start(bf16[4,16,384]{2,1,0:T(8,128)(2,1)S(1)} %get-tuple-element.12.refs_0_), channel_id=1, source_target_pairs={{0,4},{1,5},{2,6},{3,7},{4,0},{5,1},{6,2},{7,3},{8,12},{9,13},{10,... | collective-permute-start | bytes 147464 | tf_op jit(solution)/shard_map/ppermute | solution.py:342
  66.9 5.9 %collective-permute-start.18 = (bf16[4,16,384]{2,1,0:T(8,128)(2,1)S(1)}, bf16[4,16,384]{2,1,0:T(8,128)(2,1)S(1)}, u32[]{:S(2)}, u32[]{:S(2)}) collective-permute-start(bf16[4,16,384]{2,1,0:T(8,128)(2,1)S(1)} %get-tuple-element.12.refs_0_), channel_id=1, source_target_pairs={{0,6},{1,7},{2,4},{3,5},{4,2},{5,3},{6,0},{7,1},{8,14},{9,15},{10,... | collective-permute-start | bytes 147464 | tf_op jit(solution)/shard_map/ppermute | solution.py:342
  68.3 7.8 %collective-permute-start.13 = (bf16[4,16,384]{2,1,0:T(8,128)(2,1)S(1)}, bf16[4,16,384]{2,1,0:T(8,128)(2,1)S(1)}, u32[]{:S(2)}, u32[]{:S(2)}) collective-permute-start(bf16[4,16,384]{2,1,0:T(8,128)(2,1)S(1)} %get-tuple-element.12.refs_0_), channel_id=1, source_target_pairs={{0,1},{1,0},{2,3},{3,2},{4,5},{5,4},{6,7},{7,6},{8,9},{9,8},{10,11... | collective-permute-start | bytes 147464 | tf_op jit(solution)/shard_map/ppermute | solution.py:342
  68.3 7.8 %collective-permute-start.15 = (bf16[4,16,384]{2,1,0:T(8,128)(2,1)S(1)}, bf16[4,16,384]{2,1,0:T(8,128)(2,1)S(1)}, u32[]{:S(2)}, u32[]{:S(2)}) collective-permute-start(bf16[4,16,384]{2,1,0:T(8,128)(2,1)S(1)} %collective-permute-done.14.refs_2_), channel_id=1, source_target_pairs={{0,1},{1,0},{2,3},{3,2},{4,5},{5,4},{6,7},{7,6},{8,9},{9,8},{10,11... | collective-permute-start | bytes 147464 | tf_op jit(solution)/shard_map/ppermute | solution.py:342
  70.7 5.4 %collective-permute-start.17 = (bf16[4,16,384]{2,1,0:T(8,128)(2,1)S(1)}, bf16[4,16,384]{2,1,0:T(8,128)(2,1)S(1)}, u32[]{:S(2)}, u32[]{:S(2)}) collective-permute-start(bf16[4,16,384]{2,1,0:T(8,128)(2,1)S(1)} %collective-permute-done.16.refs_4_), channel_id=1, source_target_pairs={{0,1},{1,0},{2,3},{3,2},{4,5},{5,4},{6,7},{7,6},{8,9},{9,8},{10,11... | collective-permute-start | bytes 147464 | tf_op jit(solution)/shard_map/ppermute | solution.py:342
  72.8 3.3 %collective-permute-start.19 = (bf16[4,16,384]{2,1,0:T(8,128)(2,1)S(1)}, bf16[4,16,384]{2,1,0:T(8,128)(2,1)S(1)}, u32[]{:S(2)}, u32[]{:S(2)}) collective-permute-start(bf16[4,16,384]{2,1,0:T(8,128)(2,1)S(1)} %collective-permute-done.18.refs_6_), channel_id=1, source_target_pairs={{0,1},{1,0},{2,3},{3,2},{4,5},{5,4},{6,7},{7,6},{8,9},{9,8},{10,11... | collective-permute-start | bytes 147464 | tf_op jit(solution)/shard_map/ppermute | solution.py:342
  82.3 11.7 %all-to-all-start.1 = ((bf16[8,12,768]{2,1,0:T(8,128)(2,1)}), bf16[8,12,768]{2,1,0:T(8,128)(2,1)S(1)}, u32[]{:S(2)}, u32[]{:S(2)}) async-start(bf16[8,12,768]{2,1,0:T(8,128)(2,1)} %attend.1), calls=%async_computation.1 | async-start | bytes 393216 | tf_op jit(solution)/shard_map/all_to_all | solution.py:409

commit v4 on v3

--- a/solution.py
+++ b/solution.py
@@ -396,6 +396,7 @@
     )
 
     near = [pair_heads] + [send(pair_heads, 0, 2 * k) for k in range(1, chips)]
+    near, allowed = lax.optimization_barrier((near, allowed))
     biases = []
     for values in near:
         biases += [values, send(values, 0, 1)]

time: 95.5 us -> 94.1 us (0.985)
  waiting for transfers between devices: 26.7 us -> 24.8 us
    ppermute x20, waiting for transfers between devices: 14.6 us -> 12.7 us  [send(): return lax.ppermute(values, AXES, steps)]
  transfers between devices with their start and end apart: 22 -> 22, of which waited for: 5 -> 8; matrix products, arithmetic and copies ran while one was open for 8% -> 9% of each run, Pallas kernels for 24% -> 25%
where the time goes in v4:
time: 94.1 us; the launch traced here: 93.4 us
  Pallas kernels  29.3 us (31%)
  starting transfers between devices  27.9 us (30%)
  waiting for transfers between devices  24.8 us (26%)
  local copies, waits for them, and re-layouts  9.14 us (10%)
  other arithmetic  1.46 us (2%)
    pallas_call x4, Pallas kernels, call(): pl.pallas_call(kernel, in_specs=[SCALARS] * scalars + [BLOCK] * (len(oper...  29.3 us
    ppermute x20, starting transfers between devices, send(): return lax.ppermute(values, AXES, steps)  19.5 us
    ppermute x20, waiting for transfers between devices, send(): return lax.ppermute(values, AXES, steps)  12.7 us
    all_to_all x1, waiting for transfers between devices, shards(): arrived = lax.all_to_all(merged, 'col', 0, 0, tiled=True)  7.43 us
    unnamed x18, local copies, waits for them, and re-layouts  6.51 us
    all_to_all x1, starting transfers between devices, shards(): lax.all_to_all(jnp.transpose(by_token, (1, 0, 2, 3)), 'col', 0, 0, tiled=...  5.01 us
    all_to_all x1, waiting for transfers between devices, shards(): lax.all_to_all(jnp.transpose(by_token, (1, 0, 2, 3)), 'col', 0, 0, tiled=...  4.71 us
    all_to_all x1, starting transfers between devices, shards(): arrived = lax.all_to_all(merged, 'col', 0, 0, tiled=True)  3.39 us
  transfers between devices with their start and end apart: 22, of which 8 were waited for; matrix products, arithmetic and copies ran while one was open for 9% of the time, Pallas kernels for 25%

profile of v4, /device:TPU:0, one launch (start us, length us, event | category | flops | bytes accessed | tf_op | source)
XLA Modules:
  0.0 93.4 jit_solution(7523772397818678176)
XLA Ops:
  0.6 3.0 %collective-permute-start.7 = (bf16[6,192,128]{2,1,0:T(8,128)(2,1)}, bf16[6,192,128]{2,1,0:T(8,128)(2,1)S(1)}, u32[]{:S(2)}, u32[]{:S(2)}) collective-permute-start(bf16[6,192,128]{2,1,0:T(8,128)(2,1)} %refs_0_.3), channel_id=1, source_target_pairs={{0,8},{1,9},{2,10},{3,11},{4,12},{5,13},{6,14},{7,15},{8,0},{9,1},... | collective-permute-start | bytes 884744 | tf_op jit(solution)/shard_map/ppermute | solution.py:342
  3.6 1.5 %collective-permute-start.8 = (bf16[6,192,128]{2,1,0:T(8,128)(2,1)}, bf16[6,192,128]{2,1,0:T(8,128)(2,1)S(1)}, u32[]{:S(2)}, u32[]{:S(2)}) collective-permute-start(bf16[6,192,128]{2,1,0:T(8,128)(2,1)} %refs_0_.3), channel_id=1, source_target_pairs={{0,16},{1,17},{2,18},{3,19},{4,20},{5,21},{6,22},{7,23},{8,24},{9,... | collective-permute-start | bytes 884744 | tf_op jit(solution)/shard_map/ppermute | solution.py:342
  5.2 1.6 %collective-permute-start.1 = (bf16[6,192,128]{2,1,0:T(8,128)(2,1)}, bf16[6,192,128]{2,1,0:T(8,128)(2,1)S(1)}, u32[]{:S(2)}, u32[]{:S(2)}) collective-permute-start(bf16[6,192,128]{2,1,0:T(8,128)(2,1)} %refs_0_.3), channel_id=1, source_target_pairs={{0,2},{1,3},{2,0},{3,1},{4,6},{5,7},{6,4},{7,5},{8,10},{9,11},{10,... | collective-permute-start | bytes 884744 | tf_op jit(solution)/shard_map/ppermute | solution.py:342
  6.7 2.6 %collective-permute-start.3 = (bf16[6,192,128]{2,1,0:T(8,128)(2,1)}, bf16[6,192,128]{2,1,0:T(8,128)(2,1)S(1)}, u32[]{:S(2)}, u32[]{:S(2)}) collective-permute-start(bf16[6,192,128]{2,1,0:T(8,128)(2,1)} %refs_0_.3), channel_id=1, source_target_pairs={{0,4},{1,5},{2,6},{3,7},{4,0},{5,1},{6,2},{7,3},{8,12},{9,13},{10,... | collective-permute-start | bytes 884744 | tf_op jit(solution)/shard_map/ppermute | solution.py:342
  9.3 0.2 collective-permute-start.5
  9.5 1.0 %reshape.13 = bf16[6,8,2,768]{3,2,1,0:T(2,128)(2,1)S(1)} reshape(bf16[6,16,768]{2,1,0:T(8,128)(2,1)} %bitcast.17) | data formatting | bytes 294912 | tf_op jit(solution)/shard_map/reshape | solution.py:356
  10.5 0.8 copy.28
  11.3 5.0 %all-to-all-start = ((bf16[8,6,2,768]{3,2,1,0:T(2,128)(2,1)}), bf16[8,6,2,768]{3,2,1,0:T(2,128)(2,1)S(1)}, u32[]{:S(2)}, u32[]{:S(2)}) async-start(bf16[8,6,2,768]{3,2,1,0:T(2,128)(2,1)} %bitcast.14), calls=%async_computation | async-start | bytes 294912 | tf_op jit(solution)/shard_map/all_to_all | solution.py:357
  16.3 0.8 constant_dynamic-update-slice_fusion.3
  17.1 0.8 constant_dynamic-update-slice_fusion.2
  18.0 0.8 constant_dynamic-update-slice_fusion.1
  18.7 0.0 collective-permute-done.7.refs_1_
  18.8 0.5 collective-permute-start.9
  19.3 0.8 constant_dynamic-update-slice_fusion
  20.1 0.8 copy.22
  20.9 0.0 collective-permute-done.8.refs_2_
  20.9 0.3 collective-permute-start
  21.2 0.0 collective-permute-done.1.refs_2_
  21.2 0.3 collective-permute-start.2
  21.5 10.5 %collective-permute-done.3.refs_4_ = bf16[6,192,128]{2,1,0:T(8,128)(2,1)S(1)} collective-permute-done((bf16[6,192,128]{2,1,0:T(8,128)(2,1)}, bf16[6,192,128]{2,1,0:T(8,128)(2,1)S(1)}, u32[]{:S(2)}, u32[]{:S(2)}) %collective-permute-start.3) | collective-permute-done | bytes 294944 | tf_op jit(solution)/shard_map/ppermute | solution.py:342
  32.0 0.0 collective-permute-start.4
  32.0 0.0 collective-permute-done.5.refs_6_
  32.0 0.5 collective-permute-start.6
  32.5 0.7 pad_add_fusion.table_ref
  33.2 4.7 %all-to-all-done.refs_0_ = bf16[8,6,2,768]{3,2,1,0:T(2,128)(2,1)S(1)} async-done(((bf16[8,6,2,768]{3,2,1,0:T(2,128)(2,1)}), bf16[8,6,2,768]{3,2,1,0:T(2,128)(2,1)S(1)}, u32[]{:S(2)}, u32[]{:S(2)}) %all-to-all-start) | async-done | bytes 147488 | tf_op jit(solution)/shard_map/all_to_all | solution.py:357
  37.9 0.0 collective-permute-done.9.refs_3_
  37.9 0.5 collective-permute-start.10
  38.5 0.7 pad_maximum_fusion.gains_ref.refs_9_
  39.2 0.0 collective-permute-done.refs_1_
  39.2 0.6 collective-permute-start.11
  39.7 0.0 collective-permute-done.2.refs_3_
  39.7 2.5 %collective-permute-start.12 = (bf16[8,6,2,768]{3,2,1,0:T(2,128)(2,1)S(1)}, bf16[8,6,2,768]{3,2,1,0:T(2,128)(2,1)S(1)}, u32[]{:S(2)}, u32[]{:S(2)}) collective-permute-start(bf16[8,6,2,768]{3,2,1,0:T(2,128)(2,1)S(1)} %all-to-all-done.refs_0_), channel_id=1, source_target_pairs={{0,24},{1,25},{2,26},{3,27},{4,28},{5,29},{6,30},{7,31},{8,16},{9,... | collective-permute-start | bytes 442376 | tf_op jit(solution)/shard_map/ppermute | solution.py:342
  42.2 0.1 pad_add_fusion.1.place_ref
  42.3 1.0 %copy-done.1 = bf16[6,192,128]{2,1,0:T(8,128)(2,1)S(1)} copy-done((bf16[6,192,128]{2,1,0:T(8,128)(2,1)S(1)}, bf16[6,192,128]{2,1,0:T(8,128)(2,1)}, u32[]{:S(2)}) %copy-start.1) | copy-done | bytes 294936
  43.2 0.7 copy-done.4
  43.9 2.3 %right_rows.1.refs_8_ = f32[24,192,128]{2,1,0:T(8,128)S(1)} custom-call(s32[3]{0:T(128)S(1)} %pad_add_fusion.1.place_ref, s32[192]{0:T(256)S(1)} %copy-done.4, s32[2,192]{1,0:T(2,128)S(1)} %pad_add_fusion.table_ref, f32[2,128]{1,0:T(2,128)S(1)} %pad_maximum_fusion.gains_ref.refs_9_, bf16[128,896]{1,0:T(8,128)(2,1)S(1)} %pad_dynamic-update-slice_fusion.weight_ref.refs_10_, ...), custom_call_target="tpu_custom_call" | custom-call | bytes 10800000 | tf_op jit(solution)/shard_map/right_rows/pallas_call | solution.py:293
  46.2 0.0 copy-start
  46.2 0.0 collective-permute-done.4.refs_5_
  46.3 0.0 collective-permute-done.6.refs_7_
  46.3 17.6 %pair_rows.1 = (bf16[48,4,1,6,128]{4,3,2,1,0:T(8,128)(2,1)S(1)}, bf16[4,16,384]{2,1,0:T(8,128)(2,1)S(1)}) custom-call(s32[3]{0:T(128)S(1)} %pad_add_fusion.1.place_ref, s32[192]{0:T(256)S(1)} %copy-done.5, bf16[6,192,128]{2,1,0:T(8,128)(2,1)S(1)} %copy-done.2, bf16[6,192,128]{2,1,0:T(8,128)(2,1)S(1)} %collective-permute-done.refs_1_, ...), custom_call_target="tpu_custom_call" | custom-call | bytes 14400000 | tf_op jit(solution)/shard_map/pair_rows/pallas_call | solution.py:293
  63.9 0.6 collective-permute-start.13
  64.4 2.5 %collective-permute-start.14 = (bf16[4,16,384]{2,1,0:T(8,128)(2,1)S(1)}, bf16[4,16,384]{2,1,0:T(8,128)(2,1)S(1)}, u32[]{:S(2)}, u32[]{:S(2)}) collective-permute-start(bf16[4,16,384]{2,1,0:T(8,128)(2,1)S(1)} %get-tuple-element.19.refs_0_), channel_id=1, source_target_pairs={{0,4},{1,5},{2,6},{3,7},{4,0},{5,1},{6,2},{7,3},{8,12},{9,13},{10,... | collective-permute-start | bytes 147464 | tf_op jit(solution)/shard_map/ppermute | solution.py:342
  66.9 0.0 collective-permute-done.10.refs_1_
  66.9 1.4 %collective-permute-start.15 = (bf16[4,16,384]{2,1,0:T(8,128)(2,1)S(1)}, bf16[4,16,384]{2,1,0:T(8,128)(2,1)S(1)}, u32[]{:S(2)}, u32[]{:S(2)}) collective-permute-start(bf16[4,16,384]{2,1,0:T(8,128)(2,1)S(1)} %get-tuple-element.19.refs_0_), channel_id=1, source_target_pairs={{0,6},{1,7},{2,4},{3,5},{4,2},{5,3},{6,0},{7,1},{8,14},{9,15},{10,... | collective-permute-start | bytes 147464 | tf_op jit(solution)/shard_map/ppermute | solution.py:342
  68.3 0.0 collective-permute-done.11.refs_2_
  68.3 0.0 collective-permute-done.12.refs_3_
  68.3 3.2 %project_tokens.1 = (bf16[2,64,768]{2,1,0:T(8,128)(2,1)S(1)}, bf16[2,768,256]{2,1,0:T(8,128)(2,1)S(1)}, bf16[2,768,256]{2,1,0:T(8,128)(2,1)S(1)}, f32[64,256]{1,0:T(8,128)S(1)}) custom-call(s32[3]{0:T(128)S(1)} %pad_add_fusion.1.place_ref, s32[2,192]{1,0:T(2,128)S(1)} %pad_add_fusion.table_ref, bf16[768,2304]{1,0:T(8,128)(2,1)S(1)} %copy-done, ...), custom_call_target="tpu_custom_call" | custom-call | bytes 18000000 | tf_op jit(solution)/shard_map/project_tokens/pallas_call | solution.py:293
  71.5 0.0 collective-permute-done.13.refs_2_
  71.6 0.0 collective-permute-done.14.refs_4_
  71.6 1.2 %collective-permute-done.15.refs_6_ = bf16[4,16,384]{2,1,0:T(8,128)(2,1)S(1)} collective-permute-done((bf16[4,16,384]{2,1,0:T(8,128)(2,1)S(1)}, bf16[4,16,384]{2,1,0:T(8,128)(2,1)S(1)}, u32[]{:S(2)}, u32[]{:S(2)}) %collective-permute-start.15) | collective-permute-done | bytes 49184 | tf_op jit(solution)/shard_map/ppermute | solution.py:342
  72.8 0.0 collective-permute-start.16
  72.8 0.5 collective-permute-start.17
  73.3 0.0 collective-permute-start.18
  73.3 0.5 collective-permute-start.19
  73.8 0.2 collective-permute-done.16.refs_1_
  74.0 0.2 collective-permute-done.17.refs_3_
  74.2 0.3 collective-permute-done.18.refs_5_
  74.5 0.2 collective-permute-done.19.refs_7_
  74.7 6.2 %attend.1 = bf16[8,12,768]{2,1,0:T(8,128)(2,1)} custom-call(bf16[2,64,768]{2,1,0:T(8,128)(2,1)S(1)} %get-tuple-element.14.query_ref, bf16[2,768,256]{2,1,0:T(8,128)(2,1)S(1)} %get-tuple-element.15.key_ref, bf16[2,768,256]{2,1,0:T(8,128)(2,1)S(1)} %get-tuple-element.16.value_ref, bf16[4,16,384]{2,1,0:T(8,128)(2,1)S(1)} %get-tuple-element.19.refs_0_, ...), custom_call_target="tpu_custom_call" | custom-call | bytes 21600000 | tf_op jit(solution)/shard_map/attend/pallas_call | solution.py:293
  80.9 3.4 %all-to-all-start.1 = ((bf16[8,12,768]{2,1,0:T(8,128)(2,1)}), bf16[8,12,768]{2,1,0:T(8,128)(2,1)S(1)}, u32[]{:S(2)}, u32[]{:S(2)}) async-start(bf16[8,12,768]{2,1,0:T(8,128)(2,1)} %attend.1), calls=%async_computation.1 | async-start | bytes 393216 | tf_op jit(solution)/shard_map/all_to_all | solution.py:410
  84.3 0.8 copy.26
  85.1 7.4 %all-to-all-done.1 = bf16[8,12,768]{2,1,0:T(8,128)(2,1)S(1)} async-done(((bf16[8,12,768]{2,1,0:T(8,128)(2,1)}), bf16[8,12,768]{2,1,0:T(8,128)(2,1)S(1)}, u32[]{:S(2)}, u32[]{:S(2)}) %all-to-all-start.1) | async-done | bytes 147488 | tf_op jit(solution)/shard_map/all_to_all | solution.py:410
  92.6 0.1 copy.25
  92.7 0.7 reshape.15
  (11 shorter events, 0.1 us)
Async XLA Ops:
  0.6 18.1 %collective-permute-start.7 = (bf16[6,192,128]{2,1,0:T(8,128)(2,1)}, bf16[6,192,128]{2,1,0:T(8,128)(2,1)S(1)}, u32[]{:S(2)}, u32[]{:S(2)}) collective-permute-start(bf16[6,192,128]{2,1,0:T(8,128)(2,1)} %refs_0_.3), channel_id=1, source_target_pairs={{0,8},{1,9},{2,10},{3,11},{4,12},{5,13},{6,14},{7,15},{8,0},{9,1},... | collective-permute-start | bytes 884744 | tf_op jit(solution)/shard_map/ppermute | solution.py:342
  3.6 17.2 %collective-permute-start.8 = (bf16[6,192,128]{2,1,0:T(8,128)(2,1)}, bf16[6,192,128]{2,1,0:T(8,128)(2,1)S(1)}, u32[]{:S(2)}, u32[]{:S(2)}) collective-permute-start(bf16[6,192,128]{2,1,0:T(8,128)(2,1)} %refs_0_.3), channel_id=1, source_target_pairs={{0,16},{1,17},{2,18},{3,19},{4,20},{5,21},{6,22},{7,23},{8,24},{9,... | collective-permute-start | bytes 884744 | tf_op jit(solution)/shard_map/ppermute | solution.py:342
  5.2 16.0 %collective-permute-start.1 = (bf16[6,192,128]{2,1,0:T(8,128)(2,1)}, bf16[6,192,128]{2,1,0:T(8,128)(2,1)S(1)}, u32[]{:S(2)}, u32[]{:S(2)}) collective-permute-start(bf16[6,192,128]{2,1,0:T(8,128)(2,1)} %refs_0_.3), channel_id=1, source_target_pairs={{0,2},{1,3},{2,0},{3,1},{4,6},{5,7},{6,4},{7,5},{8,10},{9,11},{10,... | collective-permute-start | bytes 884744 | tf_op jit(solution)/shard_map/ppermute | solution.py:342
  6.7 25.3 %collective-permute-start.3 = (bf16[6,192,128]{2,1,0:T(8,128)(2,1)}, bf16[6,192,128]{2,1,0:T(8,128)(2,1)S(1)}, u32[]{:S(2)}, u32[]{:S(2)}) collective-permute-start(bf16[6,192,128]{2,1,0:T(8,128)(2,1)} %refs_0_.3), channel_id=1, source_target_pairs={{0,4},{1,5},{2,6},{3,7},{4,0},{5,1},{6,2},{7,3},{8,12},{9,13},{10,... | collective-permute-start | bytes 884744 | tf_op jit(solution)/shard_map/ppermute | solution.py:342
  9.3 22.7 %collective-permute-start.5 = (bf16[6,192,128]{2,1,0:T(8,128)(2,1)}, bf16[6,192,128]{2,1,0:T(8,128)(2,1)S(1)}, u32[]{:S(2)}, u32[]{:S(2)}) collective-permute-start(bf16[6,192,128]{2,1,0:T(8,128)(2,1)} %refs_0_.3), channel_id=1, source_target_pairs={{0,6},{1,7},{2,4},{3,5},{4,2},{5,3},{6,0},{7,1},{8,14},{9,15},{10,... | collective-permute-start | bytes 884744 | tf_op jit(solution)/shard_map/ppermute | solution.py:342
  11.3 35.0 %copy-start.2 = (bf16[6,192,128]{2,1,0:T(8,128)(2,1)S(1)}, bf16[6,192,128]{2,1,0:T(8,128)(2,1)}, u32[]{:S(2)}) copy-start(bf16[6,192,128]{2,1,0:T(8,128)(2,1)} %refs_0_.3) | copy-start | bytes 884740
  11.3 35.0 %copy-start.5 = (s32[192]{0:T(256)S(1)}, s32[192]{0:T(256)}, u32[]{:S(2)}) copy-start(s32[192]{0:T(256)} %mask_ref.3) | copy-start | bytes 2308
  11.3 26.7 %all-to-all-start = ((bf16[8,6,2,768]{3,2,1,0:T(2,128)(2,1)}), bf16[8,6,2,768]{3,2,1,0:T(2,128)(2,1)S(1)}, u32[]{:S(2)}, u32[]{:S(2)}) async-start(bf16[8,6,2,768]{3,2,1,0:T(2,128)(2,1)} %bitcast.14), calls=%async_computation | async-start | bytes 294912 | tf_op jit(solution)/shard_map/all_to_all | solution.py:357
  18.8 19.2 %collective-permute-start.9 = (bf16[6,192,128]{2,1,0:T(8,128)(2,1)}, bf16[6,192,128]{2,1,0:T(8,128)(2,1)S(1)}, u32[]{:S(2)}, u32[]{:S(2)}) collective-permute-start(bf16[6,192,128]{2,1,0:T(8,128)(2,1)} %refs_0_.3), channel_id=1, source_target_pairs={{0,24},{1,25},{2,26},{3,27},{4,28},{5,29},{6,30},{7,31},{8,16},{9,... | collective-permute-start | bytes 884744 | tf_op jit(solution)/shard_map/ppermute | solution.py:342
  20.9 18.3 %collective-permute-start = (bf16[6,192,128]{2,1,0:T(8,128)(2,1)}, bf16[6,192,128]{2,1,0:T(8,128)(2,1)S(1)}, u32[]{:S(2)}, u32[]{:S(2)}) collective-permute-start(bf16[6,192,128]{2,1,0:T(8,128)(2,1)} %refs_0_.3), channel_id=1, source_target_pairs={{0,1},{1,0},{2,3},{3,2},{4,5},{5,4},{6,7},{7,6},{8,9},{9,8},{10,11... | collective-permute-start | bytes 884744 | tf_op jit(solution)/shard_map/ppermute | solution.py:342
  21.2 18.6 %collective-permute-start.2 = (bf16[6,192,128]{2,1,0:T(8,128)(2,1)S(1)}, bf16[6,192,128]{2,1,0:T(8,128)(2,1)S(1)}, u32[]{:S(2)}, u32[]{:S(2)}) collective-permute-start(bf16[6,192,128]{2,1,0:T(8,128)(2,1)S(1)} %collective-permute-done.1.refs_2_), channel_id=1, source_target_pairs={{0,1},{1,0},{2,3},{3,2},{4,5},{5,4},{6,7},{7,6},{8,9},{9,8},{10,11... | collective-permute-start | bytes 884744 | tf_op jit(solution)/shard_map/ppermute | solution.py:342
  32.0 14.2 %collective-permute-start.4 = (bf16[6,192,128]{2,1,0:T(8,128)(2,1)S(1)}, bf16[6,192,128]{2,1,0:T(8,128)(2,1)S(1)}, u32[]{:S(2)}, u32[]{:S(2)}) collective-permute-start(bf16[6,192,128]{2,1,0:T(8,128)(2,1)S(1)} %collective-permute-done.3.refs_4_), channel_id=1, source_target_pairs={{0,1},{1,0},{2,3},{3,2},{4,5},{5,4},{6,7},{7,6},{8,9},{9,8},{10,11... | collective-permute-start | bytes 884744 | tf_op jit(solution)/shard_map/ppermute | solution.py:342
  32.0 14.2 %collective-permute-start.6 = (bf16[6,192,128]{2,1,0:T(8,128)(2,1)S(1)}, bf16[6,192,128]{2,1,0:T(8,128)(2,1)}, u32[]{:S(2)}, u32[]{:S(2)}) collective-permute-start(bf16[6,192,128]{2,1,0:T(8,128)(2,1)S(1)} %collective-permute-done.5.refs_6_), channel_id=1, source_target_pairs={{0,1},{1,0},{2,3},{3,2},{4,5},{5,4},{6,7},{7,6},{8,9},{9,8},{10,11... | collective-permute-start | bytes 884744 | tf_op jit(solution)/shard_map/ppermute | solution.py:342
  37.9 29.0 %collective-permute-start.10 = (bf16[8,6,2,768]{3,2,1,0:T(2,128)(2,1)S(1)}, bf16[8,6,2,768]{3,2,1,0:T(2,128)(2,1)}, u32[]{:S(2)}, u32[]{:S(2)}) collective-permute-start(bf16[8,6,2,768]{3,2,1,0:T(2,128)(2,1)S(1)} %all-to-all-done.refs_0_), channel_id=1, source_target_pairs={{0,8},{1,9},{2,10},{3,11},{4,12},{5,13},{6,14},{7,15},{8,0},{9,1},... | collective-permute-start | bytes 442376 | tf_op jit(solution)/shard_map/ppermute | solution.py:342
  39.2 29.1 %collective-permute-start.11 = (bf16[8,6,2,768]{3,2,1,0:T(2,128)(2,1)S(1)}, bf16[8,6,2,768]{3,2,1,0:T(2,128)(2,1)S(1)}, u32[]{:S(2)}, u32[]{:S(2)}) collective-permute-start(bf16[8,6,2,768]{3,2,1,0:T(2,128)(2,1)S(1)} %all-to-all-done.refs_0_), channel_id=1, source_target_pairs={{0,16},{1,17},{2,18},{3,19},{4,20},{5,21},{6,22},{7,23},{8,24},{9,... | collective-permute-start | bytes 442376 | tf_op jit(solution)/shard_map/ppermute | solution.py:342
  39.7 28.6 %collective-permute-start.12 = (bf16[8,6,2,768]{3,2,1,0:T(2,128)(2,1)S(1)}, bf16[8,6,2,768]{3,2,1,0:T(2,128)(2,1)S(1)}, u32[]{:S(2)}, u32[]{:S(2)}) collective-permute-start(bf16[8,6,2,768]{3,2,1,0:T(2,128)(2,1)S(1)} %all-to-all-done.refs_0_), channel_id=1, source_target_pairs={{0,24},{1,25},{2,26},{3,27},{4,28},{5,29},{6,30},{7,31},{8,16},{9,... | collective-permute-start | bytes 442376 | tf_op jit(solution)/shard_map/ppermute | solution.py:342
  42.3 1.0 %copy-start.1 = (bf16[6,192,128]{2,1,0:T(8,128)(2,1)S(1)}, bf16[6,192,128]{2,1,0:T(8,128)(2,1)}, u32[]{:S(2)}) copy-start(bf16[6,192,128]{2,1,0:T(8,128)(2,1)} %refs_0_.3) | copy-start | bytes 884740
  43.2 0.7 copy-start.4
  46.2 22.1 %copy-start = (bf16[768,2304]{1,0:T(8,128)(2,1)S(1)}, bf16[768,2304]{1,0:T(8,128)(2,1)}, u32[]{:S(2)}) copy-start(bf16[768,2304]{1,0:T(8,128)(2,1)} %weight_ref.1) | copy-start | bytes 10616836
  63.9 10.8 %copy-start.3 = (bf16[768,768]{1,0:T(8,128)(2,1)S(1)}, bf16[768,768]{1,0:T(8,128)(2,1)}, u32[]{:S(2)}) copy-start(bf16[768,768]{1,0:T(8,128)(2,1)} %refs_9_.1) | copy-start | bytes 3538948
  63.9 7.7 %collective-permute-start.13 = (bf16[4,16,384]{2,1,0:T(8,128)(2,1)S(1)}, bf16[4,16,384]{2,1,0:T(8,128)(2,1)S(1)}, u32[]{:S(2)}, u32[]{:S(2)}) collective-permute-start(bf16[4,16,384]{2,1,0:T(8,128)(2,1)S(1)} %get-tuple-element.19.refs_0_), channel_id=1, source_target_pairs={{0,2},{1,3},{2,0},{3,1},{4,6},{5,7},{6,4},{7,5},{8,10},{9,11},{10,... | collective-permute-start | bytes 147464 | tf_op jit(solution)/shard_map/ppermute | solution.py:342
  64.4 7.1 %collective-permute-start.14 = (bf16[4,16,384]{2,1,0:T(8,128)(2,1)S(1)}, bf16[4,16,384]{2,1,0:T(8,128)(2,1)S(1)}, u32[]{:S(2)}, u32[]{:S(2)}) collective-permute-start(bf16[4,16,384]{2,1,0:T(8,128)(2,1)S(1)} %get-tuple-element.19.refs_0_), channel_id=1, source_target_pairs={{0,4},{1,5},{2,6},{3,7},{4,0},{5,1},{6,2},{7,3},{8,12},{9,13},{10,... | collective-permute-start | bytes 147464 | tf_op jit(solution)/shard_map/ppermute | solution.py:342
  66.9 5.9 %collective-permute-start.15 = (bf16[4,16,384]{2,1,0:T(8,128)(2,1)S(1)}, bf16[4,16,384]{2,1,0:T(8,128)(2,1)S(1)}, u32[]{:S(2)}, u32[]{:S(2)}) collective-permute-start(bf16[4,16,384]{2,1,0:T(8,128)(2,1)S(1)} %get-tuple-element.19.refs_0_), channel_id=1, source_target_pairs={{0,6},{1,7},{2,4},{3,5},{4,2},{5,3},{6,0},{7,1},{8,14},{9,15},{10,... | collective-permute-start | bytes 147464 | tf_op jit(solution)/shard_map/ppermute | solution.py:342
  72.8 1.2 %collective-permute-start.16 = (bf16[4,16,384]{2,1,0:T(8,128)(2,1)S(1)}, bf16[4,16,384]{2,1,0:T(8,128)(2,1)S(1)}, u32[]{:S(2)}, u32[]{:S(2)}) collective-permute-start(bf16[4,16,384]{2,1,0:T(8,128)(2,1)S(1)} %get-tuple-element.19.refs_0_), channel_id=1, source_target_pairs={{0,1},{1,0},{2,3},{3,2},{4,5},{5,4},{6,7},{7,6},{8,9},{9,8},{10,11... | collective-permute-start | bytes 147464 | tf_op jit(solution)/shard_map/ppermute | solution.py:342
  72.8 1.4 %collective-permute-start.17 = (bf16[4,16,384]{2,1,0:T(8,128)(2,1)S(1)}, bf16[4,16,384]{2,1,0:T(8,128)(2,1)S(1)}, u32[]{:S(2)}, u32[]{:S(2)}) collective-permute-start(bf16[4,16,384]{2,1,0:T(8,128)(2,1)S(1)} %collective-permute-done.13.refs_2_), channel_id=1, source_target_pairs={{0,1},{1,0},{2,3},{3,2},{4,5},{5,4},{6,7},{7,6},{8,9},{9,8},{10,11... | collective-permute-start | bytes 147464 | tf_op jit(solution)/shard_map/ppermute | solution.py:342
  73.3 1.2 %collective-permute-start.18 = (bf16[4,16,384]{2,1,0:T(8,128)(2,1)S(1)}, bf16[4,16,384]{2,1,0:T(8,128)(2,1)S(1)}, u32[]{:S(2)}, u32[]{:S(2)}) collective-permute-start(bf16[4,16,384]{2,1,0:T(8,128)(2,1)S(1)} %collective-permute-done.14.refs_4_), channel_id=1, source_target_pairs={{0,1},{1,0},{2,3},{3,2},{4,5},{5,4},{6,7},{7,6},{8,9},{9,8},{10,11... | collective-permute-start | bytes 147464 | tf_op jit(solution)/shard_map/ppermute | solution.py:342
  73.3 1.4 %collective-permute-start.19 = (bf16[4,16,384]{2,1,0:T(8,128)(2,1)S(1)}, bf16[4,16,384]{2,1,0:T(8,128)(2,1)S(1)}, u32[]{:S(2)}, u32[]{:S(2)}) collective-permute-start(bf16[4,16,384]{2,1,0:T(8,128)(2,1)S(1)} %collective-permute-done.15.refs_6_), channel_id=1, source_target_pairs={{0,1},{1,0},{2,3},{3,2},{4,5},{5,4},{6,7},{7,6},{8,9},{9,8},{10,11... | collective-permute-start | bytes 147464 | tf_op jit(solution)/shard_map/ppermute | solution.py:342
  80.9 11.7 %all-to-all-start.1 = ((bf16[8,12,768]{2,1,0:T(8,128)(2,1)}), bf16[8,12,768]{2,1,0:T(8,128)(2,1)S(1)}, u32[]{:S(2)}, u32[]{:S(2)}) async-start(bf16[8,12,768]{2,1,0:T(8,128)(2,1)} %attend.1), calls=%async_computation.1 | async-start | bytes 393216 | tf_op jit(solution)/shard_map/all_to_all | solution.py:410

commit v5 on v4

--- a/solution.py
+++ b/solution.py
@@ -131,7 +131,7 @@
                     )
             return carry
 
-        lax.fori_loop(0, 2 * block_count, product, 0)
+        lax.fori_loop(0, 2 * block_count, product, 0, unroll=2)
         flat = pair_rows * block_count * SUB
         mixed_norm = layer_norm(mixed_f[...].reshape(flat, channels), mix).astype(jnp.bfloat16)
         pair = tile_f[...].reshape(flat, channels)

time: 94.1 us -> 93.8 us (level)
  transfers between devices with their start and end apart: 22 -> 22, of which waited for: 8 -> 8; matrix products, arithmetic and copies ran while one was open for 9% -> 9% of each run, Pallas kernels for 25% -> 24%
where the time goes in v5:
time: 93.8 us; the launch traced here: 93.1 us
  Pallas kernels  29 us (31%)
  starting transfers between devices  27.9 us (30%)
  waiting for transfers between devices  24.8 us (26%)
  local copies, waits for them, and re-layouts  9.14 us (10%)
  other arithmetic  1.46 us (2%)
    pallas_call x4, Pallas kernels, call(): pl.pallas_call(kernel, in_specs=[SCALARS] * scalars + [BLOCK] * (len(oper...  29 us
    ppermute x20, starting transfers between devices, send(): return lax.ppermute(values, AXES, steps)  19.5 us
    ppermute x20, waiting for transfers between devices, send(): return lax.ppermute(values, AXES, steps)  12.7 us
    all_to_all x1, waiting for transfers between devices, shards(): arrived = lax.all_to_all(merged, 'col', 0, 0, tiled=True)  7.43 us
    unnamed x18, local copies, waits for them, and re-layouts  6.51 us
    all_to_all x1, starting transfers between devices, shards(): lax.all_to_all(jnp.transpose(by_token, (1, 0, 2, 3)), 'col', 0, 0, tiled=...  5.01 us
    all_to_all x1, waiting for transfers between devices, shards(): lax.all_to_all(jnp.transpose(by_token, (1, 0, 2, 3)), 'col', 0, 0, tiled=...  4.71 us
    all_to_all x1, starting transfers between devices, shards(): arrived = lax.all_to_all(merged, 'col', 0, 0, tiled=True)  3.39 us
  transfers between devices with their start and end apart: 22, of which 8 were waited for; matrix products, arithmetic and copies ran while one was open for 9% of the time, Pallas kernels for 24%

profile of v5, /device:TPU:0, one launch (start us, length us, event | category | flops | bytes accessed | tf_op | source)
XLA Modules:
  0.0 93.1 jit_solution(425792892692617885)
XLA Ops:
  0.6 3.0 %collective-permute-start.7 = (bf16[6,192,128]{2,1,0:T(8,128)(2,1)}, bf16[6,192,128]{2,1,0:T(8,128)(2,1)S(1)}, u32[]{:S(2)}, u32[]{:S(2)}) collective-permute-start(bf16[6,192,128]{2,1,0:T(8,128)(2,1)} %refs_0_.3), channel_id=1, source_target_pairs={{0,8},{1,9},{2,10},{3,11},{4,12},{5,13},{6,14},{7,15},{8,0},{9,1},... | collective-permute-start | bytes 884744 | tf_op jit(solution)/shard_map/ppermute | solution.py:342
  3.6 1.5 %collective-permute-start.8 = (bf16[6,192,128]{2,1,0:T(8,128)(2,1)}, bf16[6,192,128]{2,1,0:T(8,128)(2,1)S(1)}, u32[]{:S(2)}, u32[]{:S(2)}) collective-permute-start(bf16[6,192,128]{2,1,0:T(8,128)(2,1)} %refs_0_.3), channel_id=1, source_target_pairs={{0,16},{1,17},{2,18},{3,19},{4,20},{5,21},{6,22},{7,23},{8,24},{9,... | collective-permute-start | bytes 884744 | tf_op jit(solution)/shard_map/ppermute | solution.py:342
  5.2 1.6 %collective-permute-start.1 = (bf16[6,192,128]{2,1,0:T(8,128)(2,1)}, bf16[6,192,128]{2,1,0:T(8,128)(2,1)S(1)}, u32[]{:S(2)}, u32[]{:S(2)}) collective-permute-start(bf16[6,192,128]{2,1,0:T(8,128)(2,1)} %refs_0_.3), channel_id=1, source_target_pairs={{0,2},{1,3},{2,0},{3,1},{4,6},{5,7},{6,4},{7,5},{8,10},{9,11},{10,... | collective-permute-start | bytes 884744 | tf_op jit(solution)/shard_map/ppermute | solution.py:342
  6.7 2.6 %collective-permute-start.3 = (bf16[6,192,128]{2,1,0:T(8,128)(2,1)}, bf16[6,192,128]{2,1,0:T(8,128)(2,1)S(1)}, u32[]{:S(2)}, u32[]{:S(2)}) collective-permute-start(bf16[6,192,128]{2,1,0:T(8,128)(2,1)} %refs_0_.3), channel_id=1, source_target_pairs={{0,4},{1,5},{2,6},{3,7},{4,0},{5,1},{6,2},{7,3},{8,12},{9,13},{10,... | collective-permute-start | bytes 884744 | tf_op jit(solution)/shard_map/ppermute | solution.py:342
  9.3 0.2 collective-permute-start.5
  9.5 1.0 %reshape.13 = bf16[6,8,2,768]{3,2,1,0:T(2,128)(2,1)S(1)} reshape(bf16[6,16,768]{2,1,0:T(8,128)(2,1)} %bitcast.17) | data formatting | bytes 294912 | tf_op jit(solution)/shard_map/reshape | solution.py:356
  10.5 0.8 copy.28
  11.3 5.0 %all-to-all-start = ((bf16[8,6,2,768]{3,2,1,0:T(2,128)(2,1)}), bf16[8,6,2,768]{3,2,1,0:T(2,128)(2,1)S(1)}, u32[]{:S(2)}, u32[]{:S(2)}) async-start(bf16[8,6,2,768]{3,2,1,0:T(2,128)(2,1)} %bitcast.14), calls=%async_computation | async-start | bytes 294912 | tf_op jit(solution)/shard_map/all_to_all | solution.py:357
  16.3 0.8 constant_dynamic-update-slice_fusion.3
  17.1 0.8 constant_dynamic-update-slice_fusion.2
  18.0 0.8 constant_dynamic-update-slice_fusion.1
  18.7 0.0 collective-permute-done.7.refs_1_
  18.8 0.5 collective-permute-start.9
  19.3 0.8 constant_dynamic-update-slice_fusion
  20.1 0.8 copy.22
  20.9 0.0 collective-permute-done.8.refs_2_
  20.9 0.3 collective-permute-start
  21.2 0.0 collective-permute-done.1.refs_2_
  21.2 0.3 collective-permute-start.2
  21.5 10.5 %collective-permute-done.3.refs_4_ = bf16[6,192,128]{2,1,0:T(8,128)(2,1)S(1)} collective-permute-done((bf16[6,192,128]{2,1,0:T(8,128)(2,1)}, bf16[6,192,128]{2,1,0:T(8,128)(2,1)S(1)}, u32[]{:S(2)}, u32[]{:S(2)}) %collective-permute-start.3) | collective-permute-done | bytes 294944 | tf_op jit(solution)/shard_map/ppermute | solution.py:342
  32.0 0.0 collective-permute-start.4
  32.0 0.0 collective-permute-done.5.refs_6_
  32.0 0.5 collective-permute-start.6
  32.5 0.7 pad_add_fusion.table_ref
  33.2 4.7 %all-to-all-done.refs_0_ = bf16[8,6,2,768]{3,2,1,0:T(2,128)(2,1)S(1)} async-done(((bf16[8,6,2,768]{3,2,1,0:T(2,128)(2,1)}), bf16[8,6,2,768]{3,2,1,0:T(2,128)(2,1)S(1)}, u32[]{:S(2)}, u32[]{:S(2)}) %all-to-all-start) | async-done | bytes 147488 | tf_op jit(solution)/shard_map/all_to_all | solution.py:357
  37.9 0.0 collective-permute-done.9.refs_3_
  37.9 0.5 collective-permute-start.10
  38.5 0.7 pad_maximum_fusion.gains_ref.refs_9_
  39.2 0.0 collective-permute-done.refs_1_
  39.2 0.6 collective-permute-start.11
  39.7 0.0 collective-permute-done.2.refs_3_
  39.7 2.5 %collective-permute-start.12 = (bf16[8,6,2,768]{3,2,1,0:T(2,128)(2,1)S(1)}, bf16[8,6,2,768]{3,2,1,0:T(2,128)(2,1)S(1)}, u32[]{:S(2)}, u32[]{:S(2)}) collective-permute-start(bf16[8,6,2,768]{3,2,1,0:T(2,128)(2,1)S(1)} %all-to-all-done.refs_0_), channel_id=1, source_target_pairs={{0,24},{1,25},{2,26},{3,27},{4,28},{5,29},{6,30},{7,31},{8,16},{9,... | collective-permute-start | bytes 442376 | tf_op jit(solution)/shard_map/ppermute | solution.py:342
  42.2 0.1 pad_add_fusion.1.place_ref
  42.3 1.0 %copy-done.1 = bf16[6,192,128]{2,1,0:T(8,128)(2,1)S(1)} copy-done((bf16[6,192,128]{2,1,0:T(8,128)(2,1)S(1)}, bf16[6,192,128]{2,1,0:T(8,128)(2,1)}, u32[]{:S(2)}) %copy-start.1) | copy-done | bytes 294936
  43.2 0.7 copy-done.4
  43.9 2.3 %right_rows.1.refs_8_ = f32[24,192,128]{2,1,0:T(8,128)S(1)} custom-call(s32[3]{0:T(128)S(1)} %pad_add_fusion.1.place_ref, s32[192]{0:T(256)S(1)} %copy-done.4, s32[2,192]{1,0:T(2,128)S(1)} %pad_add_fusion.table_ref, f32[2,128]{1,0:T(2,128)S(1)} %pad_maximum_fusion.gains_ref.refs_9_, bf16[128,896]{1,0:T(8,128)(2,1)S(1)} %pad_dynamic-update-slice_fusion.weight_ref.refs_10_, ...), custom_call_target="tpu_custom_call" | custom-call | bytes 10800000 | tf_op jit(solution)/shard_map/right_rows/pallas_call | solution.py:293
  46.2 0.0 copy-start
  46.2 0.0 collective-permute-done.4.refs_5_
  46.3 0.0 collective-permute-done.6.refs_7_
  46.3 17.2 %pair_rows.1 = (bf16[48,4,1,6,128]{4,3,2,1,0:T(8,128)(2,1)S(1)}, bf16[4,16,384]{2,1,0:T(8,128)(2,1)S(1)}) custom-call(s32[3]{0:T(128)S(1)} %pad_add_fusion.1.place_ref, s32[192]{0:T(256)S(1)} %copy-done.5, bf16[6,192,128]{2,1,0:T(8,128)(2,1)S(1)} %copy-done.2, bf16[6,192,128]{2,1,0:T(8,128)(2,1)S(1)} %collective-permute-done.refs_1_, ...), custom_call_target="tpu_custom_call" | custom-call | bytes 14400000 | tf_op jit(solution)/shard_map/pair_rows/pallas_call | solution.py:293
  63.5 0.6 collective-permute-start.13
  64.1 2.5 %collective-permute-start.14 = (bf16[4,16,384]{2,1,0:T(8,128)(2,1)S(1)}, bf16[4,16,384]{2,1,0:T(8,128)(2,1)S(1)}, u32[]{:S(2)}, u32[]{:S(2)}) collective-permute-start(bf16[4,16,384]{2,1,0:T(8,128)(2,1)S(1)} %get-tuple-element.19.refs_0_), channel_id=1, source_target_pairs={{0,4},{1,5},{2,6},{3,7},{4,0},{5,1},{6,2},{7,3},{8,12},{9,13},{10,... | collective-permute-start | bytes 147464 | tf_op jit(solution)/shard_map/ppermute | solution.py:342
  66.6 0.0 collective-permute-done.10.refs_1_
  66.6 1.4 %collective-permute-start.15 = (bf16[4,16,384]{2,1,0:T(8,128)(2,1)S(1)}, bf16[4,16,384]{2,1,0:T(8,128)(2,1)S(1)}, u32[]{:S(2)}, u32[]{:S(2)}) collective-permute-start(bf16[4,16,384]{2,1,0:T(8,128)(2,1)S(1)} %get-tuple-element.19.refs_0_), channel_id=1, source_target_pairs={{0,6},{1,7},{2,4},{3,5},{4,2},{5,3},{6,0},{7,1},{8,14},{9,15},{10,... | collective-permute-start | bytes 147464 | tf_op jit(solution)/shard_map/ppermute | solution.py:342
  67.9 0.0 collective-permute-done.11.refs_2_
  67.9 0.0 collective-permute-done.12.refs_3_
  67.9 3.2 %project_tokens.1 = (bf16[2,64,768]{2,1,0:T(8,128)(2,1)S(1)}, bf16[2,768,256]{2,1,0:T(8,128)(2,1)S(1)}, bf16[2,768,256]{2,1,0:T(8,128)(2,1)S(1)}, f32[64,256]{1,0:T(8,128)S(1)}) custom-call(s32[3]{0:T(128)S(1)} %pad_add_fusion.1.place_ref, s32[2,192]{1,0:T(2,128)S(1)} %pad_add_fusion.table_ref, bf16[768,2304]{1,0:T(8,128)(2,1)S(1)} %copy-done, ...), custom_call_target="tpu_custom_call" | custom-call | bytes 18000000 | tf_op jit(solution)/shard_map/project_tokens/pallas_call | solution.py:293
  71.2 0.0 collective-permute-done.13.refs_2_
  71.2 0.0 collective-permute-done.14.refs_4_
  71.2 1.2 %collective-permute-done.15.refs_6_ = bf16[4,16,384]{2,1,0:T(8,128)(2,1)S(1)} collective-permute-done((bf16[4,16,384]{2,1,0:T(8,128)(2,1)S(1)}, bf16[4,16,384]{2,1,0:T(8,128)(2,1)S(1)}, u32[]{:S(2)}, u32[]{:S(2)}) %collective-permute-start.15) | collective-permute-done | bytes 49184 | tf_op jit(solution)/shard_map/ppermute | solution.py:342
  72.5 0.0 collective-permute-start.16
  72.5 0.5 collective-permute-start.17
  73.0 0.0 collective-permute-start.18
  73.0 0.5 collective-permute-start.19
  73.5 0.2 collective-permute-done.16.refs_1_
  73.7 0.2 collective-permute-done.17.refs_3_
  73.8 0.3 collective-permute-done.18.refs_5_
  74.2 0.2 collective-permute-done.19.refs_7_
  74.4 6.2 %attend.1 = bf16[8,12,768]{2,1,0:T(8,128)(2,1)} custom-call(bf16[2,64,768]{2,1,0:T(8,128)(2,1)S(1)} %get-tuple-element.14.query_ref, bf16[2,768,256]{2,1,0:T(8,128)(2,1)S(1)} %get-tuple-element.15.key_ref, bf16[2,768,256]{2,1,0:T(8,128)(2,1)S(1)} %get-tuple-element.16.value_ref, bf16[4,16,384]{2,1,0:T(8,128)(2,1)S(1)} %get-tuple-element.19.refs_0_, ...), custom_call_target="tpu_custom_call" | custom-call | bytes 21600000 | tf_op jit(solution)/shard_map/attend/pallas_call | solution.py:293
  80.5 3.4 %all-to-all-start.1 = ((bf16[8,12,768]{2,1,0:T(8,128)(2,1)}), bf16[8,12,768]{2,1,0:T(8,128)(2,1)S(1)}, u32[]{:S(2)}, u32[]{:S(2)}) async-start(bf16[8,12,768]{2,1,0:T(8,128)(2,1)} %attend.1), calls=%async_computation.1 | async-start | bytes 393216 | tf_op jit(solution)/shard_map/all_to_all | solution.py:410
  83.9 0.8 copy.26
  84.8 7.4 %all-to-all-done.1 = bf16[8,12,768]{2,1,0:T(8,128)(2,1)S(1)} async-done(((bf16[8,12,768]{2,1,0:T(8,128)(2,1)}), bf16[8,12,768]{2,1,0:T(8,128)(2,1)S(1)}, u32[]{:S(2)}, u32[]{:S(2)}) %all-to-all-start.1) | async-done | bytes 147488 | tf_op jit(solution)/shard_map/all_to_all | solution.py:410
  92.2 0.1 copy.25
  92.4 0.7 reshape.15
  (11 shorter events, 0.1 us)
Async XLA Ops:
  0.6 18.1 %collective-permute-start.7 = (bf16[6,192,128]{2,1,0:T(8,128)(2,1)}, bf16[6,192,128]{2,1,0:T(8,128)(2,1)S(1)}, u32[]{:S(2)}, u32[]{:S(2)}) collective-permute-start(bf16[6,192,128]{2,1,0:T(8,128)(2,1)} %refs_0_.3), channel_id=1, source_target_pairs={{0,8},{1,9},{2,10},{3,11},{4,12},{5,13},{6,14},{7,15},{8,0},{9,1},... | collective-permute-start | bytes 884744 | tf_op jit(solution)/shard_map/ppermute | solution.py:342
  3.6 17.2 %collective-permute-start.8 = (bf16[6,192,128]{2,1,0:T(8,128)(2,1)}, bf16[6,192,128]{2,1,0:T(8,128)(2,1)S(1)}, u32[]{:S(2)}, u32[]{:S(2)}) collective-permute-start(bf16[6,192,128]{2,1,0:T(8,128)(2,1)} %refs_0_.3), channel_id=1, source_target_pairs={{0,16},{1,17},{2,18},{3,19},{4,20},{5,21},{6,22},{7,23},{8,24},{9,... | collective-permute-start | bytes 884744 | tf_op jit(solution)/shard_map/ppermute | solution.py:342
  5.2 16.0 %collective-permute-start.1 = (bf16[6,192,128]{2,1,0:T(8,128)(2,1)}, bf16[6,192,128]{2,1,0:T(8,128)(2,1)S(1)}, u32[]{:S(2)}, u32[]{:S(2)}) collective-permute-start(bf16[6,192,128]{2,1,0:T(8,128)(2,1)} %refs_0_.3), channel_id=1, source_target_pairs={{0,2},{1,3},{2,0},{3,1},{4,6},{5,7},{6,4},{7,5},{8,10},{9,11},{10,... | collective-permute-start | bytes 884744 | tf_op jit(solution)/shard_map/ppermute | solution.py:342
  6.7 25.3 %collective-permute-start.3 = (bf16[6,192,128]{2,1,0:T(8,128)(2,1)}, bf16[6,192,128]{2,1,0:T(8,128)(2,1)S(1)}, u32[]{:S(2)}, u32[]{:S(2)}) collective-permute-start(bf16[6,192,128]{2,1,0:T(8,128)(2,1)} %refs_0_.3), channel_id=1, source_target_pairs={{0,4},{1,5},{2,6},{3,7},{4,0},{5,1},{6,2},{7,3},{8,12},{9,13},{10,... | collective-permute-start | bytes 884744 | tf_op jit(solution)/shard_map/ppermute | solution.py:342
  9.3 22.7 %collective-permute-start.5 = (bf16[6,192,128]{2,1,0:T(8,128)(2,1)}, bf16[6,192,128]{2,1,0:T(8,128)(2,1)S(1)}, u32[]{:S(2)}, u32[]{:S(2)}) collective-permute-start(bf16[6,192,128]{2,1,0:T(8,128)(2,1)} %refs_0_.3), channel_id=1, source_target_pairs={{0,6},{1,7},{2,4},{3,5},{4,2},{5,3},{6,0},{7,1},{8,14},{9,15},{10,... | collective-permute-start | bytes 884744 | tf_op jit(solution)/shard_map/ppermute | solution.py:342
  11.3 35.0 %copy-start.2 = (bf16[6,192,128]{2,1,0:T(8,128)(2,1)S(1)}, bf16[6,192,128]{2,1,0:T(8,128)(2,1)}, u32[]{:S(2)}) copy-start(bf16[6,192,128]{2,1,0:T(8,128)(2,1)} %refs_0_.3) | copy-start | bytes 884740
  11.3 35.0 %copy-start.5 = (s32[192]{0:T(256)S(1)}, s32[192]{0:T(256)}, u32[]{:S(2)}) copy-start(s32[192]{0:T(256)} %mask_ref.3) | copy-start | bytes 2308
  11.3 26.7 %all-to-all-start = ((bf16[8,6,2,768]{3,2,1,0:T(2,128)(2,1)}), bf16[8,6,2,768]{3,2,1,0:T(2,128)(2,1)S(1)}, u32[]{:S(2)}, u32[]{:S(2)}) async-start(bf16[8,6,2,768]{3,2,1,0:T(2,128)(2,1)} %bitcast.14), calls=%async_computation | async-start | bytes 294912 | tf_op jit(solution)/shard_map/all_to_all | solution.py:357
  18.8 19.2 %collective-permute-start.9 = (bf16[6,192,128]{2,1,0:T(8,128)(2,1)}, bf16[6,192,128]{2,1,0:T(8,128)(2,1)S(1)}, u32[]{:S(2)}, u32[]{:S(2)}) collective-permute-start(bf16[6,192,128]{2,1,0:T(8,128)(2,1)} %refs_0_.3), channel_id=1, source_target_pairs={{0,24},{1,25},{2,26},{3,27},{4,28},{5,29},{6,30},{7,31},{8,16},{9,... | collective-permute-start | bytes 884744 | tf_op jit(solution)/shard_map/ppermute | solution.py:342
  20.9 18.3 %collective-permute-start = (bf16[6,192,128]{2,1,0:T(8,128)(2,1)}, bf16[6,192,128]{2,1,0:T(8,128)(2,1)S(1)}, u32[]{:S(2)}, u32[]{:S(2)}) collective-permute-start(bf16[6,192,128]{2,1,0:T(8,128)(2,1)} %refs_0_.3), channel_id=1, source_target_pairs={{0,1},{1,0},{2,3},{3,2},{4,5},{5,4},{6,7},{7,6},{8,9},{9,8},{10,11... | collective-permute-start | bytes 884744 | tf_op jit(solution)/shard_map/ppermute | solution.py:342
  21.2 18.6 %collective-permute-start.2 = (bf16[6,192,128]{2,1,0:T(8,128)(2,1)S(1)}, bf16[6,192,128]{2,1,0:T(8,128)(2,1)S(1)}, u32[]{:S(2)}, u32[]{:S(2)}) collective-permute-start(bf16[6,192,128]{2,1,0:T(8,128)(2,1)S(1)} %collective-permute-done.1.refs_2_), channel_id=1, source_target_pairs={{0,1},{1,0},{2,3},{3,2},{4,5},{5,4},{6,7},{7,6},{8,9},{9,8},{10,11... | collective-permute-start | bytes 884744 | tf_op jit(solution)/shard_map/ppermute | solution.py:342
  32.0 14.2 %collective-permute-start.4 = (bf16[6,192,128]{2,1,0:T(8,128)(2,1)S(1)}, bf16[6,192,128]{2,1,0:T(8,128)(2,1)S(1)}, u32[]{:S(2)}, u32[]{:S(2)}) collective-permute-start(bf16[6,192,128]{2,1,0:T(8,128)(2,1)S(1)} %collective-permute-done.3.refs_4_), channel_id=1, source_target_pairs={{0,1},{1,0},{2,3},{3,2},{4,5},{5,4},{6,7},{7,6},{8,9},{9,8},{10,11... | collective-permute-start | bytes 884744 | tf_op jit(solution)/shard_map/ppermute | solution.py:342
  32.0 14.2 %collective-permute-start.6 = (bf16[6,192,128]{2,1,0:T(8,128)(2,1)S(1)}, bf16[6,192,128]{2,1,0:T(8,128)(2,1)}, u32[]{:S(2)}, u32[]{:S(2)}) collective-permute-start(bf16[6,192,128]{2,1,0:T(8,128)(2,1)S(1)} %collective-permute-done.5.refs_6_), channel_id=1, source_target_pairs={{0,1},{1,0},{2,3},{3,2},{4,5},{5,4},{6,7},{7,6},{8,9},{9,8},{10,11... | collective-permute-start | bytes 884744 | tf_op jit(solution)/shard_map/ppermute | solution.py:342
  37.9 28.6 %collective-permute-start.10 = (bf16[8,6,2,768]{3,2,1,0:T(2,128)(2,1)S(1)}, bf16[8,6,2,768]{3,2,1,0:T(2,128)(2,1)}, u32[]{:S(2)}, u32[]{:S(2)}) collective-permute-start(bf16[8,6,2,768]{3,2,1,0:T(2,128)(2,1)S(1)} %all-to-all-done.refs_0_), channel_id=1, source_target_pairs={{0,8},{1,9},{2,10},{3,11},{4,12},{5,13},{6,14},{7,15},{8,0},{9,1},... | collective-permute-start | bytes 442376 | tf_op jit(solution)/shard_map/ppermute | solution.py:342
  39.2 28.8 %collective-permute-start.11 = (bf16[8,6,2,768]{3,2,1,0:T(2,128)(2,1)S(1)}, bf16[8,6,2,768]{3,2,1,0:T(2,128)(2,1)S(1)}, u32[]{:S(2)}, u32[]{:S(2)}) collective-permute-start(bf16[8,6,2,768]{3,2,1,0:T(2,128)(2,1)S(1)} %all-to-all-done.refs_0_), channel_id=1, source_target_pairs={{0,16},{1,17},{2,18},{3,19},{4,20},{5,21},{6,22},{7,23},{8,24},{9,... | collective-permute-start | bytes 442376 | tf_op jit(solution)/shard_map/ppermute | solution.py:342
  39.7 28.2 %collective-permute-start.12 = (bf16[8,6,2,768]{3,2,1,0:T(2,128)(2,1)S(1)}, bf16[8,6,2,768]{3,2,1,0:T(2,128)(2,1)S(1)}, u32[]{:S(2)}, u32[]{:S(2)}) collective-permute-start(bf16[8,6,2,768]{3,2,1,0:T(2,128)(2,1)S(1)} %all-to-all-done.refs_0_), channel_id=1, source_target_pairs={{0,24},{1,25},{2,26},{3,27},{4,28},{5,29},{6,30},{7,31},{8,16},{9,... | collective-permute-start | bytes 442376 | tf_op jit(solution)/shard_map/ppermute | solution.py:342
  42.3 1.0 %copy-start.1 = (bf16[6,192,128]{2,1,0:T(8,128)(2,1)S(1)}, bf16[6,192,128]{2,1,0:T(8,128)(2,1)}, u32[]{:S(2)}) copy-start(bf16[6,192,128]{2,1,0:T(8,128)(2,1)} %refs_0_.3) | copy-start | bytes 884740
  43.2 0.7 copy-start.4
  46.2 21.7 %copy-start = (bf16[768,2304]{1,0:T(8,128)(2,1)S(1)}, bf16[768,2304]{1,0:T(8,128)(2,1)}, u32[]{:S(2)}) copy-start(bf16[768,2304]{1,0:T(8,128)(2,1)} %weight_ref.1) | copy-start | bytes 10616836
  63.5 10.8 %copy-start.3 = (bf16[768,768]{1,0:T(8,128)(2,1)S(1)}, bf16[768,768]{1,0:T(8,128)(2,1)}, u32[]{:S(2)}) copy-start(bf16[768,768]{1,0:T(8,128)(2,1)} %refs_9_.1) | copy-start | bytes 3538948
  63.5 7.7 %collective-permute-start.13 = (bf16[4,16,384]{2,1,0:T(8,128)(2,1)S(1)}, bf16[4,16,384]{2,1,0:T(8,128)(2,1)S(1)}, u32[]{:S(2)}, u32[]{:S(2)}) collective-permute-start(bf16[4,16,384]{2,1,0:T(8,128)(2,1)S(1)} %get-tuple-element.19.refs_0_), channel_id=1, source_target_pairs={{0,2},{1,3},{2,0},{3,1},{4,6},{5,7},{6,4},{7,5},{8,10},{9,11},{10,... | collective-permute-start | bytes 147464 | tf_op jit(solution)/shard_map/ppermute | solution.py:342
  64.1 7.1 %collective-permute-start.14 = (bf16[4,16,384]{2,1,0:T(8,128)(2,1)S(1)}, bf16[4,16,384]{2,1,0:T(8,128)(2,1)S(1)}, u32[]{:S(2)}, u32[]{:S(2)}) collective-permute-start(bf16[4,16,384]{2,1,0:T(8,128)(2,1)S(1)} %get-tuple-element.19.refs_0_), channel_id=1, source_target_pairs={{0,4},{1,5},{2,6},{3,7},{4,0},{5,1},{6,2},{7,3},{8,12},{9,13},{10,... | collective-permute-start | bytes 147464 | tf_op jit(solution)/shard_map/ppermute | solution.py:342
  66.6 5.9 %collective-permute-start.15 = (bf16[4,16,384]{2,1,0:T(8,128)(2,1)S(1)}, bf16[4,16,384]{2,1,0:T(8,128)(2,1)S(1)}, u32[]{:S(2)}, u32[]{:S(2)}) collective-permute-start(bf16[4,16,384]{2,1,0:T(8,128)(2,1)S(1)} %get-tuple-element.19.refs_0_), channel_id=1, source_target_pairs={{0,6},{1,7},{2,4},{3,5},{4,2},{5,3},{6,0},{7,1},{8,14},{9,15},{10,... | collective-permute-start | bytes 147464 | tf_op jit(solution)/shard_map/ppermute | solution.py:342
  72.5 1.2 %collective-permute-start.16 = (bf16[4,16,384]{2,1,0:T(8,128)(2,1)S(1)}, bf16[4,16,384]{2,1,0:T(8,128)(2,1)S(1)}, u32[]{:S(2)}, u32[]{:S(2)}) collective-permute-start(bf16[4,16,384]{2,1,0:T(8,128)(2,1)S(1)} %get-tuple-element.19.refs_0_), channel_id=1, source_target_pairs={{0,1},{1,0},{2,3},{3,2},{4,5},{5,4},{6,7},{7,6},{8,9},{9,8},{10,11... | collective-permute-start | bytes 147464 | tf_op jit(solution)/shard_map/ppermute | solution.py:342
  72.5 1.4 %collective-permute-start.17 = (bf16[4,16,384]{2,1,0:T(8,128)(2,1)S(1)}, bf16[4,16,384]{2,1,0:T(8,128)(2,1)S(1)}, u32[]{:S(2)}, u32[]{:S(2)}) collective-permute-start(bf16[4,16,384]{2,1,0:T(8,128)(2,1)S(1)} %collective-permute-done.13.refs_2_), channel_id=1, source_target_pairs={{0,1},{1,0},{2,3},{3,2},{4,5},{5,4},{6,7},{7,6},{8,9},{9,8},{10,11... | collective-permute-start | bytes 147464 | tf_op jit(solution)/shard_map/ppermute | solution.py:342
  73.0 1.2 %collective-permute-start.18 = (bf16[4,16,384]{2,1,0:T(8,128)(2,1)S(1)}, bf16[4,16,384]{2,1,0:T(8,128)(2,1)S(1)}, u32[]{:S(2)}, u32[]{:S(2)}) collective-permute-start(bf16[4,16,384]{2,1,0:T(8,128)(2,1)S(1)} %collective-permute-done.14.refs_4_), channel_id=1, source_target_pairs={{0,1},{1,0},{2,3},{3,2},{4,5},{5,4},{6,7},{7,6},{8,9},{9,8},{10,11... | collective-permute-start | bytes 147464 | tf_op jit(solution)/shard_map/ppermute | solution.py:342
  73.0 1.4 %collective-permute-start.19 = (bf16[4,16,384]{2,1,0:T(8,128)(2,1)S(1)}, bf16[4,16,384]{2,1,0:T(8,128)(2,1)S(1)}, u32[]{:S(2)}, u32[]{:S(2)}) collective-permute-start(bf16[4,16,384]{2,1,0:T(8,128)(2,1)S(1)} %collective-permute-done.15.refs_6_), channel_id=1, source_target_pairs={{0,1},{1,0},{2,3},{3,2},{4,5},{5,4},{6,7},{7,6},{8,9},{9,8},{10,11... | collective-permute-start | bytes 147464 | tf_op jit(solution)/shard_map/ppermute | solution.py:342
  80.5 11.7 %all-to-all-start.1 = ((bf16[8,12,768]{2,1,0:T(8,128)(2,1)}), bf16[8,12,768]{2,1,0:T(8,128)(2,1)S(1)}, u32[]{:S(2)}, u32[]{:S(2)}) async-start(bf16[8,12,768]{2,1,0:T(8,128)(2,1)} %attend.1), calls=%async_computation.1 | async-start | bytes 393216 | tf_op jit(solution)/shard_map/all_to_all | solution.py:410
